TPU v7x, 32 devices: a whole 2x2x4 slice. The times are simulated.
32 devices in a mesh: dp: 8 (over y, x, core), mp: 4 (over z).
Axes of the slice: x: 2, y: 2, z: 4, core: 2. Of those that a mesh axis runs over, the one named last changes fastest.
Arguments:
- tokens: bfloat16 [3072, 2048], P(('dp', 'mp')), may hold values from -8 to 8
- teacher: bfloat16 [3072, 2048], P(('dp', 'mp')), may hold values from -6 to 6
- segments: int32 [8, 384], P('dp'), may hold values from 0 to 3, never falling along the last dimension, each value on 1 to 192 neighbouring positions
- block_counts: int32 [8], replicated, may hold values from 1 to 12, as said below
- loss_mask: int32 [3072], replicated, may hold values from 0 to 1, as said below
- mixer_in: float32 [4, 2048, 2048], P(None, 'dp', 'mp'), may hold values from -0.397747564 to 0.397747564
- mixer_in_moment: float32 [4, 2048, 2048], P(None, 'dp', 'mp'), may hold values from -1200 to 1200
- mixer_in_average: float32 [4, 2048, 2048], P(None, 'dp', 'mp'), may hold values from -0.125 to 0.125
- mixer_out: float32 [2048, 2048], P('mp', 'dp'), may hold values from -0.0625 to 0.0625
- mixer_out_moment: float32 [2048, 2048], P('mp', 'dp'), may hold values from -3600 to 3600
- mixer_out_average: float32 [2048, 2048], P('mp', 'dp'), may hold values from -0.0625 to 0.0625
- feed_in: float32 [2, 2048, 5632], P(None, 'dp', 'mp'), may hold values from -0.125 to 0.125
- feed_in_moment: float32 [2, 2048, 5632], P(None, 'dp', 'mp'), may hold values from -1800 to 1800
- feed_in_average: float32 [2, 2048, 5632], P(None, 'dp', 'mp'), may hold values from -0.125 to 0.125
- feed_out: float32 [5632, 2048], P('mp', 'dp'), may hold values from -0.109375 to 0.109375
- feed_out_moment: float32 [5632, 2048], P('mp', 'dp'), may hold values from -2400 to 2400
- feed_out_average: float32 [5632, 2048], P('mp', 'dp'), may hold values from -0.109375 to 0.109375
- norm_gains: float32 [3, 2048], P(None, 'dp'), may hold values from 0.5 to 1.5
- norm_gains_moment: float32 [3, 2048], P(None, 'dp'), may hold values from -1800 to 1800
- norm_gains_average: float32 [3, 2048], P(None, 'dp'), may hold values from 0.5 to 1.5
Outputs:
- output: bfloat16 [3072, 2048], P(('dp', 'mp'))
- tokens_grad: bfloat16 [3072, 2048], P(('dp', 'mp'))
- loss_value: float32 [], replicated
- mixer_in_grad: float32 [4, 2048, 2048], P(None, 'dp', 'mp')
- mixer_in_new: float32 [4, 2048, 2048], P(None, 'dp', 'mp')
- mixer_in_moment_new: float32 [4, 2048, 2048], P(None, 'dp', 'mp')
- mixer_in_average_new: float32 [4, 2048, 2048], P(None, 'dp', 'mp')
- mixer_out_grad: float32 [2048, 2048], P('mp', 'dp')
- mixer_out_new: float32 [2048, 2048], P('mp', 'dp')
- mixer_out_moment_new: float32 [2048, 2048], P('mp', 'dp')
- mixer_out_average_new: float32 [2048, 2048], P('mp', 'dp')
- feed_in_grad: float32 [2, 2048, 5632], P(None, 'dp', 'mp')
- feed_in_new: float32 [2, 2048, 5632], P(None, 'dp', 'mp')
- feed_in_moment_new: float32 [2, 2048, 5632], P(None, 'dp', 'mp')
- feed_in_average_new: float32 [2, 2048, 5632], P(None, 'dp', 'mp')
- feed_out_grad: float32 [5632, 2048], P('mp', 'dp')
- feed_out_new: float32 [5632, 2048], P('mp', 'dp')
- feed_out_moment_new: float32 [5632, 2048], P('mp', 'dp')
- feed_out_average_new: float32 [5632, 2048], P('mp', 'dp')
- norm_gains_grad: float32 [3, 2048], P(None, 'dp')
- norm_gains_new: float32 [3, 2048], P(None, 'dp')
- norm_gains_moment_new: float32 [3, 2048], P(None, 'dp')
- norm_gains_average_new: float32 [3, 2048], P(None, 'dp')
Inputs may be any that keep to these rules, and one draw needn't show every extreme that they name: `segments`: never falling along a sequence. The first 32 * block_counts positions of a sequence are live; some sequence has all 12 blocks live. `loss_mask`: 1 at the first position of every sequence.
All inputs are finite; a program needn't handle non-finite values.
Results may differ from a plain program's by a relative error of at most 0.019.
Values may be sent and summed in bfloat16 or wider, within the bound.
No kernel may reach another device: no remote copies, remote signals or barrier semaphores. Data moves between devices by JAX's collectives and lax.ppermute only.
A program may use at most 256 MiB of HBM per device.

v0:
```python
import jax
import jax.numpy as jnp
from jax import lax
from jax.sharding import PartitionSpec as P

D = 2048
HEAD_DIM = 128
BLOCK = 32


EPS = 1e-06
MOMENT_RATE = 0.5
AVERAGE_RATE = 0.5
LEARN_RATE = 4e-05
HIGH_PRECISION = lax.Precision.HIGHEST


def rms_scale(value_rows, gain):
    return (
        value_rows
        * lax.rsqrt(jnp.mean(value_rows * value_rows, axis=-1, keepdims=True) + EPS)
        * gain
    )


def block_update(state_matrix, seg_prev, query_rows, logf, key_rows, value_rows, segs, live):
    width = segs.shape[0]
    cumulative_decay = jnp.cumsum(logf, axis=0)
    causal = jnp.arange(width)[:, None] >= jnp.arange(width)[None, :]
    keep = jnp.where(causal & (segs[:, None] == segs[None, :]), 1.0, 0.0).astype(jnp.float32)
    spread = jnp.where(
        causal[:, :, None, None], cumulative_decay[:, None] - cumulative_decay[None, :], 0.0
    )
    decay = jnp.exp(spread) * keep[:, :, None, None]
    scores = jnp.einsum("thk,tshk,shk->hts", query_rows, decay, key_rows, precision=HIGH_PRECISION)
    inner = jnp.einsum("hts,shv->thv", scores, value_rows, precision=HIGH_PRECISION)
    carried_state = jnp.where(segs == seg_prev, 1.0, 0.0).astype(jnp.float32)
    outer_product = (
        jnp.einsum(
            "qoi,oin->qon",
            query_rows * jnp.exp(cumulative_decay),
            state_matrix,
            precision=HIGH_PRECISION,
        )
        * carried_state[:, None, None]
    )
    last_decay = cumulative_decay[-1]
    tail_keep = jnp.where(segs == segs[-1], 1.0, 0.0).astype(jnp.float32)
    tail_decay = jnp.exp(last_decay[None] - cumulative_decay) * tail_keep[:, None, None]
    kept_rows = jnp.where(segs[-1] == seg_prev, 1.0, 0.0).astype(jnp.float32)
    next_state = jnp.exp(last_decay)[:, :, None] * state_matrix * kept_rows + jnp.einsum(
        "ifm,ifg->fmg", key_rows * tail_decay, value_rows, precision=HIGH_PRECISION
    )
    return (next_state, (inner + outer_product) * live)


def sequence_run(query_rows, logf, key_rows, value_rows, segs, count_here):
    blocks = segs.shape[0]
    seg_prev = jnp.concatenate([jnp.full((1,), -1, jnp.int32), segs[:-1, -1]])
    index = jnp.arange(blocks, dtype=jnp.int32)

    def step(state_matrix, items):
        q_block, f_block, k_block, v_block, s_block, p_block, idx = items
        live = jnp.where(idx < count_here, 1.0, 0.0).astype(jnp.float32)
        return block_update(
            state_matrix, p_block, q_block, f_block, k_block, v_block, s_block, live
        )

    start = jnp.zeros((query_rows.shape[2], query_rows.shape[3], value_rows.shape[3]), jnp.float32)
    _, outs = lax.scan(
        jax.checkpoint(step), start, (query_rows, logf, key_rows, value_rows, segs, seg_prev, index)
    )
    return outs


def run_mixer(projected, segments, block_counts):
    seq_total, seq_len = segments.shape
    blocks = seq_len // BLOCK
    local_width = projected.shape[2]
    heads_here = local_width // HEAD_DIM
    shaped = projected.reshape(seq_total, blocks, BLOCK, 3, heads_here, HEAD_DIM)
    query_rows = jax.nn.silu(shaped[:, :, :, 0])
    logf = jax.nn.log_sigmoid(shaped[:, :, :, 1])
    key_rows = jax.nn.sigmoid(-shaped[:, :, :, 1])
    value_rows = shaped[:, :, :, 2]
    blocked_segs = segments.reshape(seq_total, blocks, BLOCK)

    def per_sequence(items):
        query_seq, logf_seq, keys_seq, values_seq, segs_seq, count_seq = items
        return sequence_run(query_seq, logf_seq, keys_seq, values_seq, segs_seq, count_seq)

    outputs = lax.map(
        per_sequence, (query_rows, logf, key_rows, value_rows, blocked_segs, block_counts)
    )
    return outputs.reshape(seq_total * seq_len, local_width)


def gated_unit(gate_up):
    return jax.nn.silu(gate_up[:, 0]) * gate_up[:, 1]


def apply_update(master, moment, average, gradient):
    moment_new = MOMENT_RATE * moment + gradient
    master_new = master - LEARN_RATE * (gradient + MOMENT_RATE * moment_new)
    average_new = AVERAGE_RATE * average + (1.0 - AVERAGE_RATE) * master_new
    return (gradient, master_new, moment_new, average_new)


def per_device(
    tokens,
    teacher,
    segments,
    block_counts,
    loss_mask,
    mixer_in,
    mixer_in_moment,
    mixer_in_average,
    mixer_out,
    mixer_out_moment,
    mixer_out_average,
    feed_in,
    feed_in_moment,
    feed_in_average,
    feed_out,
    feed_out_moment,
    feed_out_average,
    norm_gains,
    norm_gains_moment,
    norm_gains_average,
):
    mixer_in_work, mixer_out_work, feed_in_work, feed_out_work, gains_work = (
        lax.all_gather(mixer_in.astype(jnp.bfloat16), "dp", axis=1, tiled=True),
        lax.all_gather(mixer_out.astype(jnp.bfloat16), "dp", axis=1, tiled=True),
        lax.all_gather(feed_in.astype(jnp.bfloat16), "dp", axis=1, tiled=True),
        lax.all_gather(feed_out.astype(jnp.bfloat16), "dp", axis=1, tiled=True),
        lax.all_gather(norm_gains.astype(jnp.bfloat16), "dp", axis=1, tiled=True),
    )
    row_total = tokens.shape[0]
    seq_here, seq_len = segments.shape
    seq_all = block_counts.shape[0]
    data_rank = lax.axis_index("dp")
    model_rank = lax.axis_index("mp")
    model_size = lax.axis_size("mp")
    local_counts = lax.dynamic_slice_in_dim(block_counts, data_rank * seq_here, seq_here, 0)
    column = jnp.arange(seq_len, dtype=jnp.int32)
    live_all = jnp.where(column[None, :] < BLOCK * block_counts[:, None], 1.0, 0.0).astype(
        jnp.float32
    )
    total_count = jnp.sum(loss_mask.reshape(seq_all, seq_len).astype(jnp.float32) * live_all)
    position = model_rank * row_total + jnp.arange(row_total, dtype=jnp.int32)
    owner_seq = position // seq_len
    offset = position % seq_len
    picked = jnp.where(
        owner_seq[:, None] == jnp.arange(seq_here, dtype=jnp.int32)[None, :],
        local_counts[None, :],
        0,
    )
    row_blocks = jnp.sum(picked, axis=1)
    live_rows = jnp.where(offset < BLOCK * row_blocks, 1.0, 0.0).astype(jnp.float32)
    mask_here = lax.dynamic_slice_in_dim(
        loss_mask, (data_rank * model_size + model_rank) * row_total, row_total, 0
    )
    valid = mask_here.astype(jnp.float32) * live_rows
    inputs = tokens.astype(jnp.float32)
    gain_values = gains_work.astype(jnp.float32)
    norm_first, first_back = jax.vjp(rms_scale, inputs, gain_values[0])
    first_full = lax.all_gather(norm_first.astype(jnp.bfloat16), "mp", axis=0, tiled=True)
    projected = jnp.einsum(
        "td,jde->tje", first_full, mixer_in_work, preferred_element_type=jnp.float32
    )

    def mixer_local(proj):
        return run_mixer(proj, segments, local_counts)

    recurrent, mixer_back = jax.vjp(mixer_local, projected[:, :3])
    local_width = recurrent.shape[1]
    square_rows = lax.psum(jnp.sum(recurrent * recurrent, axis=1), "mp")
    inv_rms = lax.rsqrt(square_rows / D + EPS)
    gain_out = lax.dynamic_slice_in_dim(gain_values[2], model_rank * local_width, local_width, 0)
    normed_out = recurrent * inv_rms[:, None]
    scaled_out = normed_out * gain_out
    gate_z = projected[:, 3]
    gate_act = jax.nn.silu(gate_z)
    act_low = (scaled_out * gate_act).astype(jnp.bfloat16)
    piece = act_low
    mixed = lax.psum_scatter(
        jnp.dot(piece, mixer_out_work, preferred_element_type=jnp.float32).astype(jnp.bfloat16),
        "mp",
        scatter_dimension=0,
        tiled=True,
    ).astype(jnp.float32)
    resid = inputs + mixed
    norm_second, second_back = jax.vjp(rms_scale, resid, gain_values[1])
    second_full = lax.all_gather(norm_second.astype(jnp.bfloat16), "mp", axis=0, tiled=True)
    gate_up = jnp.einsum(
        "td,jdf->tjf", second_full, feed_in_work, preferred_element_type=jnp.float32
    )
    hidden, gated_back = jax.vjp(gated_unit, gate_up)
    hidden_low = hidden.astype(jnp.bfloat16)
    piece = hidden_low
    feed = lax.psum_scatter(
        jnp.dot(piece, feed_out_work, preferred_element_type=jnp.float32).astype(jnp.bfloat16),
        "mp",
        scatter_dimension=0,
        tiled=True,
    ).astype(jnp.float32)
    final = resid + feed
    output = final.astype(jnp.bfloat16)
    error = (final - teacher.astype(jnp.float32)) * valid[:, None]
    square_sum = jnp.sum(error * error)
    token_slots = row_total * lax.axis_size("dp") * model_size
    grad_final = token_slots / total_count * error
    grad_full = lax.all_gather(grad_final.astype(jnp.bfloat16), "mp", axis=0, tiled=True)
    grad_hidden = jnp.einsum(
        "td,fd->tf", grad_full, feed_out_work, preferred_element_type=jnp.float32
    )
    feed_out_grad = jnp.einsum(
        "tf,td->fd", hidden_low, grad_full, preferred_element_type=jnp.float32
    )
    (grad_gate_up,) = gated_back(grad_hidden)
    gate_up_low = grad_gate_up.astype(jnp.bfloat16)
    feed_in_grad = jnp.einsum(
        "td,tjf->jdf", second_full, gate_up_low, preferred_element_type=jnp.float32
    )
    piece = gate_up_low
    grad_second = lax.psum_scatter(
        jnp.einsum("tjf,jdf->td", piece, feed_in_work, preferred_element_type=jnp.float32).astype(
            jnp.bfloat16
        ),
        "mp",
        scatter_dimension=0,
        tiled=True,
    ).astype(jnp.float32)
    resid_from_norm, gain_two_grad = second_back(grad_second)
    grad_resid = grad_final + resid_from_norm
    resid_full = lax.all_gather(grad_resid.astype(jnp.bfloat16), "mp", axis=0, tiled=True)
    grad_act = jnp.einsum(
        "td,ed->te", resid_full, mixer_out_work, preferred_element_type=jnp.float32
    )
    mixer_out_grad = jnp.einsum(
        "te,td->ed", act_low, resid_full, preferred_element_type=jnp.float32
    )
    grad_normed = grad_act * gate_act
    gate_sig = jax.nn.sigmoid(gate_z)
    grad_gate = grad_act * scaled_out * gate_sig * (1.0 + gate_z * (1.0 - gate_sig))
    gain_out_local = jnp.sum(grad_normed * normed_out, axis=0)
    weighted = grad_normed * gain_out
    cross_rows = lax.psum(jnp.sum(weighted * recurrent, axis=1), "mp")
    cubed = inv_rms * inv_rms * inv_rms
    grad_recurrent = inv_rms[:, None] * weighted - recurrent * (cubed * cross_rows / D)[:, None]
    (grad_three,) = mixer_back(grad_recurrent)
    grad_proj = jnp.concatenate([grad_three, grad_gate[:, None, :]], axis=1)
    proj_low = grad_proj.astype(jnp.bfloat16)
    mixer_in_grad = jnp.einsum(
        "td,tje->jde", first_full, proj_low, preferred_element_type=jnp.float32
    )
    piece = proj_low
    grad_first = lax.psum_scatter(
        jnp.einsum("tje,jde->td", piece, mixer_in_work, preferred_element_type=jnp.float32).astype(
            jnp.bfloat16
        ),
        "mp",
        scatter_dimension=0,
        tiled=True,
    ).astype(jnp.float32)
    input_from_norm, gain_one_grad = first_back(grad_first)
    tokens_grad = (grad_resid + input_from_norm).astype(jnp.bfloat16)
    mixer_in_share, mixer_out_share, feed_in_share, feed_out_share = (
        lax.psum_scatter(
            mixer_in_grad.astype(jnp.bfloat16), "dp", scatter_dimension=1, tiled=True
        ).astype(jnp.float32),
        lax.psum_scatter(
            mixer_out_grad.astype(jnp.bfloat16), "dp", scatter_dimension=1, tiled=True
        ).astype(jnp.float32),
        lax.psum_scatter(
            feed_in_grad.astype(jnp.bfloat16), "dp", scatter_dimension=1, tiled=True
        ).astype(jnp.float32),
        lax.psum_scatter(
            feed_out_grad.astype(jnp.bfloat16), "dp", scatter_dimension=1, tiled=True
        ).astype(jnp.float32),
    )
    gain_out_full = lax.dynamic_update_slice_in_dim(
        jnp.zeros((D,), jnp.float32), gain_out_local, model_rank * local_width, 0
    )
    gain_terms = jnp.stack([gain_one_grad, gain_two_grad, gain_out_full])
    square_total, gain_total = lax.psum((square_sum, gain_terms), ("dp", "mp"))
    share_width = norm_gains.shape[1]
    gains_share = lax.dynamic_slice_in_dim(gain_total, data_rank * share_width, share_width, 1)
    loss_value = square_total / (total_count * D)
    first = apply_update(mixer_in, mixer_in_moment, mixer_in_average, mixer_in_share)
    second = apply_update(mixer_out, mixer_out_moment, mixer_out_average, mixer_out_share)
    third = apply_update(feed_in, feed_in_moment, feed_in_average, feed_in_share)
    fourth = apply_update(feed_out, feed_out_moment, feed_out_average, feed_out_share)
    fifth = apply_update(norm_gains, norm_gains_moment, norm_gains_average, gains_share)
    return (
        output,
        tokens_grad,
        loss_value,
        first[0],
        first[1],
        first[2],
        first[3],
        second[0],
        second[1],
        second[2],
        second[3],
        third[0],
        third[1],
        third[2],
        third[3],
        fourth[0],
        fourth[1],
        fourth[2],
        fourth[3],
        fifth[0],
        fifth[1],
        fifth[2],
        fifth[3],
    )


def solution(mesh):
    placed = (
        P(("dp", "mp"), None),
        P(("dp", "mp"), None),
        P("dp", None),
        P(),
        P(),
        P(None, "dp", "mp"),
        P(None, "dp", "mp"),
        P(None, "dp", "mp"),
        P("mp", "dp"),
        P("mp", "dp"),
        P("mp", "dp"),
        P(None, "dp", "mp"),
        P(None, "dp", "mp"),
        P(None, "dp", "mp"),
        P("mp", "dp"),
        P("mp", "dp"),
        P("mp", "dp"),
        P(None, "dp"),
        P(None, "dp"),
        P(None, "dp"),
    )
    return jax.shard_map(
        per_device,
        mesh=mesh,
        in_specs=placed,
        out_specs=(
            P(("dp", "mp"), None),
            P(("dp", "mp"), None),
            P(),
            P(None, "dp", "mp"),
            P(None, "dp", "mp"),
            P(None, "dp", "mp"),
            P(None, "dp", "mp"),
            P("mp", "dp"),
            P("mp", "dp"),
            P("mp", "dp"),
            P("mp", "dp"),
            P(None, "dp", "mp"),
            P(None, "dp", "mp"),
            P(None, "dp", "mp"),
            P(None, "dp", "mp"),
            P("mp", "dp"),
            P("mp", "dp"),
            P("mp", "dp"),
            P("mp", "dp"),
            P(None, "dp"),
            P(None, "dp"),
            P(None, "dp"),
            P(None, "dp"),
        ),
        check_vma=False,
    )
```

profile of v0, /device:TPU:0, one launch (start us, length us, event | category | flops | bytes accessed | tf_op | source)
XLA Modules:
  0.0 1303.5 jit_solution(3763945760638960458)
XLA Ops:
  7.9 10.3 all_gather.27
  28.0 31.0 %all-gather.9.cloned.1.call-done = bf16[384,2048]{1,0:T(8,128)(2,1)} async-done(((bf16[96,2048]{1,0:T(8,128)(2,1)}), bf16[384,2048]{1,0:T(8,128)(2,1)}) %all-gather.9.cloned.1.call-update) | async-done | bytes 1572880 | tf_op jit(solution)/shard_map/all_gather | solution.py:167
  59.0 55.8 %all-gather.11.cloned.1.call-done = bf16[4,2048,512]{2,1,0:T(8,128)(2,1)} async-done(((bf16[4,256,512]{2,1,0:T(8,128)(2,1)}), bf16[4,2048,512]{2,1,0:T(8,128)(2,1)}) %all-gather.11.cloned.1.call-update) | async-done | bytes 8388624 | tf_op jit(solution)/shard_map/all_gather | solution.py:132
  114.8 6.3 fusion.83
  131.5 199.0 %while.77 = (s32[]{:T(128)}, f32[4,128,128]{2,1,0:T(8,128)S(1)}, f32[12,32,4,128]{3,1,2,0:T(8,128)S(1)}, f32[12,4,128,128]{3,2,1,0:T(8,128)}, f32[12,32,4,128]{3...) while((s32[]{:T(128)}, f32[4,128,128]{2,1,0:T(8,128)S(1)}, ...), condition=%wide.region_3.4_spmd.clone, body=%wide.region_1.3_spmd.clone.sunk | while | flops 66031748 | bytes 7249693 | solution.py:70
  332.1 11.7 psum.28
  352.4 29.4 %reduce-scatter.9.cloned.1.call-done = bf16[96,2048]{1,0:T(8,128)(2,1)} async-done(((bf16[384,2048]{1,0:T(8,128)(2,1)}), bf16[96,2048]{1,0:T(8,128)(2,1)}) %reduce-scatter.9.cloned.1.call-update) | async-done | bytes 393232 | tf_op jit(solution)/shard_map/reduce_scatter | solution.py:186
  387.7 63.2 %all-gather.17.cloned.1.call-done = bf16[2,2048,1408]{2,1,0:T(8,128)(2,1)} async-done(((bf16[2,256,1408]{2,1,0:T(8,128)(2,1)}), bf16[2,2048,1408]{2,1,0:T(8,128)(2,1)}) %all-gather.17.cloned.1.call-update) | async-done | bytes 11534352 | tf_op jit(solution)/shard_map/all_gather | solution.py:134
  450.9 39.1 %all-gather.15.cloned.1.call-done = bf16[384,2048]{1,0:T(8,128)(2,1)} async-done(((bf16[96,2048]{1,0:T(8,128)(2,1)}), bf16[384,2048]{1,0:T(8,128)(2,1)}) %all-gather.15.cloned.1.call-update) | async-done | bytes 1572880 | tf_op jit(solution)/shard_map/all_gather | solution.py:194
  490.0 8.3 fusion.80
  502.0 33.6 %all-gather.19.cloned.1.call-done = bf16[1408,2048]{1,0:T(8,128)(2,1)} async-done(((bf16[1408,256]{1,0:T(8,128)(2,1)}), bf16[1408,2048]{1,0:T(8,128)(2,1)}) %all-gather.19.cloned.1.call-update) | async-done | bytes 5767184 | tf_op jit(solution)/shard_map/all_gather | solution.py:135
  535.7 6.7 convolution_convert_fusion.2
  544.6 33.3 %reduce-scatter.11.cloned.1.call-done = bf16[96,2048]{1,0:T(8,128)(2,1)} async-done(((bf16[384,2048]{1,0:T(8,128)(2,1)}), bf16[96,2048]{1,0:T(8,128)(2,1)}) %reduce-scatter.11.cloned.1.call-update) | async-done | bytes 393232 | tf_op jit(solution)/shard_map/reduce_scatter | solution.py:201
  579.9 36.2 %all-gather.21.cloned.1.call-done = bf16[384,2048]{1,0:T(8,128)(2,1)} async-done(((bf16[96,2048]{1,0:T(8,128)(2,1)}), bf16[384,2048]{1,0:T(8,128)(2,1)}) %all-gather.21.cloned.1.call-update) | async-done | bytes 1572880 | tf_op jit(solution)/shard_map/all_gather | solution.py:213
  616.1 7.4 multiply_bitcast_fusion.3
  625.6 13.0 bitcast_convert_fusion.1
  638.7 34.2 %reduce-scatter.13.cloned.1.call-done = bf16[96,2048]{1,0:T(8,128)(2,1)} async-done(((bf16[384,2048]{1,0:T(8,128)(2,1)}), bf16[96,2048]{1,0:T(8,128)(2,1)}) %reduce-scatter.13.cloned.1.call-update) | async-done | bytes 393232 | tf_op jit(solution)/shard_map/reduce_scatter | solution.py:226
  676.8 10.4 reduce-scatter.23.cloned.1.call-start
  687.1 7.4 convolution_convert_fusion
  694.6 18.3 %all-gather.23.cloned.1.call-done = bf16[384,2048]{1,0:T(8,128)(2,1)} async-done(((bf16[96,2048]{1,0:T(8,128)(2,1)}), bf16[384,2048]{1,0:T(8,128)(2,1)}) %all-gather.23.cloned.1.call-update) | async-done | bytes 1572880 | tf_op jit(solution)/shard_map/all_gather | solution.py:236
  713.0 4.3 multiply_reduce_fusion.1
  717.3 9.6 psum.29
  734.8 287.9 %while.78 = (s32[]{:T(128)}, f32[4,128,128]{2,1,0:T(8,128)S(1)}, f32[12,32,4,128]{3,1,2,0:T(8,128)}, f32[12,32,4,128]{3,1,2,0:T(8,128)}, f32[12,32,4,128]{3,1,2,...) while((s32[]{:T(128)}, f32[4,128,128]{2,1,0:T(8,128)S(1)}, ...), condition=%wide.region_21.22_spmd.clone, body=%wide.region_14.21_spmd.clone.sunk | while | flops 138826880 | bytes 11786091 | solution.py:70
  1027.1 10.0 bitcast_convert_fusion
  1041.3 11.5 convert_bitcast_fusion
  1052.9 8.5 convert_bitcast_fusion.1
  1080.7 5.1 add_multiply_fusion.2
  1087.3 40.2 %all-reduce.7 = (f32[]{:T(128)}, f32[3,2048]{1,0:T(4,128)S(1)}) all-reduce(f32[]{:T(128)} %get-tuple-element.997, f32[3,2048]{1,0:T(4,128)S(1)} %pad_maximum_fusion.3), channel_id=1, replica_groups=mesh['dp'=8,'mp'=4] {'dp','mp'}, use_global_device_ids=true, to_apply=%region_25.26 | all-reduce | flops 6145 | bytes 49160 | tf_op jit(solution)/shard_map/psum | solution.py:286
  1132.8 72.8 %reduce-scatter.21.cloned.1.call-done = bf16[2,256,1408]{1,2,0:T(8,128)(2,1)} async-done(((bf16[2,2048,1408]{1,2,0:T(8,128)(2,1)}), bf16[2,256,1408]{1,2,0:T(8,128)(2,1)}) %reduce-scatter.21.cloned.1.call-update) | async-done | bytes 1441808 | tf_op jit(solution)/shard_map/reduce_scatter | solution.py:275
  1205.7 8.1 add_multiply_fusion
  1228.5 51.8 %reduce-scatter.17.cloned.1.call-done = bf16[4,256,512]{1,2,0:T(8,128)(2,1)} async-done(((bf16[4,2048,512]{1,2,0:T(8,128)(2,1)}), bf16[4,256,512]{1,2,0:T(8,128)(2,1)}) %reduce-scatter.17.cloned.1.call-update) | async-done | bytes 1048592 | tf_op jit(solution)/shard_map/reduce_scatter | solution.py:269
  1280.3 5.8 add_multiply_fusion.1
  (848 shorter events, 538.1 us)
Async XLA Ops:
  7.2 51.8 %all-gather.9.cloned.1.call-start = ((), (), s32[]{:S(2)}) async-start(), calls=%async_computation.8 | async-start | bytes 1966080 | tf_op jit(solution)/shard_map/all_gather | solution.py:167
  21.5 93.3 %all-gather.11.cloned.1.call-start = ((), (), s32[]{:S(2)}) async-start(), calls=%async_computation.9 | async-start | bytes 9437184 | tf_op jit(solution)/shard_map/all_gather | solution.py:132
  24.3 321.0 %all-gather.13.cloned.1.call-start = ((), (), s32[]{:S(2)}) async-start(), calls=%async_computation.10 | async-start | bytes 2359296 | tf_op jit(solution)/shard_map/all_gather | solution.py:133
  25.1 356.7 %reduce-scatter.9.cloned.1.call-start = ((), (), s32[]{:S(2)}) async-start(), calls=%async_computation.11 | async-start | bytes 1966080 | tf_op jit(solution)/shard_map/reduce_scatter | solution.py:186
  349.1 32.7 %copy-start = (bf16[96,2048]{1,0:T(8,128)(2,1)S(1)}, bf16[96,2048]{1,0:T(8,128)(2,1)}, u32[]{:S(2)}) copy-start(bf16[96,2048]{1,0:T(8,128)(2,1)} %param.24) | copy-start | bytes 1179652
  349.2 101.7 %all-gather.17.cloned.1.call-start = ((), (), s32[]{:S(2)}) async-start(), calls=%async_computation.13 | async-start | bytes 12976128 | tf_op jit(solution)/shard_map/all_gather | solution.py:134
  352.3 137.6 %all-gather.15.cloned.1.call-start = ((), (), s32[]{:S(2)}) async-start(), calls=%async_computation.12 | async-start | bytes 1966080 | tf_op jit(solution)/shard_map/all_gather | solution.py:194
  385.0 150.7 %all-gather.19.cloned.1.call-start = ((), (), s32[]{:S(2)}) async-start(), calls=%async_computation.14 | async-start | bytes 6488064 | tf_op jit(solution)/shard_map/all_gather | solution.py:135
  387.4 190.5 %reduce-scatter.11.cloned.1.call-start = ((), (), s32[]{:S(2)}) async-start(), calls=%async_computation.15 | async-start | bytes 1966080 | tf_op jit(solution)/shard_map/reduce_scatter | solution.py:201
  502.0 40.5 %copy-start.37 = (s32[8]{0:T(128)S(1)}, s32[8]{0:T(128)}, u32[]{:S(2)}) copy-start(s32[8]{0:T(128)} %param.27) | copy-start | bytes 100
  502.0 40.5 %copy-start.28 = (s32[3072]{0:T(1024)S(1)}, s32[3072]{0:T(1024)}, u32[]{:S(2)}) copy-start(s32[3072]{0:T(1024)} %param.28) | copy-start | bytes 36868
  502.0 75.8 %copy-start.1 = (bf16[96,2048]{1,0:T(8,128)(2,1)S(1)}, bf16[96,2048]{1,0:T(8,128)(2,1)}, u32[]{:S(2)}) copy-start(bf16[96,2048]{1,0:T(8,128)(2,1)} %reduce-scatter.9.cloned.1.call-done) | copy-start | bytes 1179652
  502.0 75.8 %copy-start.12 = (bf16[96,2048]{1,0:T(8,128)(2,1)S(1)}, bf16[96,2048]{1,0:T(8,128)(2,1)}, u32[]{:S(2)}) copy-start(bf16[96,2048]{1,0:T(8,128)(2,1)} %param.25) | copy-start | bytes 1179652
  542.4 73.7 %all-gather.21.cloned.1.call-start = ((), (), s32[]{:S(2)}) async-start(), calls=%async_computation.16 | async-start | bytes 1966080 | tf_op jit(solution)/shard_map/all_gather | solution.py:213
  579.9 93.1 %reduce-scatter.13.cloned.1.call-start = ((), (), s32[]{:S(2)}) async-start(), calls=%async_computation.17 | async-start | bytes 1966080 | tf_op jit(solution)/shard_map/reduce_scatter | solution.py:226
  625.6 47.3 %copy-start.13 = (bf16[96,2048]{1,0:T(8,128)(2,1)S(1)}, bf16[96,2048]{1,0:T(8,128)(2,1)}, u32[]{:S(2)}) copy-start(bf16[96,2048]{1,0:T(8,128)(2,1)} %reduce-scatter.11.cloned.1.call-done) | copy-start | bytes 1179652
  638.7 74.3 %all-gather.23.cloned.1.call-start = ((), (), s32[]{:S(2)}) async-start(), calls=%async_computation.18 | async-start | bytes 1966080 | tf_op jit(solution)/shard_map/all_gather | solution.py:236
  676.8 404.0 %reduce-scatter.23.cloned.1.call-start = ((), (), s32[]{:S(2)}) async-start(), calls=%async_computation.23 | async-start | bytes 6488064 | tf_op jit(solution)/shard_map/reduce_scatter | solution.py:278
  694.6 391.3 %reduce-scatter.15.cloned.1.call-start = ((), (), s32[]{:S(2)}) async-start(), calls=%async_computation.19 | async-start | bytes 1966080 | tf_op jit(solution)/shard_map/reduce_scatter | solution.py:258
  734.8 287.9 %copy-start.6 = (f32[1,12,32,1,4,128]{5,4,2,1,3,0:T(4,128)S(1)}, f32[1,12,32,1,4,128]{5,4,2,1,3,0:T(4,128)}, u32[]{:S(2)}) copy-start(f32[1,12,32,1,4,128]{5,4,2,1,3,0:T(4,128)} %copy-done.5) | copy-start | bytes 2359300
  1027.1 10.1 copy-start.22
  1037.2 91.7 %reduce-scatter.19.cloned.1.call-start = ((), (), s32[]{:S(2)}) async-start(), calls=%async_computation.21 | async-start | bytes 2359296 | tf_op jit(solution)/shard_map/reduce_scatter | solution.py:272
  1041.3 164.3 %reduce-scatter.21.cloned.1.call-start = ((), (), s32[]{:S(2)}) async-start(), calls=%async_computation.22 | async-start | bytes 12976128 | tf_op jit(solution)/shard_map/reduce_scatter | solution.py:275
  1052.9 227.4 %reduce-scatter.17.cloned.1.call-start = ((), (), s32[]{:S(2)}) async-start(), calls=%async_computation.20 | async-start | bytes 9437184 | tf_op jit(solution)/shard_map/reduce_scatter | solution.py:269
  1080.6 47.6 %copy-start.35 = (f32[96]{0:T(128)S(1)}, f32[96]{0:T(128)}, u32[]{:S(2)}) copy-start(f32[96]{0:T(128)} %copy-done.34) | copy-start | bytes 1156
  1080.6 47.6 %copy-start.27 = (f32[3,256]{1,0:T(4,128)S(1)}, f32[3,256]{1,0:T(4,128)}, u32[]{:S(2)}) copy-start(f32[3,256]{1,0:T(4,128)} %param.41) | copy-start | bytes 9220
  1080.7 47.6 %copy-start.31 = (f32[3,256]{1,0:T(4,128)S(1)}, f32[3,256]{1,0:T(4,128)}, u32[]{:S(2)}) copy-start(f32[3,256]{1,0:T(4,128)} %param.43) | copy-start | bytes 9220
  1080.7 47.6 %copy-start.32 = (f32[3,256]{1,0:T(4,128)S(1)}, f32[3,256]{1,0:T(4,128)}, u32[]{:S(2)}) copy-start(f32[3,256]{1,0:T(4,128)} %param.42) | copy-start | bytes 9220
  1080.7 48.2 %copy-start.17 = (f32[512,256]{1,0:T(8,128)S(1)}, f32[512,256]{1,0:T(8,128)}, u32[]{:S(2)}) copy-start(f32[512,256]{1,0:T(8,128)} %param.32) | copy-start | bytes 1572868
  1087.3 44.5 %copy-start.14 = (f32[96,2048]{1,0:T(8,128)S(1)}, f32[96,2048]{1,0:T(8,128)}, u32[]{:S(2)}) copy-start(f32[96,2048]{1,0:T(8,128)} %get-tuple-element.1077) | copy-start | bytes 2359300
  1087.3 44.5 %copy-start.19 = (bf16[96,2048]{1,0:T(8,128)(2,1)S(1)}, bf16[96,2048]{1,0:T(8,128)(2,1)}, u32[]{:S(2)}) copy-start(bf16[96,2048]{1,0:T(8,128)(2,1)} %reduce-scatter.15.cloned.1.call-done) | copy-start | bytes 1179652
  1225.3 55.0 %copy-start.3 = (f32[4,256,512]{1,2,0:T(8,128)S(1)}, f32[4,256,512]{1,2,0:T(8,128)}, u32[]{:S(2)}) copy-start(f32[4,256,512]{1,2,0:T(8,128)} %copy.143) | copy-start | bytes 6291460
  (25 other events, 76.2 us)
Sparse Core Ops, SparseCore 0:
  21.6 37.3 all-gather.8
  61.5 53.2 all-gather.10
  117.2 28.1 all-gather.12
  349.3 32.5 reduce-scatter.8
  384.1 66.6 all-gather.16
  452.8 37.0 all-gather.14
  492.4 43.2 all-gather.18
  542.5 35.2 reduce-scatter.10
  580.0 36.0 all-gather.20
  638.8 34.1 reduce-scatter.12
  676.9 36.0 all-gather.22
  716.3 57.9 reduce-scatter.22
  1037.3 33.5 reduce-scatter.14
  1075.0 40.3 reduce-scatter.18
  1118.7 86.8 reduce-scatter.20
  1209.0 71.2 reduce-scatter.16
where the time goes:
time: 1320 us; the launch traced here: 1300 us
  waiting for transfers between devices  499 us (38%)
  matrix products  262 us (20%)
  local copies, waits for them, and re-layouts  189 us (14%)
  other arithmetic  188 us (14%)
  blocking collectives  71.8 us (5%)
  loops' own time  63.6 us (5%)
  between operations  18.2 us (1%)
    dot_general x36, matrix products, block_update(): jnp.einsum('thk,tshk,shk->hts', query_rows, decay, key_rows, precision=HI...  109 us
    reduce_scatter x1, waiting for transfers between devices, per_device(): lax.psum_scatter(feed_in_grad.astype(jnp.bfloat16), 'dp', scatter_dimensi...  72.8 us
    another operation x2, loops' own time, sequence_run(): lax.scan(jax.checkpoint(step), start, (query_rows, logf, key_rows, value_...  63.6 us
    all_gather x1, waiting for transfers between devices, per_device(): lax.all_gather(feed_in.astype(jnp.bfloat16), 'dp', axis=1, tiled=True)  63.2 us
    all_gather x1, waiting for transfers between devices, per_device(): lax.all_gather(mixer_in.astype(jnp.bfloat16), 'dp', axis=1, tiled=True)  55.8 us
    reduce_scatter x1, waiting for transfers between devices, per_device(): lax.psum_scatter(mixer_in_grad.astype(jnp.bfloat16), 'dp', scatter_dimens...  51.8 us
    squeeze x60, local copies, waits for them, and re-layouts, sequence_run(): lax.scan(jax.checkpoint(step), start, (query_rows, logf, key_rows, value_...  51.1 us
    unnamed x98, local copies, waits for them, and re-layouts  50.8 us
  transfers between devices with their start and end apart: 16, of which 12 were waited for; matrix products, arithmetic and copies ran while one was open for 44% of the time, Pallas kernels for 0%

commit v1 on v0

v1 whole, which is shorter than its diff:
```python
import functools

import jax
import jax.numpy as jnp
import numpy as np
from jax import lax
from jax.experimental import pallas as pl
from jax.experimental.pallas import tpu as pltpu
from jax.sharding import PartitionSpec as P

D = 2048
HEAD_DIM = 128
BLOCK = 32
CHUNK = 128
LEVELS = 7

EPS = 1e-06
MOMENT_RATE = 0.5
AVERAGE_RATE = 0.5
LEARN_RATE = 4e-05

BF = jnp.bfloat16
F32 = jnp.float32


def decay_sums():
    t = np.arange(CHUNK)[:, None]
    r = np.arange(CHUNK)[None, :]
    mats = []
    for level in range(LEVELS):
        half = 1 << level
        mid = (t // (2 * half)) * (2 * half) + half
        right = t >= mid
        mats.append(np.where(right, (r >= mid) & (r <= t), (r > t) & (r < mid)))
    mats.append(r <= t)
    mats.append(r > t)
    return np.stack(mats).astype(np.float32)


def dot(a, b):
    return lax.dot_general(a, b, (((1,), (0,)), ((), ())), preferred_element_type=F32)


def dot_nt(a, b):
    return lax.dot_general(a, b, (((1,), (1,)), ((), ())), preferred_element_type=F32)


def dot_tn(a, b):
    return lax.dot_general(a, b, (((0,), (0,)), ((), ())), preferred_element_type=F32)


def sigmoid(v):
    return 1.0 / (1.0 + jnp.exp(-v))


def forget_parts(z):
    small = jnp.exp(-jnp.abs(z))
    logf = jnp.minimum(z, 0.0) - jnp.log1p(small)
    key = jnp.where(z >= 0.0, small, 1.0) / (1.0 + small)
    return logf, key


def split_sum(mat, logf_pair):
    both = dot(mat, logf_pair)
    return both[:, :HEAD_DIM] + both[:, HEAD_DIM:]


def chunk_masks():
    row = lax.broadcasted_iota(jnp.int32, (CHUNK, CHUNK), 0)
    col = lax.broadcasted_iota(jnp.int32, (CHUNK, CHUNK), 1)
    return row, col, row ^ col


def mixer_forward_kernel(
    count_ref, z_ref, gain_ref, seg_row_ref, seg_col_ref, sums_ref, o_ref, act_ref, square_ref, state_ref, pair_ref
):
    head = pl.program_id(1)
    seq = pl.program_id(0)
    chunks = z_ref.shape[1] // CHUNK
    row, col, differ = chunk_masks()
    live_end = count_ref[seq] * BLOCK
    state = jnp.zeros((HEAD_DIM, HEAD_DIM), F32)
    gain = gain_ref[...]
    for c in range(chunks):
        rows = pl.ds(c * CHUNK, CHUNK)
        z0, z1, value, z3 = (z_ref[j, rows, :] for j in range(4))
        query = z0 * sigmoid(z0)
        logf, key = forget_parts(z1)
        high = logf.astype(BF)
        pair = jnp.concatenate([high, (logf - high.astype(F32)).astype(BF)], axis=1)
        seg_col = seg_col_ref[0, rows, :]
        seg_row = seg_row_ref[0, :, c * CHUNK : (c + 1) * CHUNK]
        seg_last = seg_row[:, CHUNK - 1 :]
        value_low = value.astype(BF)
        scores = None
        for level in reversed(range(LEVELS)):
            decay = jnp.exp(split_sum(sums_ref[level], pair))
            right = ((row >> level) & 1) == 1
            mixed = (decay * jnp.where(right, query, key)).astype(BF)
            product = dot_nt(mixed, mixed)
            scores = product if scores is None else jnp.where(differ < (2 << level), product, scores)
        diagonal = jnp.sum(query * key, axis=1, keepdims=True)
        scores = jnp.where(differ == 0, diagonal, scores)
        scores = jnp.where(seg_col == seg_row, scores, 0.0).astype(BF)
        pair_ref[0, 0, c] = scores
        out = dot(jnp.where(row >= col, scores, jnp.zeros_like(scores)), value_low)
        from_start = jnp.exp(split_sum(sums_ref[LEVELS], pair))
        if c > 0:
            carried = seg_col == seg_before
            reach = jnp.where(carried, query * from_start, 0.0).astype(BF)
            out = out + dot_nt(reach, state.astype(BF))
        state_ref[0, 0, c] = state
        position = c * CHUNK + lax.broadcasted_iota(jnp.int32, (CHUNK, 1), 0)
        out = jnp.where(position < live_end, out, 0.0)
        o_ref[rows, :] = out
        act_ref[rows, :] = (out * gain * (z3 * sigmoid(z3))).astype(BF)
        square = jnp.sum(out * out, axis=1, keepdims=True)
        square_ref[rows, :] = jnp.where(head == 0, square, square_ref[rows, :] + square)
        if c < chunks - 1:
            to_end = jnp.exp(split_sum(sums_ref[LEVELS + 1], pair))
            tail = jnp.where(seg_col == seg_last, key * to_end, 0.0).astype(BF)
            fresh = dot_tn(value_low, tail)
            if c > 0:
                kept = jnp.where(seg_last == seg_before, from_start[CHUNK - 1 :], 0.0)
                fresh = fresh + state * kept
            state = fresh
            seg_before = seg_last


def mixer_backward_kernel(
    count_ref, z_ref, o_ref, dact_ref, inv_ref, coef_ref, gain_ref, seg_row_ref, seg_col_ref,
    sums_ref, sums_t_ref, state_ref, pair_ref, dz_ref, gain_grad_ref,
):
    seq = pl.program_id(1)
    chunks = z_ref.shape[1] // CHUNK
    row, col, differ = chunk_masks()
    live_end = count_ref[seq] * BLOCK
    gain = gain_ref[...]
    dstate = jnp.zeros((HEAD_DIM, HEAD_DIM), F32)
    gain_total = jnp.zeros((1, HEAD_DIM), F32)
    for c in reversed(range(chunks)):
        rows = pl.ds(c * CHUNK, CHUNK)
        z0, z1, value, z3 = (z_ref[j, rows, :] for j in range(4))
        gate0 = sigmoid(z0)
        query = z0 * gate0
        logf, key = forget_parts(z1)
        high = logf.astype(BF)
        pair = jnp.concatenate([high, (logf - high.astype(F32)).astype(BF)], axis=1)
        seg_col = seg_col_ref[0, rows, :]
        seg_row = seg_row_ref[0, :, c * CHUNK : (c + 1) * CHUNK]
        seg_last = seg_row[:, CHUNK - 1 :]
        value_low = value.astype(BF)

        out = o_ref[rows, :]
        dact = dact_ref[rows, :]
        inv = inv_ref[rows, :]
        gate3 = sigmoid(z3)
        normed = out * inv
        dnorm = dact * (z3 * gate3)
        gain_total = gain_total + jnp.sum(dnorm * normed, axis=0, keepdims=True)
        dz_ref[3, rows, :] = (dact * (normed * gain) * gate3 * (1.0 + z3 * (1.0 - gate3))).astype(BF)
        dout = inv * (dnorm * gain) - out * coef_ref[rows, :]
        position = c * CHUNK + lax.broadcasted_iota(jnp.int32, (CHUNK, 1), 0)
        dout = jnp.where(position < live_end, dout, 0.0)
        dout_low = dout.astype(BF)

        dscore = jnp.where(row > col, dot_nt(dout_low, value_low), dot_nt(value_low, dout_low))
        dscore = jnp.where(seg_col == seg_row, dscore, 0.0).astype(BF)
        scores = pair_ref[0, 0, c]
        zero = jnp.zeros_like(scores)
        dvalue = dot(jnp.where(col >= row, scores, zero), dout_low)
        diagonal = jnp.sum(dout * value, axis=1, keepdims=True)
        dquery = diagonal * key
        dkey = diagonal * query
        dlogf = jnp.zeros((CHUNK, HEAD_DIM), F32)
        for level in range(LEVELS):
            decay = jnp.exp(split_sum(sums_ref[level], pair))
            right = ((row >> level) & 1) == 1
            mixed = decay * jnp.where(right, query, key)
            dmixed = dot(jnp.where((differ >> level) == 1, dscore, zero), mixed.astype(BF))
            through = dmixed * decay
            dquery = dquery + jnp.where(right, through, 0.0)
            dkey = dkey + jnp.where(right, 0.0, through)
            dlogf = dlogf + dot(sums_t_ref[level], (dmixed * mixed).astype(BF))
        from_start = jnp.exp(split_sum(sums_ref[LEVELS], pair))
        total = from_start[CHUNK - 1 :]
        if c > 0:
            seg_before = seg_row_ref[0, :, c * CHUNK - 1 : c * CHUNK]
            carried = seg_col == seg_before
            state = state_ref[0, 0, c]
            reach = jnp.where(carried, query * from_start, 0.0)
            dreach = jnp.where(carried, dot(dout_low, state.astype(BF)), 0.0)
            dquery = dquery + dreach * from_start
            dlogf = dlogf + dot(sums_t_ref[LEVELS], (dreach * reach).astype(BF))
            dstate_new = dot_tn(dout_low, reach.astype(BF))
        if c < chunks - 1:
            to_end = jnp.exp(split_sum(sums_ref[LEVELS + 1], pair))
            in_tail = seg_col == seg_last
            tail = jnp.where(in_tail, key * to_end, 0.0)
            dstate_low = dstate.astype(BF)
            dtail = jnp.where(in_tail, dot(value_low, dstate_low), 0.0)
            dkey = dkey + dtail * to_end
            dlogf = dlogf + dot(sums_t_ref[LEVELS + 1], (dtail * tail).astype(BF))
            dvalue = dvalue + dot_nt(tail.astype(BF), dstate_low)
            if c > 0:
                kept = jnp.where(seg_last == seg_before, total, 0.0)
                dlogf = dlogf + jnp.sum(state * dstate, axis=0, keepdims=True) * kept
                dstate_new = dstate_new + dstate * kept
        if c > 0:
            dstate = dstate_new
        dz_ref[0, rows, :] = (dquery * gate0 * (1.0 + z0 * (1.0 - gate0))).astype(BF)
        dz_ref[1, rows, :] = ((dlogf - dkey * (1.0 - key)) * key).astype(BF)
        dz_ref[2, rows, :] = dvalue.astype(BF)
    gain_grad_ref[...] = jnp.where(seq == 0, gain_total, gain_grad_ref[...] + gain_total)


def mixer_forward(z, gain, segments, counts):
    seqs, seq_len = segments.shape
    rows, width = z.shape[1:]
    heads = width // HEAD_DIM
    chunks = seq_len // CHUNK
    sums = jnp.asarray(decay_sums(), BF)
    grid = (seqs, heads)
    token_spec = pl.BlockSpec((seq_len, HEAD_DIM), lambda s, h: (s, h))
    square_spec = pl.BlockSpec((seq_len, 1), lambda s, h: (s, 0))
    state_spec = pl.BlockSpec((1, 1, chunks, HEAD_DIM, HEAD_DIM), lambda s, h: (s, h, 0, 0, 0))
    return pl.pallas_call(
        mixer_forward_kernel,
        grid=grid,
        in_specs=[
            pl.BlockSpec(memory_space=pltpu.SMEM),
            pl.BlockSpec((4, seq_len, HEAD_DIM), lambda s, h: (0, s, h)),
            pl.BlockSpec((1, HEAD_DIM), lambda s, h: (0, h)),
            pl.BlockSpec((1, 1, seq_len), lambda s, h: (s, 0, 0)),
            pl.BlockSpec((1, seq_len, 1), lambda s, h: (s, 0, 0)),
            pl.BlockSpec(sums.shape, lambda s, h: (0, 0, 0)),
        ],
        out_specs=[token_spec, token_spec, square_spec, state_spec, state_spec],
        out_shape=[
            jax.ShapeDtypeStruct((rows, width), F32),
            jax.ShapeDtypeStruct((rows, width), BF),
            jax.ShapeDtypeStruct((rows, 1), F32),
            jax.ShapeDtypeStruct((seqs, heads, chunks, HEAD_DIM, HEAD_DIM), F32),
            jax.ShapeDtypeStruct((seqs, heads, chunks, HEAD_DIM, HEAD_DIM), BF),
        ],
        compiler_params=pltpu.CompilerParams(vmem_limit_bytes=48 * 1024 * 1024),
        name="mixer_forward",
    )(counts, z, gain, segments[:, None, :], segments[:, :, None], sums)


def mixer_backward(z, o, dact, inv, coef, gain, segments, counts, states, pairs):
    seqs, seq_len = segments.shape
    rows, width = o.shape
    heads = width // HEAD_DIM
    chunks = seq_len // CHUNK
    sums = decay_sums()
    sums_t = jnp.asarray(sums.transpose(0, 2, 1), BF)
    sums = jnp.asarray(sums, BF)
    grid = (heads, seqs)
    token_spec = pl.BlockSpec((seq_len, HEAD_DIM), lambda h, s: (s, h))
    column_spec = pl.BlockSpec((seq_len, 1), lambda h, s: (s, 0))
    z_spec = pl.BlockSpec((4, seq_len, HEAD_DIM), lambda h, s: (0, s, h))
    state_spec = pl.BlockSpec((1, 1, chunks, HEAD_DIM, HEAD_DIM), lambda h, s: (s, h, 0, 0, 0))
    gain_spec = pl.BlockSpec((1, HEAD_DIM), lambda h, s: (0, h))
    sums_spec = pl.BlockSpec(sums.shape, lambda h, s: (0, 0, 0))
    return pl.pallas_call(
        mixer_backward_kernel,
        grid=grid,
        in_specs=[
            pl.BlockSpec(memory_space=pltpu.SMEM),
            z_spec,
            token_spec,
            token_spec,
            column_spec,
            column_spec,
            gain_spec,
            pl.BlockSpec((1, 1, seq_len), lambda h, s: (s, 0, 0)),
            pl.BlockSpec((1, seq_len, 1), lambda h, s: (s, 0, 0)),
            sums_spec,
            sums_spec,
            state_spec,
            state_spec,
        ],
        out_specs=[z_spec, gain_spec],
        out_shape=[
            jax.ShapeDtypeStruct((4, rows, width), BF),
            jax.ShapeDtypeStruct((1, width), F32),
        ],
        compiler_params=pltpu.CompilerParams(vmem_limit_bytes=48 * 1024 * 1024),
        name="mixer_backward",
    )(counts, z, o, dact, inv, coef, gain, segments[:, None, :], segments[:, :, None], sums, sums_t, states, pairs)


def turn(v, axis, step):
    n = lax.axis_size(axis)
    return lax.ppermute(v, axis, [(i, (i + step) % n) for i in range(n)])


def swap(v, axis, bit):
    n = lax.axis_size(axis)
    return lax.ppermute(v, axis, [(i, i ^ bit) for i in range(n)])


def gather_rows(v, axis):
    n = lax.axis_size(axis)
    me = lax.axis_index(axis)
    rows = v.shape[0]
    whole = jnp.zeros((n * rows,) + v.shape[1:], v.dtype)
    pieces = [v] + [turn(v, axis, k) for k in range(1, n)]
    for k, piece in enumerate(pieces):
        whole = lax.dynamic_update_slice_in_dim(whole, piece, (me - k) % n * rows, 0)
    return whole


def gather_near(v, axis):
    n = lax.axis_size(axis)
    return jnp.concatenate([v] + [turn(v, axis, k) for k in range(1, n)], axis=0)


def scatter_rows(v, axis):
    n = lax.axis_size(axis)
    me = lax.axis_index(axis)
    rows = v.shape[0] // n
    pieces = [lax.dynamic_slice_in_dim(v, (me + k) % n * rows, rows, 0) for k in range(n)]
    total = pieces[0].astype(F32)
    for k in range(1, n):
        total = total + turn(pieces[k], axis, k).astype(F32)
    return total


def scatter_near(v, axis):
    n = lax.axis_size(axis)
    rows = v.shape[0] // n
    total = v[:rows].astype(F32)
    for k in range(1, n):
        total = total + turn(v[k * rows : (k + 1) * rows], axis, -k).astype(F32)
    return total


def sum_everywhere(v, axis):
    n = lax.axis_size(axis)
    total = v
    for k in range(1, n):
        total = total + turn(v, axis, k)
    return total


def gather_gains(v):
    bit = 1
    me = lax.axis_index("dp")
    while bit < lax.axis_size("dp"):
        other = swap(v, "dp", bit)
        upper = (me & bit) > 0
        v = jnp.concatenate([jnp.where(upper, other, v), jnp.where(upper, v, other)], axis=1)
        bit *= 2
    return v


def sum_to_slices(v):
    me = lax.axis_index("dp")
    bit = lax.axis_size("dp") // 2
    while bit:
        upper = (me & bit) > 0
        half = v.shape[1] // 2
        keep = jnp.where(upper, v[:, half:], v[:, :half])
        give = jnp.where(upper, v[:, :half], v[:, half:])
        v = keep + swap(give, "dp", bit)
        bit //= 2
    bit = lax.axis_size("mp") // 2
    while bit:
        v = v + swap(v, "mp", bit)
        bit //= 2
    return v


def mean_square(v):
    return jnp.mean(v * v, axis=-1, keepdims=True)


def norm_back(v, scale, weighted):
    return scale * weighted - v * (scale * scale * scale * jnp.mean(weighted * v, axis=-1, keepdims=True))


def apply_update(master, moment, average, gradient):
    moment_new = MOMENT_RATE * moment + gradient
    master_new = master - LEARN_RATE * (gradient + MOMENT_RATE * moment_new)
    average_new = AVERAGE_RATE * average + (1.0 - AVERAGE_RATE) * master_new
    return (gradient, master_new, moment_new, average_new)


def gather_weight(w, dim):
    return lax.all_gather(w.astype(BF), "dp", axis=dim, tiled=True)


def scatter_gradient(g, dim):
    return lax.psum_scatter(g.astype(BF), "dp", scatter_dimension=dim, tiled=True).astype(F32)


def per_device(
    tokens,
    teacher,
    segments,
    block_counts,
    loss_mask,
    mixer_in,
    mixer_in_moment,
    mixer_in_average,
    mixer_out,
    mixer_out_moment,
    mixer_out_average,
    feed_in,
    feed_in_moment,
    feed_in_average,
    feed_out,
    feed_out_moment,
    feed_out_average,
    norm_gains,
    norm_gains_moment,
    norm_gains_average,
):
    mixer_in_work = gather_weight(mixer_in, 1)
    mixer_out_work = gather_weight(mixer_out, 1)
    feed_in_work = gather_weight(feed_in, 1)
    feed_out_work = gather_weight(feed_out, 1)
    gains = gather_gains(norm_gains.astype(BF)).astype(F32)

    row_total = tokens.shape[0]
    seq_here, seq_len = segments.shape
    seq_all = block_counts.shape[0]
    data_rank = lax.axis_index("dp")
    model_rank = lax.axis_index("mp")
    model_size = lax.axis_size("mp")
    local_counts = lax.dynamic_slice_in_dim(block_counts, data_rank * seq_here, seq_here, 0)
    column = jnp.arange(seq_len, dtype=jnp.int32)
    live_all = (column[None, :] < BLOCK * block_counts[:, None]).astype(F32)
    total_count = jnp.sum(loss_mask.reshape(seq_all, seq_len).astype(F32) * live_all)
    first_row = (data_rank * model_size + model_rank) * row_total
    valid = lax.dynamic_slice_in_dim(loss_mask.astype(F32) * live_all.reshape(-1), first_row, row_total, 0)

    inputs = tokens.astype(F32)
    inputs_scale = lax.rsqrt(mean_square(inputs) + EPS)
    tokens_full = gather_rows(tokens, "mp").astype(F32)
    first_full = (tokens_full * lax.rsqrt(mean_square(tokens_full) + EPS) * gains[0]).astype(BF)
    z = jnp.einsum("td,jde->jte", first_full, mixer_in_work, preferred_element_type=F32)
    local_width = z.shape[2]
    gain_out = lax.dynamic_slice_in_dim(gains[2], model_rank * local_width, local_width, 0)[None]
    recurrent, act_raw, square, states, pairs = mixer_forward(z, gain_out, segments, local_counts)
    square = sum_everywhere(square.reshape(-1), "mp")
    out_scale = lax.rsqrt(square / D + EPS)
    out_scale_here = lax.dynamic_slice_in_dim(out_scale, model_rank * row_total, row_total, 0)[:, None]
    mixed = out_scale_here * scatter_rows(dot(act_raw, mixer_out_work).astype(BF), "mp")

    resid = inputs + mixed
    resid_scale = lax.rsqrt(mean_square(resid) + EPS)
    second_full = gather_near((resid * resid_scale * gains[1]).astype(BF), "mp")
    gate_up = jnp.einsum("td,jdf->jtf", second_full, feed_in_work, preferred_element_type=F32)
    gate_sig = jax.nn.sigmoid(gate_up[0])
    gate_act = gate_up[0] * gate_sig
    hidden_low = (gate_act * gate_up[1]).astype(BF)
    final = resid + scatter_near(dot(hidden_low, feed_out_work).astype(BF), "mp")
    output = final.astype(BF)

    error = (final - teacher.astype(F32)) * valid[:, None]
    square_sum = jnp.sum(error * error)
    token_slots = row_total * lax.axis_size("dp") * model_size
    grad_final = token_slots / total_count * error

    grad_full = gather_near(grad_final.astype(BF), "mp")
    grad_hidden = dot_nt(grad_full, feed_out_work)
    grad_gate = (grad_hidden * gate_up[1] * gate_sig * (1.0 + gate_up[0] * (1.0 - gate_sig))).astype(BF)
    grad_up = (grad_hidden * gate_act).astype(BF)
    grad_second = scatter_near(
        (dot_nt(grad_gate, feed_in_work[0]) + dot_nt(grad_up, feed_in_work[1])).astype(BF), "mp"
    )
    feed_out_grad = dot_tn(hidden_low, grad_full)
    feed_in_grad = jnp.stack([dot_tn(second_full, grad_gate), dot_tn(second_full, grad_up)])
    grad_resid = grad_final + norm_back(resid, resid_scale, grad_second * gains[1])
    gain_two_grad = jnp.sum(grad_second * resid * resid_scale, axis=0)

    grad_resid_low = grad_resid.astype(BF)
    coef_here = out_scale_here * out_scale_here * jnp.mean(
        grad_resid_low.astype(F32) * mixed, axis=-1, keepdims=True
    )
    coef = gather_rows(coef_here[:, 0], "mp")
    resid_full = gather_rows(grad_resid_low, "mp")
    grad_act = dot_nt(resid_full, mixer_out_work)
    act_low = (act_raw.astype(F32) * out_scale[:, None]).astype(BF)
    mixer_out_grad = dot_tn(act_low, resid_full)
    dz, gain_out_grad = mixer_backward(
        z, recurrent, grad_act, out_scale[:, None], coef[:, None], gain_out, segments, local_counts, states, pairs
    )
    mixer_in_grad = jnp.einsum("td,jte->jde", first_full, dz, preferred_element_type=F32)
    grad_first = scatter_rows(
        jnp.einsum("jte,jde->td", dz, mixer_in_work, preferred_element_type=F32).astype(BF), "mp"
    )
    tokens_grad = (grad_resid + norm_back(inputs, inputs_scale, grad_first * gains[0])).astype(BF)
    gain_one_grad = jnp.sum(grad_first * inputs * inputs_scale, axis=0)

    feed_out_share = scatter_gradient(feed_out_grad, 1)
    feed_in_share = scatter_gradient(feed_in_grad, 1)
    mixer_out_share = scatter_gradient(mixer_out_grad, 1)
    mixer_in_share = scatter_gradient(mixer_in_grad, 1)

    gain_out_full = lax.dynamic_update_slice_in_dim(
        jnp.zeros((D,), F32), gain_out_grad[0], model_rank * local_width, 0
    )
    sums = sum_to_slices(
        jnp.stack([gain_one_grad, gain_two_grad, gain_out_full, jnp.full((D,), square_sum)])
    )
    gains_share = sums[:3]
    loss_value = sums[3, 0] / (total_count * D)
    first = apply_update(mixer_in, mixer_in_moment, mixer_in_average, mixer_in_share)
    second = apply_update(mixer_out, mixer_out_moment, mixer_out_average, mixer_out_share)
    third = apply_update(feed_in, feed_in_moment, feed_in_average, feed_in_share)
    fourth = apply_update(feed_out, feed_out_moment, feed_out_average, feed_out_share)
    fifth = apply_update(norm_gains, norm_gains_moment, norm_gains_average, gains_share)
    return (output, tokens_grad, loss_value) + first + second + third + fourth + fifth


def solution(mesh):
    tokens = P(("dp", "mp"), None)
    stacked = P(None, "dp", "mp")
    flat = P("mp", "dp")
    gains = P(None, "dp")
    return jax.shard_map(
        per_device,
        mesh=mesh,
        in_specs=(tokens, tokens, P("dp", None), P(), P())
        + (stacked,) * 3 + (flat,) * 3 + (stacked,) * 3 + (flat,) * 3 + (gains,) * 3,
        out_specs=(tokens, tokens, P()) + (stacked,) * 4 + (flat,) * 4 + (stacked,) * 4 + (flat,) * 4 + (gains,) * 4,
        check_vma=False,
    )
```

time: 1320 us -> 681 us (0.52)
  matrix products: 262 us -> 70 us
  local copies, waits for them, and re-layouts: 189 us -> 34.3 us
  other arithmetic: 188 us -> 46.8 us
  waiting for transfers between devices: 499 us -> 382 us
  starting transfers between devices: 11.2 us -> 84.5 us
  blocking collectives: 71.8 us -> 0 us
  loops' own time: 63.6 us -> 0 us
  Pallas kernels: 0 us -> 37.7 us
    all_gather x8 -> x4, waiting for transfers between devices: 277 us -> 44.6 us  [gather_weight(): return lax.all_gather(w.astype(BF), 'dp', axis=dim, tiled=True)]
    ppermute x0 -> x38, waiting for transfers between devices: none -> 223 us  [the longest x30 212 us: turn(): return lax.ppermute(v, axis, [(i, (i + step) % n) for i in range(n)])]
    dot_general x156 -> x14, matrix products: 262 us -> 70 us  [the longest x4 19.2 us: dot_tn(): lax.dot_general(a, b, (((0,), (0,)), ((), ())), preferred_element_type=F32)]
    reduce_scatter x8 -> x4, waiting for transfers between devices: 222 us -> 114 us  [scatter_gradient(): lax.psum_scatter(g.astype(BF), 'dp', scatter_dimension=dim, tiled=True)]
    ppermute x0 -> x38, starting transfers between devices: none -> 83.7 us  [the longest x30 72.4 us: turn(): return lax.ppermute(v, axis, [(i, (i + step) % n) for i in range(n)])]
    another operation x2 -> x0, loops' own time: 63.6 us -> none  [sequence_run(): lax.scan(jax.checkpoint(step), start, (query_rows, logf, key_rows, value_...]
    psum x3 -> x0, blocking collectives: 61.5 us -> none  [the longest x1 40.2 us: per_device(): square_total, gain_total = lax.psum((square_sum, gain_terms), ('dp', 'mp'))]
    squeeze x74 -> x0, local copies, waits for them, and re-layouts: 53 us -> none  [the longest x60 51.1 us: sequence_run(): lax.scan(jax.checkpoint(step), start, (query_rows, logf, key_rows, value_...]
  transfers between devices with their start and end apart: 16 -> 46, of which waited for: 12 -> 30; matrix products, arithmetic and copies ran while one was open for 44% -> 15% of each run, Pallas kernels for 0% -> 6%
where the time goes in v1:
time: 681 us; the launch traced here: 674 us
  waiting for transfers between devices  382 us (56%)
  starting transfers between devices  84.5 us (12%)
  matrix products  70 us (10%)
  other arithmetic  46.8 us (7%)
  Pallas kernels  37.7 us (6%)
  local copies, waits for them, and re-layouts  34.3 us (5%)
  between operations  18.7 us (3%)
    ppermute x30, waiting for transfers between devices, turn(): return lax.ppermute(v, axis, [(i, (i + step) % n) for i in range(n)])  212 us
    reduce_scatter x4, waiting for transfers between devices, scatter_gradient(): lax.psum_scatter(g.astype(BF), 'dp', scatter_dimension=dim, tiled=True)  114 us
    ppermute x30, starting transfers between devices, turn(): return lax.ppermute(v, axis, [(i, (i + step) % n) for i in range(n)])  72.4 us
    all_gather x4, waiting for transfers between devices, gather_weight(): return lax.all_gather(w.astype(BF), 'dp', axis=dim, tiled=True)  44.6 us
    unnamed x133, local copies, waits for them, and re-layouts  28.6 us
    add x5, other arithmetic, apply_update(): average_new = AVERAGE_RATE * average + (1.0 - AVERAGE_RATE) * master_new  21.9 us
    pallas_call x1, Pallas kernels, mixer_backward(): pl.pallas_call(mixer_backward_kernel, grid=grid, in_specs=[pl.BlockSpec(m...  21.4 us
    dot_general x4, matrix products, dot_tn(): lax.dot_general(a, b, (((0,), (0,)), ((), ())), preferred_element_type=F32)  19.2 us
  transfers between devices with their start and end apart: 46, of which 30 were waited for; matrix products, arithmetic and copies ran while one was open for 15% of the time, Pallas kernels for 6%

profile of v1, /device:TPU:0, one launch (start us, length us, event | category | flops | bytes accessed | tf_op | source)
XLA Modules:
  0.0 673.6 jit_solution(6059131458787605389)
XLA Ops:
  32.9 15.8 %collective-permute-done.1 = bf16[96,2048]{1,0:T(8,128)(2,1)S(1)} collective-permute-done((bf16[96,2048]{1,0:T(8,128)(2,1)S(1)}, bf16[96,2048]{1,0:T(8,128)(2,1)S(1)}, u32[]{:S(2)}, u32[]{:S(2)}) %collective-permute-start.1) | collective-permute-done | bytes 393248 | tf_op jit(solution)/shard_map/ppermute | solution.py:296
  49.8 17.9 %all-gather.5.cloned.1.call-done = bf16[4,2048,512]{2,1,0:T(8,128)(2,1)} async-done(((bf16[4,256,512]{2,1,0:T(8,128)(2,1)}), bf16[4,2048,512]{2,1,0:T(8,128)(2,1)}) %all-gather.5.cloned.1.call-update) | async-done | bytes 8388624 | tf_op jit(solution)/shard_map/all_gather | solution.py:392
  67.7 6.5 convolution_bitcast_fusion.1.z_ref
  74.3 16.3 %mixer_forward.1 = (f32[384,512]{1,0:T(8,128)S(1)}, bf16[384,512]{1,0:T(8,128)(2,1)S(1)}, f32[384,1]{1,0:T(8,128)S(1)}, f32[1,4,3,128,128]{4,3,2,1,0:T(8,128)S(1)}, bf16[1,4,3,128,128]{4,3,2,1,0:T(8,128)(2,1)S(1)}) custom-call(s32[1]{0:T(128)} %dynamic_slice.36.count_ref, f32[4,384,512]{2,1,0:T(8,128)S(1)} %convolution_bitcast_fusion.1.z_ref, ...), custom_call_target="tpu_custom_call" | custom-call | tf_op jit(solution)/shard_map/mixer_forward/pallas_call | solution.py:227
  111.2 21.0 %collective-permute-done.8 = f32[384]{0:T(512)S(1)} collective-permute-done((f32[384]{0:T(512)S(1)}, f32[384]{0:T(512)S(1)}, u32[]{:S(2)}, u32[]{:S(2)}) %collective-permute-start.8) | collective-permute-done | bytes 1568 | tf_op jit(solution)/shard_map/ppermute | solution.py:296
  132.2 9.0 %collective-permute-start.6 = (f32[384]{0:T(512)S(1)}, f32[384]{0:T(512)S(1)}, u32[]{:S(2)}, u32[]{:S(2)}) collective-permute-start(f32[384]{0:T(512)S(1)} %reduce.1), channel_id=1, source_target_pairs={{0,1},{1,2},{2,3},{3,0},{4,5},{5,6},{6,7},{7,4},{8,9},{9,10},{10,1... | collective-permute-start | bytes 4616 | tf_op jit(solution)/shard_map/ppermute | solution.py:296
  148.7 7.5 %collective-permute-done.14 = bf16[96,2048]{1,0:T(8,128)(2,1)S(1)} collective-permute-done((bf16[96,2048]{1,0:T(8,128)(2,1)S(1)}, bf16[96,2048]{1,0:T(8,128)(2,1)S(1)}, u32[]{:S(2)}, u32[]{:S(2)}) %collective-permute-start.14) | collective-permute-done | bytes 393248 | tf_op jit(solution)/shard_map/ppermute | solution.py:296
  156.2 25.4 %collective-permute-done.13 = bf16[96,2048]{1,0:T(8,128)(2,1)S(1)} collective-permute-done((bf16[96,2048]{1,0:T(8,128)(2,1)S(1)}, bf16[96,2048]{1,0:T(8,128)(2,1)S(1)}, u32[]{:S(2)}, u32[]{:S(2)}) %collective-permute-start.13) | collective-permute-done | bytes 393248 | tf_op jit(solution)/shard_map/ppermute | solution.py:296
  181.6 8.1 %convolution_bitcast_fusion = f32[2,384,1408]{2,1,0:T(8,128)S(1)} fusion(bf16[2,2048,1408]{2,1,0:T(8,128)(2,1)} %all-gather.9.cloned.1.call-done, bf16[96,2048]{1,0:T(8,128)(2,1)S(1)} %collective-permute-done.14, bf16[96,2048]{1,0:T(8,128)(2,1)S(1)} %collective-permute-done.13, bf16[96,2048]{1,0:T(8,128)(2,1)} %collective-permute-done.12, ...), kind=kOutput, calls=%fused_computation.13 | convolution fusion | flops 4435476480 | bytes 17432576 | tf_op jit(solution)/shard_map/td,jdf->jtf/dot_general | solution.py:456
  193.5 22.0 %all-gather.11.cloned.1.call-done = bf16[1408,2048]{1,0:T(8,128)(2,1)} async-done(((bf16[1408,256]{1,0:T(8,128)(2,1)}), bf16[1408,2048]{1,0:T(8,128)(2,1)}) %all-gather.11.cloned.1.call-update) | async-done | bytes 5767184 | tf_op jit(solution)/shard_map/all_gather | solution.py:392
  228.9 7.4 %collective-permute-done.17 = bf16[96,2048]{1,0:T(8,128)(2,1)} collective-permute-done((bf16[96,2048]{1,0:T(8,128)(2,1)}, bf16[96,2048]{1,0:T(8,128)(2,1)}, u32[]{:S(2)}, u32[]{:S(2)}) %collective-permute-start.17) | collective-permute-done | bytes 393248 | tf_op jit(solution)/shard_map/ppermute | solution.py:296
  236.3 16.2 %collective-permute-done.16 = bf16[96,2048]{1,0:T(8,128)(2,1)} collective-permute-done((bf16[96,2048]{1,0:T(8,128)(2,1)}, bf16[96,2048]{1,0:T(8,128)(2,1)}, u32[]{:S(2)}, u32[]{:S(2)}) %collective-permute-start.16) | collective-permute-done | bytes 393248 | tf_op jit(solution)/shard_map/ppermute | solution.py:296
  254.9 9.9 %collective-permute-start.20 = (bf16[96,2048]{1,0:T(8,128)(2,1)S(1)}, bf16[96,2048]{1,0:T(8,128)(2,1)S(1)}, u32[]{:S(2)}, u32[]{:S(2)}) collective-permute-start(bf16[96,2048]{1,0:T(8,128)(2,1)S(1)} %multiply_convert_fusion.5), channel_id=1, source_target_pairs={{0,3},{1,0},{2,1},{3,2},{4,7},{5,4},{6,5},{7,6},{8,11},{9,8},{10,9... | collective-permute-start | bytes 1179656 | tf_op jit(solution)/shard_map/ppermute | solution.py:296
  265.4 9.0 %collective-permute-done.20 = bf16[96,2048]{1,0:T(8,128)(2,1)S(1)} collective-permute-done((bf16[96,2048]{1,0:T(8,128)(2,1)S(1)}, bf16[96,2048]{1,0:T(8,128)(2,1)S(1)}, u32[]{:S(2)}, u32[]{:S(2)}) %collective-permute-start.20) | collective-permute-done | bytes 393248 | tf_op jit(solution)/shard_map/ppermute | solution.py:296
  274.3 25.2 %collective-permute-done.19 = bf16[96,2048]{1,0:T(8,128)(2,1)S(1)} collective-permute-done((bf16[96,2048]{1,0:T(8,128)(2,1)S(1)}, bf16[96,2048]{1,0:T(8,128)(2,1)S(1)}, u32[]{:S(2)}, u32[]{:S(2)}) %collective-permute-start.19) | collective-permute-done | bytes 393248 | tf_op jit(solution)/shard_map/ppermute | solution.py:296
  299.6 6.0 multiply_convert_fusion.1
  315.3 9.9 %collective-permute-done.23 = bf16[96,2048]{1,0:T(8,128)(2,1)S(1)} collective-permute-done((bf16[96,2048]{1,0:T(8,128)(2,1)S(1)}, bf16[96,2048]{1,0:T(8,128)(2,1)S(1)}, u32[]{:S(2)}, u32[]{:S(2)}) %collective-permute-start.23) | collective-permute-done | bytes 393248 | tf_op jit(solution)/shard_map/ppermute | solution.py:296
  325.2 15.1 %collective-permute-done.22 = bf16[96,2048]{1,0:T(8,128)(2,1)S(1)} collective-permute-done((bf16[96,2048]{1,0:T(8,128)(2,1)S(1)}, bf16[96,2048]{1,0:T(8,128)(2,1)S(1)}, u32[]{:S(2)}, u32[]{:S(2)}) %collective-permute-start.22) | collective-permute-done | bytes 393248 | tf_op jit(solution)/shard_map/ppermute | solution.py:296
  343.8 8.1 %collective-permute-start.24 = (bf16[96,2048]{1,0:T(8,128)(2,1)S(1)}, bf16[96,2048]{1,0:T(8,128)(2,1)S(1)}, u32[]{:S(2)}, u32[]{:S(2)}) collective-permute-start(bf16[96,2048]{1,0:T(8,128)(2,1)S(1)} %get-tuple-element.109), channel_id=1, source_target_pairs={{0,1},{1,2},{2,3},{3,0},{4,5},{5,6},{6,7},{7,4},{8,9},{9,10},{10,1... | collective-permute-start | bytes 1179656 | tf_op jit(solution)/shard_map/ppermute | solution.py:296
  354.5 7.6 %collective-permute-done.24 = bf16[96,2048]{1,0:T(8,128)(2,1)S(1)} collective-permute-done((bf16[96,2048]{1,0:T(8,128)(2,1)S(1)}, bf16[96,2048]{1,0:T(8,128)(2,1)S(1)}, u32[]{:S(2)}, u32[]{:S(2)}) %collective-permute-start.24) | collective-permute-done | bytes 393248 | tf_op jit(solution)/shard_map/ppermute | solution.py:296
  362.2 14.3 %collective-permute-done.25 = bf16[96,2048]{1,0:T(8,128)(2,1)S(1)} collective-permute-done((bf16[96,2048]{1,0:T(8,128)(2,1)S(1)}, bf16[96,2048]{1,0:T(8,128)(2,1)S(1)}, u32[]{:S(2)}, u32[]{:S(2)}) %collective-permute-start.25) | collective-permute-done | bytes 393248 | tf_op jit(solution)/shard_map/ppermute | solution.py:296
  380.6 6.9 %convolution_convert_fusion = bf16[1408,2048]{1,0:T(8,128)(2,1)} fusion(bf16[384,1408]{1,0:T(8,128)(2,1)S(1)} %copy-done.35, bf16[96,2048]{1,0:T(8,128)(2,1)} %copy-done.52, bf16[96,2048]{1,0:T(8,128)(2,1)} %copy-done.53, bf16[96,2048]{1,0:T(8,128)(2,1)} %copy-done.54, bf16[96,2048]{1,0:T(8,128)(2,1)S(1)} %copy-done.40), kind=kOutput, calls=%fused_computation.2 | convolution fusion | flops 2223767552 | bytes 8421376 | tf_op jit(solution)/shard_map/dot_general | solution.py:49
  387.8 8.8 %collective-permute-start.27 = (f32[96]{0:T(128)S(1)}, f32[96]{0:T(128)S(1)}, u32[]{:S(2)}, u32[]{:S(2)}) collective-permute-start(f32[96]{0:T(128)S(1)} %multiply_multiply_fusion.2), channel_id=1, source_target_pairs={{0,1},{1,2},{2,3},{3,0},{4,5},{5,6},{6,7},{7,4},{8,9},{9,10},{10,1... | collective-permute-start | bytes 1160 | tf_op jit(solution)/shard_map/ppermute | solution.py:296
  406.6 21.4 %mixer_backward.1 = (bf16[4,384,512]{2,1,0:T(8,128)(2,1)S(1)}, f32[1,512]{1,0:T(1,128)S(1)}) custom-call(s32[1]{0:T(128)} %dynamic_slice.36.count_ref, f32[4,384,512]{2,1,0:T(8,128)} %copy-done, f32[384,512]{1,0:T(8,128)S(1)} %copy-done.4, f32[384,512]{1,0:T(8,128)S(1)} %fusion.31.dact_ref, f32[384,1]{1,0:T(8,128)S(1)} %broadcast_in_dim.47.inv_ref, ...), custom_call_target="tpu_custom_call" | custom-call | tf_op jit(solution)/shard_map/mixer_backward/pallas_call | solution.py:266
  428.0 7.0 %convert_bitcast_fusion = bf16[4,2048,512]{1,2,0:T(8,128)(2,1)} fusion(bf16[4,384,512]{2,1,0:T(8,128)(2,1)S(1)} %get-tuple-element.35, bf16[384,2048]{1,0:T(8,128)(2,1)S(1)} %copy-done.19, f32[2048]{0:T(1024)S(1)} %bitcast.80, f32[384]{0:T(512)S(1)} %copy-done.47), kind=kOutput, calls=%fused_computation.1 | convolution fusion | flops 3228565504 | bytes 11544064 | tf_op jit(solution)/shard_map/td,jte->jde/dot_general | solution.py:492
  451.1 6.9 %bitcast_convert_fusion = bf16[384,2048]{1,0:T(8,128)(2,1)S(1)} fusion(bf16[4,384,512]{2,1,0:T(8,128)(2,1)S(1)} %get-tuple-element.35, bf16[4,2048,512]{2,1,0:T(8,128)(2,1)} %all-gather.5.cloned.1.call-done), kind=kOutput, calls=%fused_computation.17 | convolution fusion | flops 3222011904 | bytes 11534336 | tf_op jit(solution)/shard_map/jte,jde->td/dot_general | solution.py:494
  461.8 7.7 %collective-permute-done.32 = bf16[96,2048]{1,0:T(8,128)(2,1)S(1)} collective-permute-done((bf16[96,2048]{1,0:T(8,128)(2,1)S(1)}, bf16[96,2048]{1,0:T(8,128)(2,1)S(1)}, u32[]{:S(2)}, u32[]{:S(2)}) %collective-permute-start.32) | collective-permute-done | bytes 393248 | tf_op jit(solution)/shard_map/ppermute | solution.py:296
  469.6 21.9 %collective-permute-done.31 = bf16[96,2048]{1,0:T(8,128)(2,1)S(1)} collective-permute-done((bf16[96,2048]{1,0:T(8,128)(2,1)S(1)}, bf16[96,2048]{1,0:T(8,128)(2,1)S(1)}, u32[]{:S(2)}, u32[]{:S(2)}) %collective-permute-start.31) | collective-permute-done | bytes 393248 | tf_op jit(solution)/shard_map/ppermute | solution.py:296
  526.6 40.1 %reduce-scatter.5.cloned.1.call-done = bf16[4,256,512]{1,2,0:T(8,128)(2,1)} async-done(((bf16[4,2048,512]{1,2,0:T(8,128)(2,1)}), bf16[4,256,512]{1,2,0:T(8,128)(2,1)}) %reduce-scatter.5.cloned.1.call-update) | async-done | bytes 1048592 | tf_op jit(solution)/shard_map/reduce_scatter | solution.py:396
  566.8 5.8 add_multiply_fusion.1
  583.6 73.8 %reduce-scatter.9.cloned.1.call-done = bf16[2,256,1408]{2,1,0:T(8,128)(2,1)} async-done(((bf16[2,2048,1408]{2,1,0:T(8,128)(2,1)}), bf16[2,256,1408]{2,1,0:T(8,128)(2,1)}) %reduce-scatter.9.cloned.1.call-update) | async-done | bytes 1441808 | tf_op jit(solution)/shard_map/reduce_scatter | solution.py:396
  657.5 8.0 %add_multiply_fusion = (f32[2,256,1408]{2,1,0:T(8,128)}, f32[2,256,1408]{2,1,0:T(8,128)}, f32[2,256,1408]{2,1,0:T(8,128)}, f32[2,256,1408]{2,1,0:T(8,128)}) fusion(f32[2,256,1408]{2,1,0:T(8,128)} %param.36, f32[2,256,1408]{2,1,0:T(8,128)S(1)} %copy-done.14, f32[2,256,1408]{2,1,0:T(8,128)} %param.35, bf16[2,256,1408]{2,1,0:T(8,128)(2,1)} %reduce-scatter.9.cloned.1.call-done), kind=kLoop, calls=%fused_computation.20 | loop fusion | flops 6488064 | bytes 21626880 | tf_op jit(solution)/shard_map/add | solution.py:387
  (299 shorter events, 168.6 us)
Async XLA Ops:
  7.2 60.5 %all-gather.5.cloned.1.call-start = ((), (), s32[]{:S(2)}) async-start(), calls=%async_computation.4 | async-start | bytes 9437184 | tf_op jit(solution)/shard_map/all_gather | solution.py:392
  10.1 88.4 %all-gather.7.cloned.1.call-start = ((), (), s32[]{:S(2)}) async-start(), calls=%async_computation.5 | async-start | bytes 2359296 | tf_op jit(solution)/shard_map/all_gather | solution.py:392
  10.9 170.6 %all-gather.9.cloned.1.call-start = ((), (), s32[]{:S(2)}) async-start(), calls=%async_computation.6 | async-start | bytes 12976128 | tf_op jit(solution)/shard_map/all_gather | solution.py:392
  12.3 203.2 %all-gather.11.cloned.1.call-start = ((), (), s32[]{:S(2)}) async-start(), calls=%async_computation.7 | async-start | bytes 6488064 | tf_op jit(solution)/shard_map/all_gather | solution.py:392
  14.6 504.5 %reduce-scatter.7.cloned.1.call-start = ((), (), s32[]{:S(2)}) async-start(), calls=%async_computation.9 | async-start | bytes 2359296 | tf_op jit(solution)/shard_map/reduce_scatter | solution.py:396
  18.9 13.9 %collective-permute-start = (bf16[96,2048]{1,0:T(8,128)(2,1)S(1)}, bf16[96,2048]{1,0:T(8,128)(2,1)S(1)}, u32[]{:S(2)}, u32[]{:S(2)}) collective-permute-start(bf16[96,2048]{1,0:T(8,128)(2,1)S(1)} %copy-done.20), channel_id=1, source_target_pairs={{0,1},{1,2},{2,3},{3,0},{4,5},{5,6},{6,7},{7,4},{8,9},{9,10},{10,1... | collective-permute-start | bytes 1179656 | tf_op jit(solution)/shard_map/ppermute | solution.py:296
  20.5 28.2 %collective-permute-start.1 = (bf16[96,2048]{1,0:T(8,128)(2,1)S(1)}, bf16[96,2048]{1,0:T(8,128)(2,1)S(1)}, u32[]{:S(2)}, u32[]{:S(2)}) collective-permute-start(bf16[96,2048]{1,0:T(8,128)(2,1)S(1)} %copy-done.20), channel_id=1, source_target_pairs={{0,2},{1,3},{2,0},{3,1},{4,6},{5,7},{6,4},{7,5},{8,10},{9,11},{10,... | collective-permute-start | bytes 1179656 | tf_op jit(solution)/shard_map/ppermute | solution.py:296
  23.1 25.6 %collective-permute-start.2 = (bf16[96,2048]{1,0:T(8,128)(2,1)S(1)}, bf16[96,2048]{1,0:T(8,128)(2,1)S(1)}, u32[]{:S(2)}, u32[]{:S(2)}) collective-permute-start(bf16[96,2048]{1,0:T(8,128)(2,1)S(1)} %copy-done.20), channel_id=1, source_target_pairs={{0,3},{1,0},{2,1},{3,2},{4,7},{5,4},{6,5},{7,6},{8,11},{9,8},{10,9... | collective-permute-start | bytes 1179656 | tf_op jit(solution)/shard_map/ppermute | solution.py:296
  102.8 39.8 %collective-permute-start.11 = (bf16[96,2048]{1,0:T(8,128)(2,1)}, bf16[96,2048]{1,0:T(8,128)(2,1)S(1)}, u32[]{:S(2)}, u32[]{:S(2)}) collective-permute-start(bf16[96,2048]{1,0:T(8,128)(2,1)} %get-tuple-element.128), channel_id=1, source_target_pairs={{0,3},{1,0},{2,1},{3,2},{4,7},{5,4},{6,5},{7,6},{8,11},{9,8},{10,9... | collective-permute-start | bytes 1179656 | tf_op jit(solution)/shard_map/ppermute | solution.py:296
  106.1 36.5 %collective-permute-start.10 = (bf16[96,2048]{1,0:T(8,128)(2,1)}, bf16[96,2048]{1,0:T(8,128)(2,1)S(1)}, u32[]{:S(2)}, u32[]{:S(2)}) collective-permute-start(bf16[96,2048]{1,0:T(8,128)(2,1)} %get-tuple-element.129), channel_id=1, source_target_pairs={{0,2},{1,3},{2,0},{3,1},{4,6},{5,7},{6,4},{7,5},{8,10},{9,11},{10,... | collective-permute-start | bytes 1179656 | tf_op jit(solution)/shard_map/ppermute | solution.py:296
  106.1 36.5 %collective-permute-start.9 = (bf16[96,2048]{1,0:T(8,128)(2,1)}, bf16[96,2048]{1,0:T(8,128)(2,1)S(1)}, u32[]{:S(2)}, u32[]{:S(2)}) collective-permute-start(bf16[96,2048]{1,0:T(8,128)(2,1)} %get-tuple-element.127), channel_id=1, source_target_pairs={{0,1},{1,2},{2,3},{3,0},{4,5},{5,6},{6,7},{7,4},{8,9},{9,10},{10,1... | collective-permute-start | bytes 1179656 | tf_op jit(solution)/shard_map/ppermute | solution.py:296
  107.4 24.8 %collective-permute-start.8 = (f32[384]{0:T(512)S(1)}, f32[384]{0:T(512)S(1)}, u32[]{:S(2)}, u32[]{:S(2)}) collective-permute-start(f32[384]{0:T(512)S(1)} %reduce.1), channel_id=1, source_target_pairs={{0,3},{1,0},{2,1},{3,2},{4,7},{5,4},{6,5},{7,6},{8,11},{9,8},{10,9... | collective-permute-start | bytes 4616 | tf_op jit(solution)/shard_map/ppermute | solution.py:296
  110.1 31.1 %collective-permute-start.7 = (f32[384]{0:T(512)S(1)}, f32[384]{0:T(512)S(1)}, u32[]{:S(2)}, u32[]{:S(2)}) collective-permute-start(f32[384]{0:T(512)S(1)} %reduce.1), channel_id=1, source_target_pairs={{0,2},{1,3},{2,0},{3,1},{4,6},{5,7},{6,4},{7,5},{8,10},{9,11},{10,... | collective-permute-start | bytes 4616 | tf_op jit(solution)/shard_map/ppermute | solution.py:296
  146.5 35.0 %collective-permute-start.13 = (bf16[96,2048]{1,0:T(8,128)(2,1)S(1)}, bf16[96,2048]{1,0:T(8,128)(2,1)S(1)}, u32[]{:S(2)}, u32[]{:S(2)}) collective-permute-start(bf16[96,2048]{1,0:T(8,128)(2,1)S(1)} %multiply_convert_fusion.4), channel_id=1, source_target_pairs={{0,2},{1,3},{2,0},{3,1},{4,6},{5,7},{6,4},{7,5},{8,10},{9,11},{10,... | collective-permute-start | bytes 1179656 | tf_op jit(solution)/shard_map/ppermute | solution.py:296
  148.5 33.1 %collective-permute-start.12 = (bf16[96,2048]{1,0:T(8,128)(2,1)S(1)}, bf16[96,2048]{1,0:T(8,128)(2,1)}, u32[]{:S(2)}, u32[]{:S(2)}) collective-permute-start(bf16[96,2048]{1,0:T(8,128)(2,1)S(1)} %multiply_convert_fusion.4), channel_id=1, source_target_pairs={{0,1},{1,2},{2,3},{3,0},{4,5},{5,6},{6,7},{7,4},{8,9},{9,10},{10,1... | collective-permute-start | bytes 1179656 | tf_op jit(solution)/shard_map/ppermute | solution.py:296
  222.1 14.2 %collective-permute-start.17 = (bf16[96,2048]{1,0:T(8,128)(2,1)}, bf16[96,2048]{1,0:T(8,128)(2,1)}, u32[]{:S(2)}, u32[]{:S(2)}) collective-permute-start(bf16[96,2048]{1,0:T(8,128)(2,1)} %get-tuple-element.125), channel_id=1, source_target_pairs={{0,1},{1,2},{2,3},{3,0},{4,5},{5,6},{6,7},{7,4},{8,9},{9,10},{10,1... | collective-permute-start | bytes 1179656 | tf_op jit(solution)/shard_map/ppermute | solution.py:296
  223.6 28.9 %collective-permute-start.16 = (bf16[96,2048]{1,0:T(8,128)(2,1)}, bf16[96,2048]{1,0:T(8,128)(2,1)}, u32[]{:S(2)}, u32[]{:S(2)}) collective-permute-start(bf16[96,2048]{1,0:T(8,128)(2,1)} %get-tuple-element.126), channel_id=1, source_target_pairs={{0,2},{1,3},{2,0},{3,1},{4,6},{5,7},{6,4},{7,5},{8,10},{9,11},{10,... | collective-permute-start | bytes 1179656 | tf_op jit(solution)/shard_map/ppermute | solution.py:296
  226.0 26.5 %collective-permute-start.15 = (bf16[96,2048]{1,0:T(8,128)(2,1)}, bf16[96,2048]{1,0:T(8,128)(2,1)}, u32[]{:S(2)}, u32[]{:S(2)}) collective-permute-start(bf16[96,2048]{1,0:T(8,128)(2,1)} %get-tuple-element.124), channel_id=1, source_target_pairs={{0,3},{1,0},{2,1},{3,2},{4,7},{5,4},{6,5},{7,6},{8,11},{9,8},{10,9... | collective-permute-start | bytes 1179656 | tf_op jit(solution)/shard_map/ppermute | solution.py:296
  254.9 19.5 %collective-permute-start.20 = (bf16[96,2048]{1,0:T(8,128)(2,1)S(1)}, bf16[96,2048]{1,0:T(8,128)(2,1)S(1)}, u32[]{:S(2)}, u32[]{:S(2)}) collective-permute-start(bf16[96,2048]{1,0:T(8,128)(2,1)S(1)} %multiply_convert_fusion.5), channel_id=1, source_target_pairs={{0,3},{1,0},{2,1},{3,2},{4,7},{5,4},{6,5},{7,6},{8,11},{9,8},{10,9... | collective-permute-start | bytes 1179656 | tf_op jit(solution)/shard_map/ppermute | solution.py:296
  264.7 34.8 %collective-permute-start.19 = (bf16[96,2048]{1,0:T(8,128)(2,1)S(1)}, bf16[96,2048]{1,0:T(8,128)(2,1)S(1)}, u32[]{:S(2)}, u32[]{:S(2)}) collective-permute-start(bf16[96,2048]{1,0:T(8,128)(2,1)S(1)} %multiply_convert_fusion.5), channel_id=1, source_target_pairs={{0,2},{1,3},{2,0},{3,1},{4,6},{5,7},{6,4},{7,5},{8,10},{9,11},{10,... | collective-permute-start | bytes 1179656 | tf_op jit(solution)/shard_map/ppermute | solution.py:296
  265.3 34.3 %collective-permute-start.18 = (bf16[96,2048]{1,0:T(8,128)(2,1)S(1)}, bf16[96,2048]{1,0:T(8,128)(2,1)S(1)}, u32[]{:S(2)}, u32[]{:S(2)}) collective-permute-start(bf16[96,2048]{1,0:T(8,128)(2,1)S(1)} %multiply_convert_fusion.5), channel_id=1, source_target_pairs={{0,1},{1,2},{2,3},{3,0},{4,5},{5,6},{6,7},{7,4},{8,9},{9,10},{10,1... | collective-permute-start | bytes 1179656 | tf_op jit(solution)/shard_map/ppermute | solution.py:296
  311.2 14.0 %collective-permute-start.23 = (bf16[96,2048]{1,0:T(8,128)(2,1)S(1)}, bf16[96,2048]{1,0:T(8,128)(2,1)S(1)}, u32[]{:S(2)}, u32[]{:S(2)}) collective-permute-start(bf16[96,2048]{1,0:T(8,128)(2,1)S(1)} %get-tuple-element.122), channel_id=1, source_target_pairs={{0,1},{1,2},{2,3},{3,0},{4,5},{5,6},{6,7},{7,4},{8,9},{9,10},{10,1... | collective-permute-start | bytes 1179656 | tf_op jit(solution)/shard_map/ppermute | solution.py:296
  311.3 29.0 %collective-permute-start.22 = (bf16[96,2048]{1,0:T(8,128)(2,1)S(1)}, bf16[96,2048]{1,0:T(8,128)(2,1)S(1)}, u32[]{:S(2)}, u32[]{:S(2)}) collective-permute-start(bf16[96,2048]{1,0:T(8,128)(2,1)S(1)} %get-tuple-element.123), channel_id=1, source_target_pairs={{0,2},{1,3},{2,0},{3,1},{4,6},{5,7},{6,4},{7,5},{8,10},{9,11},{10,... | collective-permute-start | bytes 1179656 | tf_op jit(solution)/shard_map/ppermute | solution.py:296
  312.2 28.1 %collective-permute-start.21 = (bf16[96,2048]{1,0:T(8,128)(2,1)S(1)}, bf16[96,2048]{1,0:T(8,128)(2,1)S(1)}, u32[]{:S(2)}, u32[]{:S(2)}) collective-permute-start(bf16[96,2048]{1,0:T(8,128)(2,1)S(1)} %get-tuple-element.121), channel_id=1, source_target_pairs={{0,3},{1,0},{2,1},{3,2},{4,7},{5,4},{6,5},{7,6},{8,11},{9,8},{10,9... | collective-permute-start | bytes 1179656 | tf_op jit(solution)/shard_map/ppermute | solution.py:296
  343.8 18.4 %collective-permute-start.24 = (bf16[96,2048]{1,0:T(8,128)(2,1)S(1)}, bf16[96,2048]{1,0:T(8,128)(2,1)S(1)}, u32[]{:S(2)}, u32[]{:S(2)}) collective-permute-start(bf16[96,2048]{1,0:T(8,128)(2,1)S(1)} %get-tuple-element.109), channel_id=1, source_target_pairs={{0,1},{1,2},{2,3},{3,0},{4,5},{5,6},{6,7},{7,4},{8,9},{9,10},{10,1... | collective-permute-start | bytes 1179656 | tf_op jit(solution)/shard_map/ppermute | solution.py:296
  351.9 24.6 %collective-permute-start.25 = (bf16[96,2048]{1,0:T(8,128)(2,1)S(1)}, bf16[96,2048]{1,0:T(8,128)(2,1)S(1)}, u32[]{:S(2)}, u32[]{:S(2)}) collective-permute-start(bf16[96,2048]{1,0:T(8,128)(2,1)S(1)} %get-tuple-element.109), channel_id=1, source_target_pairs={{0,2},{1,3},{2,0},{3,1},{4,6},{5,7},{6,4},{7,5},{8,10},{9,11},{10,... | collective-permute-start | bytes 1179656 | tf_op jit(solution)/shard_map/ppermute | solution.py:296
  352.6 24.0 %collective-permute-start.26 = (bf16[96,2048]{1,0:T(8,128)(2,1)S(1)}, bf16[96,2048]{1,0:T(8,128)(2,1)S(1)}, u32[]{:S(2)}, u32[]{:S(2)}) collective-permute-start(bf16[96,2048]{1,0:T(8,128)(2,1)S(1)} %get-tuple-element.109), channel_id=1, source_target_pairs={{0,3},{1,0},{2,1},{3,2},{4,7},{5,4},{6,5},{7,6},{8,11},{9,8},{10,9... | collective-permute-start | bytes 1179656 | tf_op jit(solution)/shard_map/ppermute | solution.py:296
  379.3 142.3 %reduce-scatter.11.cloned.1.call-start = ((), (), s32[]{:S(2)}) async-start(), calls=%async_computation.11 | async-start | bytes 6488064 | tf_op jit(solution)/shard_map/reduce_scatter | solution.py:396
  387.5 179.2 %reduce-scatter.5.cloned.1.call-start = ((), (), s32[]{:S(2)}) async-start(), calls=%async_computation.8 | async-start | bytes 9437184 | tf_op jit(solution)/shard_map/reduce_scatter | solution.py:396
  435.0 222.4 %reduce-scatter.9.cloned.1.call-start = ((), (), s32[]{:S(2)}) async-start(), calls=%async_computation.10 | async-start | bytes 12976128 | tf_op jit(solution)/shard_map/reduce_scatter | solution.py:396
  459.9 31.5 %collective-permute-start.31 = (bf16[96,2048]{1,0:T(8,128)(2,1)S(1)}, bf16[96,2048]{1,0:T(8,128)(2,1)S(1)}, u32[]{:S(2)}, u32[]{:S(2)}) collective-permute-start(bf16[96,2048]{1,0:T(8,128)(2,1)S(1)} %get-tuple-element.120), channel_id=1, source_target_pairs={{0,2},{1,3},{2,0},{3,1},{4,6},{5,7},{6,4},{7,5},{8,10},{9,11},{10,... | collective-permute-start | bytes 1179656 | tf_op jit(solution)/shard_map/ppermute | solution.py:296
  459.9 31.5 %collective-permute-start.30 = (bf16[96,2048]{1,0:T(8,128)(2,1)S(1)}, bf16[96,2048]{1,0:T(8,128)(2,1)S(1)}, u32[]{:S(2)}, u32[]{:S(2)}) collective-permute-start(bf16[96,2048]{1,0:T(8,128)(2,1)S(1)} %get-tuple-element.118), channel_id=1, source_target_pairs={{0,1},{1,2},{2,3},{3,0},{4,5},{5,6},{6,7},{7,4},{8,9},{9,10},{10,1... | collective-permute-start | bytes 1179656 | tf_op jit(solution)/shard_map/ppermute | solution.py:296
  (77 other events, 1228.4 us)
Sparse Core Ops, SparseCore 0:
  10.5 57.1 all-gather.4
  70.2 28.2 all-gather.6
  101.0 67.7 all-gather.8
  171.1 44.3 all-gather.10
  379.5 49.4 reduce-scatter.6
  432.6 59.0 reduce-scatter.10
  495.2 71.5 reduce-scatter.4
  570.7 86.7 reduce-scatter.8

commit v2 on v1

v2 whole, which is shorter than its diff:
```python
import functools
import math

import jax
import jax.numpy as jnp
import numpy as np
from jax import lax
from jax.experimental import pallas as pl
from jax.experimental.pallas import tpu as pltpu
from jax.sharding import PartitionSpec as P

D = 2048
HEAD_DIM = 128
BLOCK = 32
CHUNK = 128
LEVELS = 7
VMEM_LIMIT = 16 * 1024 * 1024

EPS = 1e-06
MOMENT_RATE = 0.5
AVERAGE_RATE = 0.5
LEARN_RATE = 4e-05

BF = jnp.bfloat16
F32 = jnp.float32


def decay_sums():
    t = np.arange(CHUNK)[:, None]
    r = np.arange(CHUNK)[None, :]
    mats = []
    for level in range(LEVELS):
        half = 1 << level
        mid = (t // (2 * half)) * (2 * half) + half
        right = t >= mid
        mats.append(np.where(right, (r >= mid) & (r <= t), (r > t) & (r < mid)))
    mats.append(r <= t)
    mats.append(r > t)
    return np.stack(mats).astype(np.float32)


def dot(a, b):
    return lax.dot_general(a, b, (((1,), (0,)), ((), ())), preferred_element_type=F32)


def dot_nt(a, b):
    return lax.dot_general(a, b, (((1,), (1,)), ((), ())), preferred_element_type=F32)


def dot_tn(a, b):
    return lax.dot_general(a, b, (((0,), (0,)), ((), ())), preferred_element_type=F32)


def sigmoid(v):
    return 1.0 / (1.0 + jnp.exp(-v))


def mean_square(v):
    return jnp.mean(v * v, axis=-1, keepdims=True)


def norm_back(v, scale, weighted):
    return scale * weighted - v * (scale * scale * scale * jnp.mean(weighted * v, axis=-1, keepdims=True))


def forget_parts(z):
    small = jnp.exp(-jnp.abs(z))
    logf = jnp.minimum(z, 0.0) - jnp.log1p(small)
    key = jnp.where(z >= 0.0, small, 1.0) / (1.0 + small)
    return logf, key


def split_sum(mat, logf_pair):
    both = dot(mat, logf_pair)
    return both[:, :HEAD_DIM] + both[:, HEAD_DIM:]


def chunk_masks():
    row = lax.broadcasted_iota(jnp.int32, (CHUNK, CHUNK), 0)
    col = lax.broadcasted_iota(jnp.int32, (CHUNK, CHUNK), 1)
    return row, col, row ^ col


class RingRows:
    def __init__(self, rank, ranks, rows):
        self.rank = rank
        self.ranks = ranks
        self.size = rows // ranks
        self.step = math.gcd(CHUNK, self.size)

    def pieces(self, first):
        for at in range(first, first + CHUNK, self.step):
            place = lax.rem(self.rank - at // self.size + self.ranks, self.ranks)
            yield pl.ds(pl.multiple_of(place * self.size + at % self.size, self.step), self.step)

    def load(self, ref, first, *index):
        return jnp.concatenate([ref[(*index, piece)] for piece in self.pieces(first)], axis=0)

    def store(self, ref, first, value, *index):
        for i, piece in enumerate(self.pieces(first)):
            ref[(*index, piece)] = value[i * self.step : (i + 1) * self.step]


def mixer_forward_kernel(ranks, scalar_ref, z_ref, seg_row_ref, seg_col_ref, sums_ref, o_ref, square_ref, state_ref, pair_ref):
    head = pl.program_id(0)
    seqs, _, seq_len = seg_row_ref.shape
    chunks = seq_len // CHUNK
    ring = RingRows(scalar_ref[seqs], ranks, z_ref.shape[1])
    row, col, differ = chunk_masks()
    for seq, c in ((s, c) for s in range(seqs) for c in range(chunks)):
        first = seq * seq_len + c * CHUNK
        if c == 0:
            state = jnp.zeros((HEAD_DIM, HEAD_DIM), F32)
        z0, z1, value = (ring.load(z_ref, first, j) for j in range(3))
        query = z0 * sigmoid(z0)
        logf, key = forget_parts(z1)
        high = logf.astype(BF)
        pair = jnp.concatenate([high, (logf - high.astype(F32)).astype(BF)], axis=1)
        seg_col = seg_col_ref[seq, c * CHUNK : (c + 1) * CHUNK, :]
        seg_row = seg_row_ref[seq, :, c * CHUNK : (c + 1) * CHUNK]
        seg_last = seg_row[:, CHUNK - 1 :]
        value_low = value.astype(BF)
        scores = None
        for level in reversed(range(LEVELS)):
            decay = jnp.exp(split_sum(sums_ref[level], pair))
            right = ((row >> level) & 1) == 1
            mixed = (decay * jnp.where(right, query, key)).astype(BF)
            product = dot_nt(mixed, mixed)
            scores = product if scores is None else jnp.where(differ < (2 << level), product, scores)
        diagonal = jnp.sum(query * key, axis=1, keepdims=True)
        scores = jnp.where(differ == 0, diagonal, scores)
        scores = jnp.where(seg_col == seg_row, scores, 0.0).astype(BF)
        pair_ref[seq, 0, c] = scores
        out = dot(jnp.where(row >= col, scores, jnp.zeros_like(scores)), value_low)
        from_start = jnp.exp(split_sum(sums_ref[LEVELS], pair))
        if c > 0:
            carried = seg_col == seg_before
            reach = jnp.where(carried, query * from_start, 0.0).astype(BF)
            out = out + dot_nt(reach, state.astype(BF))
        state_ref[seq, 0, c] = state
        position = c * CHUNK + lax.broadcasted_iota(jnp.int32, (CHUNK, 1), 0)
        out = jnp.where(position < scalar_ref[seq] * BLOCK, out, 0.0)
        ring.store(o_ref, first, out)
        square = jnp.sum(out * out, axis=1, keepdims=True)
        square = jnp.where(head == 0, square, ring.load(square_ref, first) + square)
        ring.store(square_ref, first, square)
        if c < chunks - 1:
            to_end = jnp.exp(split_sum(sums_ref[LEVELS + 1], pair))
            tail = jnp.where(seg_col == seg_last, key * to_end, 0.0).astype(BF)
            fresh = dot_tn(value_low, tail)
            if c > 0:
                kept = jnp.where(seg_last == seg_before, from_start[CHUNK - 1 :], 0.0)
                fresh = fresh + state * kept
            state = fresh
            seg_before = seg_last


def mixer_backward_kernel(
    ranks, scalar_ref, z_ref, dout_ref, gate_ref, seg_row_ref, seg_col_ref, sums_ref, sums_t_ref, state_ref, pair_ref, dz_ref
):
    seqs, _, seq_len = seg_row_ref.shape
    chunks = seq_len // CHUNK
    ring = RingRows(scalar_ref[seqs], ranks, z_ref.shape[1])
    row, col, differ = chunk_masks()
    dz_ref[3] = gate_ref[...]
    for seq, c in ((s, c) for s in range(seqs) for c in reversed(range(chunks))):
        first = seq * seq_len + c * CHUNK
        z0, z1, value = (ring.load(z_ref, first, j) for j in range(3))
        gate0 = sigmoid(z0)
        query = z0 * gate0
        logf, key = forget_parts(z1)
        high = logf.astype(BF)
        pair = jnp.concatenate([high, (logf - high.astype(F32)).astype(BF)], axis=1)
        seg_col = seg_col_ref[seq, c * CHUNK : (c + 1) * CHUNK, :]
        seg_row = seg_row_ref[seq, :, c * CHUNK : (c + 1) * CHUNK]
        seg_last = seg_row[:, CHUNK - 1 :]
        value_low = value.astype(BF)
        position = c * CHUNK + lax.broadcasted_iota(jnp.int32, (CHUNK, 1), 0)
        dout = jnp.where(position < scalar_ref[seq] * BLOCK, ring.load(dout_ref, first), 0.0)
        dout_low = dout.astype(BF)

        dscore = jnp.where(row > col, dot_nt(dout_low, value_low), dot_nt(value_low, dout_low))
        dscore = jnp.where(seg_col == seg_row, dscore, 0.0).astype(BF)
        scores = pair_ref[seq, 0, c]
        zero = jnp.zeros_like(scores)
        dvalue = dot(jnp.where(col >= row, scores, zero), dout_low)
        diagonal = jnp.sum(dout * value, axis=1, keepdims=True)
        dquery = diagonal * key
        dkey = diagonal * query
        dlogf = jnp.zeros((CHUNK, HEAD_DIM), F32)
        for level in range(LEVELS):
            decay = jnp.exp(split_sum(sums_ref[level], pair))
            right = ((row >> level) & 1) == 1
            mixed = decay * jnp.where(right, query, key)
            dmixed = dot(jnp.where((differ >> level) == 1, dscore, zero), mixed.astype(BF))
            through = dmixed * decay
            dquery = dquery + jnp.where(right, through, 0.0)
            dkey = dkey + jnp.where(right, 0.0, through)
            dlogf = dlogf + dot(sums_t_ref[level], (dmixed * mixed).astype(BF))
        from_start = jnp.exp(split_sum(sums_ref[LEVELS], pair))
        total = from_start[CHUNK - 1 :]
        if c > 0:
            seg_before = seg_row_ref[seq, :, c * CHUNK - 1 : c * CHUNK]
            carried = seg_col == seg_before
            state = state_ref[seq, 0, c]
            reach = jnp.where(carried, query * from_start, 0.0)
            dreach = jnp.where(carried, dot(dout_low, state.astype(BF)), 0.0)
            dquery = dquery + dreach * from_start
            dlogf = dlogf + dot(sums_t_ref[LEVELS], (dreach * reach).astype(BF))
            dstate_new = dot_tn(dout_low, reach.astype(BF))
        if c < chunks - 1:
            to_end = jnp.exp(split_sum(sums_ref[LEVELS + 1], pair))
            in_tail = seg_col == seg_last
            tail = jnp.where(in_tail, key * to_end, 0.0)
            dstate_low = dstate.astype(BF)
            dtail = jnp.where(in_tail, dot(value_low, dstate_low), 0.0)
            dkey = dkey + dtail * to_end
            dlogf = dlogf + dot(sums_t_ref[LEVELS + 1], (dtail * tail).astype(BF))
            dvalue = dvalue + dot_nt(tail.astype(BF), dstate_low)
            if c > 0:
                kept = jnp.where(seg_last == seg_before, total, 0.0)
                dlogf = dlogf + jnp.sum(state * dstate, axis=0, keepdims=True) * kept
                dstate_new = dstate_new + dstate * kept
        if c > 0:
            dstate = dstate_new
        ring.store(dz_ref, first, (dquery * gate0 * (1.0 + z0 * (1.0 - gate0))).astype(BF), 0)
        ring.store(dz_ref, first, ((dlogf - dkey * (1.0 - key)) * key).astype(BF), 1)
        ring.store(dz_ref, first, dvalue.astype(BF), 2)


def mixer_call(kernel, name, operands, kinds, outputs, segments, z, ranks):
    seqs, seq_len = segments.shape
    rows, width = z.shape[1:]
    heads = width // HEAD_DIM
    chunks = seq_len // CHUNK
    matrices = (seqs, heads, chunks, HEAD_DIM, HEAD_DIM)
    shapes = {
        "z": (None, pl.BlockSpec((3, rows, HEAD_DIM), lambda h: (0, 0, h))),
        "dz": ((4, rows, width), pl.BlockSpec((4, rows, HEAD_DIM), lambda h: (0, 0, h))),
        "token": ((rows, width), pl.BlockSpec((rows, HEAD_DIM), lambda h: (0, h))),
        "column": ((rows, 1), pl.BlockSpec((rows, 1), lambda h: (0, 0))),
        "matrix": (matrices, pl.BlockSpec((seqs, 1) + matrices[2:], lambda h: (0, h, 0, 0, 0))),
        "segment_row": (None, pl.BlockSpec((seqs, 1, seq_len), lambda h: (0, 0, 0))),
        "segment_column": (None, pl.BlockSpec((seqs, seq_len, 1), lambda h: (0, 0, 0))),
        "sums": (None, pl.BlockSpec((LEVELS + 2, CHUNK, CHUNK), lambda h: (0, 0, 0))),
        "scalar": (None, pl.BlockSpec(memory_space=pltpu.SMEM)),
    }
    return pl.pallas_call(
        functools.partial(kernel, ranks),
        grid=(heads,),
        in_specs=[shapes[kind][1] for kind in kinds],
        out_specs=[shapes[kind][1] for kind, _ in outputs],
        out_shape=[jax.ShapeDtypeStruct(shapes[kind][0], dtype) for kind, dtype in outputs],
        compiler_params=pltpu.CompilerParams(vmem_limit_bytes=VMEM_LIMIT),
        name=name,
    )(*[pltpu.with_memory_space_constraint(v, pltpu.HBM) if v.ndim > 1 else v for v in operands])


def mixer_forward(z, segments, scalars, ranks):
    sums = jnp.asarray(decay_sums(), BF)
    return mixer_call(
        mixer_forward_kernel,
        "mixer_forward",
        (scalars, z, segments[:, None, :], segments[:, :, None], sums),
        ("scalar", "z", "segment_row", "segment_column", "sums"),
        (("token", F32), ("column", F32), ("matrix", F32), ("matrix", BF)),
        segments,
        z,
        ranks,
    )


def mixer_backward(z, dout, gate_dz, segments, scalars, states, pairs, ranks):
    sums = decay_sums()
    sums_t = jnp.asarray(sums.transpose(0, 2, 1), BF)
    return mixer_call(
        mixer_backward_kernel,
        "mixer_backward",
        (scalars, z, dout, gate_dz, segments[:, None, :], segments[:, :, None], jnp.asarray(sums, BF), sums_t, states, pairs),
        ("scalar", "z", "token", "token", "segment_row", "segment_column", "sums", "sums", "matrix", "matrix"),
        (("dz", BF),),
        segments,
        z,
        ranks,
    )[0]


FREE = pl.CostEstimate(flops=0, bytes_accessed=0, transcendentals=0)


EXTRA = 128
SMALL = 8


def to_columns(small):
    high = small.astype(BF).astype(F32)
    zeros = jnp.zeros((EXTRA - 2 * SMALL, small.shape[1]), F32)
    return jnp.concatenate([high, small - high, zeros], axis=0).T.astype(BF)


def from_columns(columns):
    rows = columns.astype(F32).T
    return rows[:SMALL] + rows[SMALL : 2 * SMALL]


def mixer_gradient_kernel(rows_ref, grads_ref, small_ref, *refs):
    *arrived, out_ref = refs
    rows = rows_ref[...]
    width = grads_ref.shape[2]
    for j in range(grads_ref.shape[0]):
        columns = slice(j * width, (j + 1) * width)
        total = dot_tn(rows, grads_ref[j])
        for ref in arrived:
            total = total + ref[:, columns].astype(F32)
        out_ref[:, columns] = total.astype(BF)
    last = slice(grads_ref.shape[0] * width, out_ref.shape[1])
    small = small_ref[...]
    for ref in arrived:
        small = small + from_columns(ref[:, last])
    out_ref[:, last] = to_columns(small)


def mixer_gradient(rows, span, grads, small, arrived, tile):
    tokens = rows.shape[0]
    count, _, width = grads.shape
    first, last = span
    tile = min(tile, last - first)
    whole = count * width + EXTRA
    return pl.pallas_call(
        mixer_gradient_kernel,
        grid=((last - first) // tile,),
        in_specs=[
            pl.BlockSpec((tokens, tile), lambda i: (0, first // tile + i)),
            pl.BlockSpec((count, tokens, width), lambda i: (0, 0, 0)),
            pl.BlockSpec((SMALL, tile), lambda i: (0, first // tile + i)),
        ]
        + [pl.BlockSpec((tile, whole), lambda i, at=at: (at // tile + i, 0)) for _, at in arrived],
        out_specs=pl.BlockSpec((tile, whole), lambda i: (i, 0)),
        out_shape=jax.ShapeDtypeStruct((last - first, whole), BF),
        compiler_params=pltpu.CompilerParams(vmem_limit_bytes=2 * VMEM_LIMIT),
        cost_estimate=FREE,
        name="mixer_gradient",
    )(rows, grads, small, *[a for a, _ in arrived])


def mixer_in_update_kernel(count, rows_ref, grads_ref, small_ref, *refs):
    arrived, columns = refs[:count], refs[count : 2 * count]
    (master_ref, moment_ref, average_ref, grad_out, master_out, moment_out, average_out, gain_out, small_out) = refs[
        2 * count :
    ]
    total = dot_tn(rows_ref[...], grads_ref[0])
    for ref in arrived:
        total = total + ref[...].astype(F32)
    moment = MOMENT_RATE * moment_ref[0] + total
    master = master_ref[0] - LEARN_RATE * (total + MOMENT_RATE * moment)
    grad_out[0] = total
    moment_out[0] = moment
    master_out[0] = master
    average_out[0] = AVERAGE_RATE * average_ref[0] + (1.0 - AVERAGE_RATE) * master
    product = (master_ref[0].astype(BF).astype(F32) * total).astype(BF)
    gain = dot_nt(jnp.ones((SMALL, product.shape[1]), BF), product)
    gain_out[...] = jnp.where(pl.program_id(0) == 0, gain, gain_out[...] + gain)
    small = small_ref[...]
    for ref in columns:
        small = small + from_columns(ref[...])
    small_out[...] = small


def mixer_in_update(rows, grads, small, arrived, master, moment, average):
    n = master.shape[1]
    count, tokens, width = grads.shape
    last = rows.shape[1] // n - 1
    weight = pl.BlockSpec((1, n, width), lambda k: (k, 0, 0))
    thin = pl.BlockSpec((SMALL, n), lambda k: (0, 0))
    behind = count * width // EXTRA
    return pl.pallas_call(
        functools.partial(mixer_in_update_kernel, len(arrived)),
        grid=(count,),
        in_specs=[
            pl.BlockSpec((tokens, n), lambda k: (0, last)),
            pl.BlockSpec((1, tokens, width), lambda k: (k, 0, 0)),
            pl.BlockSpec((SMALL, n), lambda k: (0, last)),
        ]
        + [pl.BlockSpec((n, width), lambda k, at=at: (at // n, k)) for _, at in arrived]
        + [pl.BlockSpec((n, EXTRA), lambda k, at=at: (at // n, behind)) for _, at in arrived]
        + [weight] * 3,
        out_specs=[weight] * 4 + [thin] * 2,
        out_shape=[jax.ShapeDtypeStruct(master.shape, F32)] * 4 + [jax.ShapeDtypeStruct((SMALL, n), F32)] * 2,
        compiler_params=pltpu.CompilerParams(vmem_limit_bytes=2 * VMEM_LIMIT),
        name="mixer_in_update",
    )(rows, grads, small, *[a for a, _ in arrived], *[a for a, _ in arrived], master, moment, average)


def pair_gradient_kernel(rows_ref, first_ref, second_ref, *refs):
    *arrived, out_ref = refs
    rows = rows_ref[...]
    for j, side in enumerate((first_ref, second_ref)):
        total = dot_tn(rows, side[...])
        for ref in arrived:
            total = total + ref[j].astype(F32)
        out_ref[j] = total.astype(BF)


def pair_gradient(rows, span, first_side, second_side, arrived, tile):
    tokens = rows.shape[0]
    width = first_side.shape[1]
    first, last = span
    tile = min(tile, last - first)
    side = pl.BlockSpec((tokens, width), lambda i: (0, 0))
    return pl.pallas_call(
        pair_gradient_kernel,
        grid=((last - first) // tile,),
        in_specs=[pl.BlockSpec((tokens, tile), lambda i: (0, first // tile + i)), side, side]
        + [pl.BlockSpec((2, tile, width), lambda i, at=at: (0, at // tile + i, 0)) for _, at in arrived],
        out_specs=pl.BlockSpec((2, tile, width), lambda i: (0, i, 0)),
        out_shape=jax.ShapeDtypeStruct((2, last - first, width), BF),
        compiler_params=pltpu.CompilerParams(vmem_limit_bytes=2 * VMEM_LIMIT),
        cost_estimate=FREE,
        name="pair_gradient",
    )(rows, first_side, second_side, *[a for a, _ in arrived])


def wide_gradient_kernel(left_ref, right_ref, *refs):
    *arrived, out_ref = refs
    total = dot_tn(left_ref[...], right_ref[...])
    for ref in arrived:
        total = total + ref[...].astype(F32)
    out_ref[...] = total.astype(BF)


def wide_gradient(left, right, span, arrived, tile):
    tokens, n = left.shape
    first, last = span
    tile = min(tile, last - first)
    return pl.pallas_call(
        wide_gradient_kernel,
        grid=((last - first) // tile,),
        in_specs=[
            pl.BlockSpec((tokens, n), lambda i: (0, 0)),
            pl.BlockSpec((tokens, tile), lambda i: (0, first // tile + i)),
        ]
        + [pl.BlockSpec((n, tile), lambda i, at=at: (0, at // tile + i)) for _, at in arrived],
        out_specs=pl.BlockSpec((n, tile), lambda i: (0, i)),
        out_shape=jax.ShapeDtypeStruct((n, last - first), BF),
        compiler_params=pltpu.CompilerParams(vmem_limit_bytes=VMEM_LIMIT),
        cost_estimate=FREE,
        name="wide_gradient",
    )(left, right, *[a for a, _ in arrived])


def split_column(v):
    high = v.astype(BF)
    return high, (v - high.astype(F32)).astype(BF)


def after_mixer_kernel(count, own_ref, square_ref, tokens_ref, gain_ref, *refs):
    arrived = refs[:count]
    resid_ref, scale_ref, norm_ref = refs[count:]
    mixed = own_ref[...].astype(F32)
    square = square_ref[...]
    for ref in arrived:
        mixed = mixed + ref[:, :D].astype(F32)
        square = square + ref[:, D : D + 1].astype(F32) + ref[:, D + 1 : D + 2].astype(F32)
    scale = lax.rsqrt(square / D + EPS)
    resid = tokens_ref[...].astype(F32) + mixed * scale
    resid_ref[...] = resid
    scale_ref[...] = scale
    norm_ref[...] = (resid * lax.rsqrt(mean_square(resid) + EPS) * gain_ref[...]).astype(BF)


def after_mixer(parts, square, tokens, gain, arrived):
    rows = tokens.shape[0]
    whole = pl.BlockSpec((rows, D), lambda i: (0, 0))
    column = pl.BlockSpec((rows, 1), lambda i: (0, 0))
    return pl.pallas_call(
        functools.partial(after_mixer_kernel, len(arrived)),
        grid=(1,),
        in_specs=[whole, column, whole, pl.BlockSpec((1, D), lambda i: (0, 0))]
        + [pl.BlockSpec((rows, D + EXTRA), lambda i: (0, 0))] * len(arrived),
        out_specs=[whole, column, whole],
        out_shape=[
            jax.ShapeDtypeStruct((rows, D), F32),
            jax.ShapeDtypeStruct((rows, 1), F32),
            jax.ShapeDtypeStruct((rows, D), BF),
        ],
        compiler_params=pltpu.CompilerParams(vmem_limit_bytes=VMEM_LIMIT),
        name="after_mixer",
    )(parts, square, tokens, gain, *arrived)


def after_feed_kernel(count, own_ref, resid_ref, tokens_ref, final_ref, gain_ref, scale_ref, *refs):
    arrived = refs[:count]
    grad_ref, payload_ref = refs[count:]
    grad = own_ref[...].astype(F32)
    for ref in arrived:
        grad = grad + ref[...].astype(F32)
    resid = resid_ref[...]
    grad = final_ref[...] + norm_back(resid, lax.rsqrt(mean_square(resid) + EPS), grad * gain_ref[...])
    grad_ref[...] = grad
    low = grad.astype(BF)
    payload_ref[:, :D] = low
    scale = scale_ref[...]
    mixed = resid - tokens_ref[...].astype(F32)
    coef = scale * scale * jnp.mean(low.astype(F32) * mixed, axis=-1, keepdims=True)
    columns = [part for v in (scale, coef) for part in split_column(v)]
    lane = lax.broadcasted_iota(jnp.int32, (low.shape[0], EXTRA), 1)
    extra = jnp.zeros((low.shape[0], EXTRA), F32)
    for i, part in enumerate(columns):
        extra = jnp.where(lane == i, part.astype(F32), extra)
    payload_ref[:, D:] = extra.astype(BF)


def after_feed(parts, resid, tokens, final, gain, scale, arrived):
    rows = tokens.shape[0]
    whole = pl.BlockSpec((rows, D), lambda i: (0, 0))
    column = pl.BlockSpec((rows, 1), lambda i: (0, 0))
    return pl.pallas_call(
        functools.partial(after_feed_kernel, len(arrived)),
        grid=(1,),
        in_specs=[whole] * 4 + [pl.BlockSpec((1, D), lambda i: (0, 0)), column] + [whole] * len(arrived),
        out_specs=[whole, pl.BlockSpec((rows, D + EXTRA), lambda i: (0, 0))],
        out_shape=[jax.ShapeDtypeStruct((rows, D), F32), jax.ShapeDtypeStruct((rows, D + EXTRA), BF)],
        compiler_params=pltpu.CompilerParams(vmem_limit_bytes=VMEM_LIMIT),
        name="after_feed",
    )(parts, resid, tokens, final, gain, scale, *arrived)


def column_sums_kernel(left_ref, right_ref, out_ref):
    product = left_ref[...].astype(F32) * right_ref[...].astype(F32)
    out_ref[...] = jnp.sum(product, axis=0, keepdims=True)


def column_sums(left, right):
    rows, width = left.shape
    tile = width // 4
    block = pl.BlockSpec((rows, tile), lambda i: (0, i))
    return pl.pallas_call(
        column_sums_kernel,
        grid=(4,),
        in_specs=[block, block],
        out_specs=pl.BlockSpec((1, tile), lambda i: (0, i)),
        out_shape=jax.ShapeDtypeStruct((1, width), F32),
        compiler_params=pltpu.CompilerParams(vmem_limit_bytes=VMEM_LIMIT),
        cost_estimate=FREE,
        name="column_sums",
    )(left, right)[0]


def project_back_kernel(grads_ref, weight_ref, out_ref):
    total = dot_nt(grads_ref[0], weight_ref[0])
    for j in range(1, grads_ref.shape[0]):
        total = total + dot_nt(grads_ref[j], weight_ref[j])
    out_ref[...] = total.astype(BF)


def project_back(grads, weight, tile):
    count, rows, width = grads.shape
    n = weight.shape[1]
    return pl.pallas_call(
        project_back_kernel,
        grid=(n // tile,),
        in_specs=[
            pl.BlockSpec((count, rows, width), lambda i: (0, 0, 0)),
            pl.BlockSpec((count, tile, width), lambda i: (0, i, 0)),
        ],
        out_specs=pl.BlockSpec((rows, tile), lambda i: (0, i)),
        out_shape=jax.ShapeDtypeStruct((rows, n), BF),
        compiler_params=pltpu.CompilerParams(vmem_limit_bytes=VMEM_LIMIT),
        cost_estimate=pl.CostEstimate(flops=0, bytes_accessed=100_000_000, transcendentals=0),
        name="project_back",
    )(grads, weight)


def take_blocks_kernel(order_ref, in_ref, out_ref):
    out_ref[...] = in_ref[...]


def take_blocks(v, order):
    rows, width = v.shape
    count = order.shape[0]
    block = (rows, width // count)
    return pl.pallas_call(
        take_blocks_kernel,
        grid_spec=pltpu.PrefetchScalarGridSpec(
            num_scalar_prefetch=1,
            grid=(count,),
            in_specs=[pl.BlockSpec(block, lambda i, order: (0, order[i]))],
            out_specs=pl.BlockSpec(block, lambda i, order: (0, i)),
        ),
        out_shape=jax.ShapeDtypeStruct(v.shape, v.dtype),
        compiler_params=pltpu.CompilerParams(vmem_limit_bytes=VMEM_LIMIT),
        cost_estimate=FREE,
        name="take_blocks",
    )(order, v)


def mixer_out_update_kernel(count, act_ref, rows_ref, *refs):
    arrived = refs[:count]
    master_ref, moment_ref, average_ref, grad_out, master_out, moment_out, average_out = refs[count:]
    total = arrived[0][...].astype(F32)
    for ref in arrived[1:]:
        total = total + ref[...].astype(F32)
    total = dot_tn(act_ref[...], rows_ref[...]) + total.T
    moment = MOMENT_RATE * moment_ref[...] + total
    master = master_ref[...] - LEARN_RATE * (total + MOMENT_RATE * moment)
    grad_out[...] = total
    moment_out[...] = moment
    master_out[...] = master
    average_out[...] = AVERAGE_RATE * average_ref[...] + (1.0 - AVERAGE_RATE) * master


def mixer_out_update(act, rows, arrived, master, moment, average):
    n = master.shape[1]
    tokens, width = act.shape
    last = rows.shape[1] // n - 1
    whole = pl.BlockSpec((width, n), lambda i: (0, 0))
    return pl.pallas_call(
        functools.partial(mixer_out_update_kernel, len(arrived)),
        grid=(1,),
        in_specs=[pl.BlockSpec((tokens, width), lambda i: (0, 0)), pl.BlockSpec((tokens, n), lambda i: (0, last))]
        + [pl.BlockSpec((n, width), lambda i, at=at: (at // n, 0)) for _, at in arrived]
        + [whole] * 3,
        out_specs=[whole] * 4,
        out_shape=[jax.ShapeDtypeStruct(master.shape, F32)] * 4,
        compiler_params=pltpu.CompilerParams(vmem_limit_bytes=VMEM_LIMIT),
        name="mixer_out_update",
    )(act, rows, *[a for a, _ in arrived], master, moment, average)


def turn(v, axis, step):
    n = lax.axis_size(axis)
    return lax.ppermute(v, axis, [(i, (i + step) % n) for i in range(n)])


def swap(v, axis, bit):
    n = lax.axis_size(axis)
    return lax.ppermute(v, axis, [(i, i ^ bit) for i in range(n)])


def gather_near(v, axis):
    n = lax.axis_size(axis)
    return jnp.concatenate([v] + [turn(v, axis, k) for k in range(1, n)], axis=0)


def scatter_near(v, axis):
    n = lax.axis_size(axis)
    rows = v.shape[0] // n
    total = v[:rows].astype(F32)
    for k in range(1, n):
        total = total + turn(v[k * rows : (k + 1) * rows], axis, -k).astype(F32)
    return total


def gather_gains(v):
    bit = 1
    me = lax.axis_index("dp")
    while bit < lax.axis_size("dp"):
        other = swap(v, "dp", bit)
        upper = (me & bit) > 0
        v = jnp.concatenate([jnp.where(upper, other, v), jnp.where(upper, v, other)], axis=1)
        bit *= 2
    return v


def apply_update(master, moment, average, gradient):
    moment_new = MOMENT_RATE * moment + gradient
    master_new = master - LEARN_RATE * (gradient + MOMENT_RATE * moment_new)
    average_new = AVERAGE_RATE * average + (1.0 - AVERAGE_RATE) * master_new
    return (gradient, master_new, moment_new, average_new)


def gather_weight(w, dim):
    return lax.all_gather(w.astype(BF), "dp", axis=dim, tiled=True)


def link_bits():
    bits = []
    bit = 2
    while bit < lax.axis_size("dp"):
        bits.append(bit)
        bit *= 2
    return bits, bits[::-1]


def block_order(bits):
    if not bits:
        return [0]
    rest = block_order(bits[1:])
    return [bits[0] ^ r for r in rest] + rest


def exchange_order(me):
    even, odd = (block_order(bits) for bits in link_bits())
    order_even = [1 ^ r for r in odd] + even
    order_odd = [1 ^ r for r in even] + odd
    return me ^ jnp.where((me & 1) == 0, jnp.array(order_even, jnp.int32), jnp.array(order_odd, jnp.int32))


def cross_swap(v, stage):
    even, odd = link_bits()
    n = lax.axis_size("dp")
    return lax.ppermute(v, "dp", [(i, i ^ (odd if i & 1 else even)[stage]) for i in range(n)])


def after(v, *others):
    return lax.optimization_barrier((v,) + others)[0]


class GradientSum:
    def __init__(self, piece):
        self.piece = piece
        self.at = 0
        self.left = D
        self.received = []

    def arrived(self):
        return [(r, self.at - first) for r, first in self.received]

    def send(self):
        self.left //= 2
        give = self.piece(self.at, self.at + self.left, self.arrived())
        stage = len(self.received) - 1
        self.at += self.left
        self.received.append((swap(give, "dp", 1) if stage < 0 else cross_swap(give, stage), self.at))
        return give

    def send_rest(self):
        while self.left > D // lax.axis_size("dp"):
            give = self.send()
        return give

    def last(self):
        return self.at, D, self.arrived()


def two_parts(v):
    high = lax.reduce_precision(v, 8, 7)
    return [high.astype(BF), (v - high).astype(BF)]


def pack_columns(values):
    parts = jnp.stack([part for v in values for part in two_parts(v)], axis=1)
    return jnp.pad(parts, ((0, 0), (0, EXTRA - parts.shape[1])))


def unpack_columns(v, count):
    return [v[:, 2 * i].astype(F32) + v[:, 2 * i + 1].astype(F32) for i in range(count)]


def gather_block_weight(w, dim):
    me = lax.axis_index("dp")
    core = me & 1
    even, odd = (block_order(bits) for bits in link_bits())
    order_even = [1 ^ r for r in odd] + even
    order_odd = [1 ^ r for r in even] + odd
    v = w.astype(BF)
    width = v.shape[dim]
    for stage in reversed(range(len(link_bits()[0]))):
        v = jnp.concatenate([cross_swap(v, stage), v], axis=dim)
    parts = [swap(v, "dp", 1), v]
    shape = list(v.shape)
    shape[dim] *= 2
    whole = jnp.zeros(shape, BF)
    for i, (a, b) in enumerate(zip(order_even, order_odd)):
        part = parts[i * 2 // len(order_even)]
        at = i % (len(order_even) // 2) * width
        block = lax.slice_in_dim(part, at, at + width, axis=dim)
        whole = lax.dynamic_update_slice_in_dim(whole, block, (me ^ jnp.where(core == 0, a, b)) * width, dim)
    return whole


def per_device(
    tokens,
    teacher,
    segments,
    block_counts,
    loss_mask,
    mixer_in,
    mixer_in_moment,
    mixer_in_average,
    mixer_out,
    mixer_out_moment,
    mixer_out_average,
    feed_in,
    feed_in_moment,
    feed_in_average,
    feed_out,
    feed_out_moment,
    feed_out_average,
    norm_gains,
    norm_gains_moment,
    norm_gains_average,
):
    mixer_in_work = gather_weight(mixer_in, 1)
    mixer_out_work = gather_block_weight(mixer_out, 1)
    feed_in_work = gather_weight(feed_in, 1)
    feed_out_work = gather_weight(feed_out, 1)
    gains = gather_gains(norm_gains.astype(BF)).astype(F32)

    row_total = tokens.shape[0]
    seq_here, seq_len = segments.shape
    seq_all = block_counts.shape[0]
    data_rank = lax.axis_index("dp")
    model_rank = lax.axis_index("mp")
    model_size = lax.axis_size("mp")
    local_counts = lax.dynamic_slice_in_dim(block_counts, data_rank * seq_here, seq_here, 0)
    order = exchange_order(data_rank.astype(jnp.int32))
    scalars = jnp.concatenate([local_counts, model_rank[None].astype(jnp.int32)])
    column = jnp.arange(seq_len, dtype=jnp.int32)
    live_all = (column[None, :] < BLOCK * block_counts[:, None]).astype(F32)
    total_count = jnp.sum(loss_mask.reshape(seq_all, seq_len).astype(F32) * live_all)
    first_row = (data_rank * model_size + model_rank) * row_total
    valid = lax.dynamic_slice_in_dim(loss_mask.astype(F32) * live_all.reshape(-1), first_row, row_total, 0)

    inputs = tokens.astype(F32)
    inputs_scale = lax.rsqrt(mean_square(inputs) + EPS)
    tokens_full = gather_near(tokens, "mp").astype(F32)
    first_full = (tokens_full * lax.rsqrt(mean_square(tokens_full) + EPS) * gains[0]).astype(BF)
    z = jnp.einsum("td,jde->jte", first_full, mixer_in_work, preferred_element_type=F32)
    gate_z = z[3]
    local_width = z.shape[2]
    gain_out = lax.dynamic_slice_in_dim(gains[2], model_rank * local_width, local_width, 0)[None]
    recurrent, square, states, pairs = mixer_forward(z, segments, scalars, model_size)
    gate_z_sig = jax.nn.sigmoid(gate_z)
    gate_z_act = gate_z * gate_z_sig
    act_raw = (recurrent * gain_out * gate_z_act).astype(BF)
    mixed_parts = dot(act_raw, mixer_out_work).astype(BF)
    arrived = []
    for k in range(1, model_size):
        rows = slice(k * row_total, (k + 1) * row_total)
        payload = jnp.concatenate([mixed_parts[rows], pack_columns([square[rows, 0]])], axis=1)
        arrived.append(turn(payload, "mp", -k))
    first_blocks = take_blocks(first_full, order)
    *arrived, first_blocks = lax.optimization_barrier((*arrived, first_blocks))
    resid, out_scale_here, norm_second = after_mixer(mixed_parts, square, tokens, gains[1:2], arrived)

    second_full = gather_near(norm_second, "mp")
    gate_up = jnp.einsum("td,jdf->jtf", second_full, feed_in_work, preferred_element_type=F32)
    gate_sig = jax.nn.sigmoid(gate_up[0])
    gate_act = gate_up[0] * gate_sig
    hidden_low = (gate_act * gate_up[1]).astype(BF)
    final = resid + scatter_near(dot(hidden_low, feed_out_work).astype(BF), "mp")
    output = final.astype(BF)

    error = (final - teacher.astype(F32)) * valid[:, None]
    square_sum = jnp.sum(error * error)
    token_slots = row_total * lax.axis_size("dp") * model_size
    grad_final = token_slots / total_count * error

    grad_full = gather_near(grad_final.astype(BF), "mp")
    grad_hidden = dot_nt(grad_full, feed_out_work)
    grad_gate = (grad_hidden * gate_up[1] * gate_sig * (1.0 + gate_up[0] * (1.0 - gate_sig))).astype(BF)
    grad_up = (grad_hidden * gate_act).astype(BF)
    grad_second_parts = (dot_nt(grad_gate, feed_in_work[0]) + dot_nt(grad_up, feed_in_work[1])).astype(BF)
    parts = [grad_second_parts[k * row_total : (k + 1) * row_total] for k in range(1, model_size)]
    *parts, grad_late = lax.optimization_barrier((*parts, grad_full))
    arrived = [turn(part, "mp", -k) for k, part in enumerate(parts, 1)]
    grad_blocks = take_blocks(grad_late, order)
    feed_out_sum = GradientSum(
        lambda a, b, arrived: wide_gradient(hidden_low, grad_blocks, (a, b), arrived, 512)
    )
    sent = feed_out_sum.send()
    feed_in_grad = pair_gradient(second_full, (0, D), grad_gate, after(grad_up, sent), [], 256)
    gain_two_grad = column_sums(grad_second_parts, after(second_full, feed_in_grad)) / gains[1]
    sent = feed_out_sum.send()
    *arrived, feed_in_grad, gain_two_grad, _ = lax.optimization_barrier((*arrived, feed_in_grad, gain_two_grad, sent))
    grad_resid, payload = after_feed(
        grad_second_parts, resid, tokens, grad_final, gains[1:2], out_scale_here, arrived
    )

    pieces = [payload] + [turn(payload, "mp", k) for k in range(1, model_size)]
    *pieces, _ = lax.optimization_barrier((*pieces, feed_out_sum.send_rest()))
    payload = jnp.concatenate(pieces, axis=0)
    resid_full = payload[:, :D]
    out_scale, coef = (v[:, None] for v in unpack_columns(payload[:, D:], 2))
    grad_act = dot_nt(resid_full, mixer_out_work)
    act_low = (act_raw.astype(F32) * out_scale).astype(BF)
    normed = recurrent * out_scale
    gate_dz = (grad_act * normed * gain_out * gate_z_sig * (1.0 + gate_z * (1.0 - gate_z_sig))).astype(BF)
    grad_normed = grad_act * gate_z_act
    gain_out_grad = jnp.sum(grad_normed * normed, axis=0)
    grad_recurrent = out_scale * (grad_normed * gain_out) - recurrent * coef

    gain_out_full = lax.dynamic_update_slice_in_dim(
        jnp.zeros((D,), F32), gain_out_grad, model_rank * local_width, 0
    )
    zero = jnp.zeros((D,), F32)
    small = jnp.stack([gain_two_grad, gain_out_full, jnp.full((D,), square_sum)] + [zero] * (SMALL - 3))
    small = take_blocks(small, order)
    dz = mixer_backward(z, grad_recurrent, gate_dz, segments, scalars, states, pairs, model_size)

    in_sum = GradientSum(None)

    def in_piece(dz_then):
        return lambda a, b, arrived: mixer_gradient(first_blocks, (a, b), dz_then, small, arrived, 256)

    in_sum.piece = in_piece(dz)
    sent = in_sum.send()
    grad_first_parts = project_back(after(dz, sent), mixer_in_work, 512)
    in_sum.piece = in_piece(after(dz, grad_first_parts))
    sent = in_sum.send()
    parts = [grad_first_parts[k * row_total : (k + 1) * row_total] for k in range(1, model_size)]
    *parts, act_low, resid_full, dz_then, grad_blocks = lax.optimization_barrier(
        (*parts, act_low, resid_full, dz, grad_blocks, sent)
    )[:-1]
    arrived = [turn(part, "mp", -k) for k, part in enumerate(parts, 1)]

    resid_blocks = take_blocks(resid_full, order)

    def out_piece(a, b, arrived, dtype=BF):
        out = dot_tn(resid_blocks[:, a:b], act_low)
        for r, at in arrived:
            out = out + r[at : at + b - a].astype(F32)
        return out.astype(dtype)

    out_sum = GradientSum(out_piece)
    out_sum.send()
    at, _, feed_arrived = feed_out_sum.last()
    feed_out_share = wide_gradient(hidden_low, grad_blocks, (at, D), feed_arrived, 512)
    fourth = apply_update(feed_out, feed_out_moment, feed_out_average, feed_out_share.astype(F32))

    in_sum.piece = in_piece(dz_then)
    sent = in_sum.send_rest()
    out_sum.send()
    resid_blocks = after(resid_blocks, sent)
    out_sum.send_rest()
    feed_in_share = lax.psum_scatter(feed_in_grad, "dp", scatter_dimension=1, tiled=True)
    feed_in_share = after(feed_in_share, sent)
    third = apply_update(feed_in, feed_in_moment, feed_in_average, feed_in_share.astype(F32))
    *arrived, _ = lax.optimization_barrier((*arrived, sent))
    grad_first = grad_first_parts[:row_total].astype(F32)
    for piece in arrived:
        grad_first = grad_first + piece.astype(F32)
    tokens_grad = (grad_resid + norm_back(inputs, inputs_scale, grad_first * gains[0])).astype(BF)
    *first, gain_one, small = mixer_in_update(
        first_blocks, after(dz, third[3], tokens_grad), small, in_sum.last()[2], mixer_in, mixer_in_moment, mixer_in_average
    )
    sums = jnp.concatenate([gain_one[:1], small[:3]])
    resid_blocks = after(resid_blocks, sums)
    second = tuple(
        mixer_out_update(act_low, resid_blocks, out_sum.last()[2], mixer_out, mixer_out_moment, mixer_out_average)
    )
    sums = sums + sum(turn(sums, "mp", k) for k in range(1, model_size))
    sums = after(sums, second[3])
    gains_share = jnp.concatenate([sums[:1] / norm_gains[:1].astype(BF).astype(F32), sums[1:3]])
    loss_value = sums[3, 0] / (total_count * D)
    fifth = apply_update(norm_gains, norm_gains_moment, norm_gains_average, gains_share)
    return (output, tokens_grad, loss_value) + tuple(first) + second + third + fourth + fifth


def solution(mesh):
    tokens = P(("dp", "mp"), None)
    stacked = P(None, "dp", "mp")
    flat = P("mp", "dp")
    gains = P(None, "dp")
    return jax.shard_map(
        per_device,
        mesh=mesh,
        in_specs=(tokens, tokens, P("dp", None), P(), P())
        + (stacked,) * 3 + (flat,) * 3 + (stacked,) * 3 + (flat,) * 3 + (gains,) * 3,
        out_specs=(tokens, tokens, P()) + (stacked,) * 4 + (flat,) * 4 + (stacked,) * 4 + (flat,) * 4 + (gains,) * 4,
        check_vma=False,
    )
```

time: 681 us -> 530 us (0.78)
  waiting for transfers between devices: 382 us -> 187 us
  Pallas kernels: 37.7 us -> 87.8 us
  matrix products: 70 us -> 44.6 us
  local copies, waits for them, and re-layouts: 34.3 us -> 52.2 us
  other arithmetic: 46.8 us -> 39.9 us
    reduce_scatter x4 -> x1, waiting for transfers between devices: 114 us -> 0.01 us  [per_device(): lax.psum_scatter(feed_in_grad, 'dp', scatter_dimension=1, tiled=True)]
    ppermute x30 -> x27, waiting for transfers between devices: 212 us -> 153 us  [turn(): return lax.ppermute(v, axis, [(i, (i + step) % n) for i in range(n)])]
    pallas_call x2 -> x20, Pallas kernels: 37.7 us -> 87.8 us  [the longest x2 37.8 us: mixer_call(): pl.pallas_call(functools.partial(kernel, ranks), grid=(heads,), in_specs=...]
    all_gather x4 -> x3, waiting for transfers between devices: 44.6 us -> 9.67 us  [gather_weight(): return lax.all_gather(w.astype(BF), 'dp', axis=dim, tiled=True)]
    ppermute x0 -> x8, waiting for transfers between devices: none -> 21 us  [cross_swap(): lax.ppermute(v, 'dp', [(i, i ^ (odd if i & 1 else even)[stage]) for i in...]
    dot_general x4 -> x3, matrix products: 19.2 us -> 4.19 us  [dot_tn(): lax.dot_general(a, b, (((0,), (0,)), ((), ())), preferred_element_type=F32)]
    dot_general x2 -> x0, matrix products: 13.9 us -> none  [the longest x1 7 us: per_device(): jnp.einsum('td,jte->jde', first_full, dz, preferred_element_type=F32)]
    unnamed x133 -> x208, local copies, waits for them, and re-layouts: 28.6 us -> 39.2 us
  transfers between devices with their start and end apart: 46 -> 46, of which waited for: 30 -> 21; matrix products, arithmetic and copies ran while one was open for 15% -> 14% of each run, Pallas kernels for 6% -> 16%
where the time goes in v2:
time: 530 us; the launch traced here: 521 us
  waiting for transfers between devices  187 us (35%)
  starting transfers between devices  91.3 us (17%)
  Pallas kernels  87.8 us (17%)
  local copies, waits for them, and re-layouts  52.2 us (10%)
  matrix products  44.6 us (8%)
  other arithmetic  39.9 us (8%)
  between operations  18.6 us (4%)
    ppermute x27, waiting for transfers between devices, turn(): return lax.ppermute(v, axis, [(i, (i + step) % n) for i in range(n)])  153 us
    ppermute x27, starting transfers between devices, turn(): return lax.ppermute(v, axis, [(i, (i + step) % n) for i in range(n)])  74.8 us
    unnamed x208, local copies, waits for them, and re-layouts  39.2 us
    pallas_call x2, Pallas kernels, mixer_call(): pl.pallas_call(functools.partial(kernel, ranks), grid=(heads,), in_specs=...  37.8 us
    ppermute x8, waiting for transfers between devices, cross_swap(): lax.ppermute(v, 'dp', [(i, i ^ (odd if i & 1 else even)[stage]) for i in...  21 us
    dot_general x4, matrix products, dot_nt(): lax.dot_general(a, b, (((1,), (1,)), ((), ())), preferred_element_type=F32)  15.7 us
    add x3, other arithmetic, apply_update(): average_new = AVERAGE_RATE * average + (1.0 - AVERAGE_RATE) * master_new  12.4 us
  transfers between devices with their start and end apart: 46, of which 21 were waited for; matrix products, arithmetic and copies ran while one was open for 14% of the time, Pallas kernels for 16%

profile of v2, /device:TPU:0, one launch (start us, length us, event | category | flops | bytes accessed | tf_op | source)
XLA Modules:
  0.0 521.2 jit_solution(15206182625143332745)
XLA Ops:
  13.8 4.7 collective-permute-start.2
  24.3 6.6 %collective-permute-done.6 = bf16[512,256]{1,0:T(8,128)(2,1)S(1)} collective-permute-done((bf16[512,256]{1,0:T(8,128)(2,1)S(1)}, bf16[512,256]{1,0:T(8,128)(2,1)S(1)}, u32[]{:S(2)}, u32[]{:S(2)}) %collective-permute-start.6) | collective-permute-done | bytes 262176 | tf_op jit(solution)/shard_map/ppermute | solution.py:702
  36.5 5.0 collective-permute-done.7
  43.6 9.1 %collective-permute-done.1 = bf16[96,2048]{1,0:T(8,128)(2,1)} collective-permute-done((bf16[96,2048]{1,0:T(8,128)(2,1)S(1)}, bf16[96,2048]{1,0:T(8,128)(2,1)}, u32[]{:S(2)}, u32[]{:S(2)}) %collective-permute-start.1) | collective-permute-done | bytes 393248 | tf_op jit(solution)/shard_map/ppermute | solution.py:632
  63.4 9.6 %all-gather.4.cloned.1.call-done.weight_ref = bf16[4,2048,512]{2,1,0:T(8,128)(2,1)} async-done(((bf16[4,256,512]{2,1,0:T(8,128)(2,1)}), bf16[4,2048,512]{2,1,0:T(8,128)(2,1)}) %all-gather.4.cloned.1.call-update) | async-done | bytes 8388624 | tf_op jit(solution)/shard_map/all_gather | solution.py:673
  73.0 8.4 %convolution_bitcast_fusion.1.z_ref = f32[4,384,512]{2,1,0:T(8,128)} fusion(bf16[4,2048,512]{2,1,0:T(8,128)(2,1)} %all-gather.4.cloned.1.call-done.weight_ref, bf16[384,2048]{1,0:T(8,128)(2,1)S(1)} %fusion.4.in_ref), kind=kOutput, calls=%fused_computation.23 | convolution fusion | flops 3221225472 | bytes 13107200 | tf_op jit(solution)/shard_map/td,jde->jte/dot_general | solution.py:819
  81.4 16.5 %mixer_forward.1 = (f32[384,512]{1,0:T(8,128)S(1)}, f32[384,1]{1,0:T(8,128)S(1)}, f32[1,4,3,128,128]{4,3,2,1,0:T(8,128)S(1)}, bf16[1,4,3,128,128]{4,3,2,1,0:T(8,128)(2,1)S(1)}) custom-call(s32[2]{0:T(128)S(1)} %pad_add_fusion.scalar_ref, f32[4,384,512]{2,1,0:T(8,128)} %convolution_bitcast_fusion.1.z_ref, s32[1,1,384]{2,1,0:T(1,128)} %bitcast.75, ...), custom_call_target="tpu_custom_call" | custom-call | tf_op jit(solution)/shard_map/mixer_forward/pallas_call | solution.py:248
  114.0 5.6 %collective-permute-done.9.refs_0_ = bf16[96,2176]{1,0:T(8,128)(2,1)} collective-permute-done((bf16[96,2176]{1,0:T(8,128)(2,1)}, bf16[96,2176]{1,0:T(8,128)(2,1)}, u32[]{:S(2)}, u32[]{:S(2)}) %collective-permute-start.9) | collective-permute-done | bytes 417824 | tf_op jit(solution)/shard_map/ppermute | solution.py:632
  119.6 26.2 %collective-permute-done.10.refs_1_ = bf16[96,2176]{1,0:T(8,128)(2,1)} collective-permute-done((bf16[96,2176]{1,0:T(8,128)(2,1)}, bf16[96,2176]{1,0:T(8,128)(2,1)}, u32[]{:S(2)}, u32[]{:S(2)}) %collective-permute-start.10) | collective-permute-done | bytes 417824 | tf_op jit(solution)/shard_map/ppermute | solution.py:632
  153.0 13.8 %collective-permute-start.14 = (bf16[96,2048]{1,0:T(8,128)(2,1)S(1)}, bf16[96,2048]{1,0:T(8,128)(2,1)S(1)}, u32[]{:S(2)}, u32[]{:S(2)}) collective-permute-start(bf16[96,2048]{1,0:T(8,128)(2,1)S(1)} %get-tuple-element.84), channel_id=1, source_target_pairs={{0,3},{1,0},{2,1},{3,2},{4,7},{5,4},{6,5},{7,6},{8,11},{9,8},{10,9... | collective-permute-start | bytes 1179656 | tf_op jit(solution)/shard_map/ppermute | solution.py:632
  166.9 11.5 %collective-permute-done.13 = bf16[96,2048]{1,0:T(8,128)(2,1)S(1)} collective-permute-done((bf16[96,2048]{1,0:T(8,128)(2,1)S(1)}, bf16[96,2048]{1,0:T(8,128)(2,1)S(1)}, u32[]{:S(2)}, u32[]{:S(2)}) %collective-permute-start.13) | collective-permute-done | bytes 393248 | tf_op jit(solution)/shard_map/ppermute | solution.py:632
  178.4 4.6 collective-permute-done.14
  183.0 7.9 %convolution_bitcast_fusion = f32[2,384,1408]{2,1,0:T(8,128)S(1)} fusion(bf16[2,2048,1408]{2,1,0:T(8,128)(2,1)} %all-gather.6.cloned.1.call-done, bf16[384,2048]{1,0:T(8,128)(2,1)S(1)} %constant_dynamic-update-slice_fusion.rows_ref.right_ref), kind=kOutput, calls=%fused_computation.6 | convolution fusion | flops 4429185024 | bytes 17432576 | tf_op jit(solution)/shard_map/td,jdf->jtf/dot_general | solution.py:838
  194.8 5.6 %convolution_convert_fusion = bf16[384,2048]{1,0:T(8,128)(2,1)S(1)} fusion(bf16[384,1408]{1,0:T(8,128)(2,1)S(1)} %multiply_convert_fusion.2.left_ref, bf16[1408,2048]{1,0:T(8,128)(2,1)} %all-gather.8.cloned.1.call-done), kind=kOutput, calls=%fused_computation.14 | convolution fusion | flops 2215378944 | bytes 8421376 | tf_op jit(solution)/shard_map/dot_general | solution.py:43
  210.9 8.3 %collective-permute-done.17 = bf16[96,2048]{1,0:T(8,128)(2,1)S(1)} collective-permute-done((bf16[96,2048]{1,0:T(8,128)(2,1)}, bf16[96,2048]{1,0:T(8,128)(2,1)S(1)}, u32[]{:S(2)}, u32[]{:S(2)}) %collective-permute-start.17) | collective-permute-done | bytes 393248 | tf_op jit(solution)/shard_map/ppermute | solution.py:632
  219.3 14.9 %collective-permute-done.16 = bf16[96,2048]{1,0:T(8,128)(2,1)S(1)} collective-permute-done((bf16[96,2048]{1,0:T(8,128)(2,1)}, bf16[96,2048]{1,0:T(8,128)(2,1)S(1)}, u32[]{:S(2)}, u32[]{:S(2)}) %collective-permute-start.16) | collective-permute-done | bytes 393248 | tf_op jit(solution)/shard_map/ppermute | solution.py:632
  238.7 9.5 %collective-permute-start.20 = (bf16[96,2048]{1,0:T(8,128)(2,1)S(1)}, bf16[96,2048]{1,0:T(8,128)(2,1)S(1)}, u32[]{:S(2)}, u32[]{:S(2)}) collective-permute-start(bf16[96,2048]{1,0:T(8,128)(2,1)S(1)} %get-tuple-element.151), channel_id=1, source_target_pairs={{0,3},{1,0},{2,1},{3,2},{4,7},{5,4},{6,5},{7,6},{8,11},{9,8},{10,9... | collective-permute-start | bytes 1179656 | tf_op jit(solution)/shard_map/ppermute | solution.py:632
  248.9 8.9 %collective-permute-done.20 = bf16[96,2048]{1,0:T(8,128)(2,1)S(1)} collective-permute-done((bf16[96,2048]{1,0:T(8,128)(2,1)S(1)}, bf16[96,2048]{1,0:T(8,128)(2,1)S(1)}, u32[]{:S(2)}, u32[]{:S(2)}) %collective-permute-start.20) | collective-permute-done | bytes 393248 | tf_op jit(solution)/shard_map/ppermute | solution.py:632
  257.8 25.0 %collective-permute-done.19 = bf16[96,2048]{1,0:T(8,128)(2,1)S(1)} collective-permute-done((bf16[96,2048]{1,0:T(8,128)(2,1)S(1)}, bf16[96,2048]{1,0:T(8,128)(2,1)S(1)}, u32[]{:S(2)}, u32[]{:S(2)}) %collective-permute-start.19) | collective-permute-done | bytes 393248 | tf_op jit(solution)/shard_map/ppermute | solution.py:632
  282.8 5.7 %multiply_convert_fusion.1 = (bf16[384,1408]{1,0:T(8,128)(2,1)S(1)}, bf16[384,1408]{1,0:T(8,128)(2,1)S(1)}) fusion(f32[2,384,1408]{2,1,0:T(8,128)S(1)} %copy-done.64, bf16[1408,2048]{1,0:T(8,128)(2,1)} %all-gather.8.cloned.1.call-done, bf16[96,2048]{1,0:T(8,128)(2,1)S(1)} %collective-permute-done.20, bf16[96,2048]{1,0:T(8,128)(2,1)S(1)} %collective-permute-done.19, ...), kind=kOutput, calls=%fused_computation.19 | convolution fusion | flops 2227912704 | bytes 13828096 | tf_op jit(solution)/shard_map/dot_general | solution.py:47
  303.5 8.9 %pair_gradient.1 = bf16[2,2048,1408]{2,1,0:T(8,128)(2,1)S(1)} custom-call(bf16[384,2048]{1,0:T(8,128)(2,1)S(1)} %copy-done.18, bf16[384,1408]{1,0:T(8,128)(2,1)S(1)} %get-tuple-element.155.first_ref, bf16[384,1408]{1,0:T(8,128)(2,1)S(1)} %get-tuple-element.90.second_ref), custom_call_target="tpu_custom_call" | custom-call | tf_op jit(solution)/shard_map/pair_gradient/pallas_call | solution.py:410
  324.1 12.7 %collective-permute-done.22.refs_1_ = bf16[96,2048]{1,0:T(8,128)(2,1)} collective-permute-done((bf16[96,2048]{1,0:T(8,128)(2,1)}, bf16[96,2048]{1,0:T(8,128)(2,1)}, u32[]{:S(2)}, u32[]{:S(2)}) %collective-permute-start.22) | collective-permute-done | bytes 393248 | tf_op jit(solution)/shard_map/ppermute | solution.py:632
  362.2 15.5 %collective-permute-done.26 = bf16[96,2176]{1,0:T(8,128)(2,1)S(1)} collective-permute-done((bf16[96,2176]{1,0:T(8,128)(2,1)S(1)}, bf16[96,2176]{1,0:T(8,128)(2,1)S(1)}, u32[]{:S(2)}, u32[]{:S(2)}) %collective-permute-start.26) | collective-permute-done | bytes 417824 | tf_op jit(solution)/shard_map/ppermute | solution.py:632
  378.2 4.7 multiply_convert_fusion.4
  384.5 21.2 %mixer_backward.1.grads_ref = bf16[4,384,512]{2,1,0:T(8,128)(2,1)S(1)} custom-call(s32[2]{0:T(128)S(1)} %pad_add_fusion.scalar_ref, f32[4,384,512]{2,1,0:T(8,128)} %convolution_bitcast_fusion.1.z_ref, f32[384,512]{1,0:T(8,128)} %get-tuple-element.158.dout_ref, bf16[384,512]{1,0:T(8,128)(2,1)} %get-tuple-element.157.gate_ref, s32[1,1,384]{2,1,0:T(1,128)} %bitcast.76, ...), custom_call_target="tpu_custom_call" | custom-call | tf_op jit(solution)/shard_map/mixer_backward/pallas_call | solution.py:248
  408.9 4.7 project_back.1
  428.5 9.5 %collective-permute-start.30 = (bf16[96,2048]{1,0:T(8,128)(2,1)}, bf16[96,2048]{1,0:T(8,128)(2,1)}, u32[]{:S(2)}, u32[]{:S(2)}) collective-permute-start(bf16[96,2048]{1,0:T(8,128)(2,1)} %get-tuple-element.107), channel_id=1, source_target_pairs={{0,3},{1,0},{2,1},{3,2},{4,7},{5,4},{6,5},{7,6},{8,11},{9,8},{10,9... | collective-permute-start | bytes 1179656 | tf_op jit(solution)/shard_map/ppermute | solution.py:632
  438.3 4.8 collective-permute-done.41.refs_2_
  444.0 8.6 %collective-permute-start.32 = (bf16[96,2048]{1,0:T(8,128)(2,1)}, bf16[96,2048]{1,0:T(8,128)(2,1)}, u32[]{:S(2)}, u32[]{:S(2)}) collective-permute-start(bf16[96,2048]{1,0:T(8,128)(2,1)} %get-tuple-element.109), channel_id=1, source_target_pairs={{0,1},{1,2},{2,3},{3,0},{4,5},{5,6},{6,7},{7,4},{8,9},{9,10},{10,1... | collective-permute-start | bytes 1179656 | tf_op jit(solution)/shard_map/ppermute | solution.py:632
  466.1 7.2 %collective-permute-done.31 = bf16[96,2048]{1,0:T(8,128)(2,1)} collective-permute-done((bf16[96,2048]{1,0:T(8,128)(2,1)}, bf16[96,2048]{1,0:T(8,128)(2,1)}, u32[]{:S(2)}, u32[]{:S(2)}) %collective-permute-start.31) | collective-permute-done | bytes 393248 | tf_op jit(solution)/shard_map/ppermute | solution.py:632
  479.9 9.0 %add_multiply_fusion = (f32[2,256,1408]{2,1,0:T(8,128)}, f32[2,256,1408]{2,1,0:T(8,128)}, f32[2,256,1408]{2,1,0:T(8,128)}, f32[2,256,1408]{2,1,0:T(8,128)}) fusion(f32[2,256,1408]{2,1,0:T(8,128)} %param.38, f32[2,256,1408]{2,1,0:T(8,128)} %param.36, f32[2,256,1408]{2,1,0:T(8,128)} %param.37, bf16[2,256,1408]{2,1,0:T(8,128)(2,1)} %reduce-scatter.2.cloned.1.call-done), kind=kLoop, calls=%fused_computation.11 | loop fusion | flops 6488064 | bytes 21626880 | tf_op jit(solution)/shard_map/add | solution.py:668
  495.2 6.4 %mixer_in_update.1 = (f32[4,256,512]{2,1,0:T(8,128)}, f32[4,256,512]{2,1,0:T(8,128)}, f32[4,256,512]{2,1,0:T(8,128)}, f32[4,256,512]{2,1,0:T(8,128)}, f32[8,256]{1,0:T(8,128)S(1)}, /*index=5*/f32[8,256]{1,0:T(8,128)S(1)}) custom-call(bf16[384,2048]{1,0:T(8,128)(2,1)S(1)} %take_blocks.4.rows_ref, bf16[4,384,512]{2,1,0:T(8,128)(2,1)S(1)} %mixer_backward.1.grads_ref, ...), custom_call_target="tpu_custom_call" | custom-call | tf_op jit(solution)/shard_map/mixer_in_update/pallas_call | solution.py:376
  (381 shorter events, 182.0 us)
Async XLA Ops:
  7.2 65.8 %all-gather.4.cloned.1.call-start = ((), (), s32[]{:S(2)}) async-start(), calls=%async_computation.1 | async-start | bytes 9437184 | tf_op jit(solution)/shard_map/all_gather | solution.py:673
  10.0 173.0 %all-gather.6.cloned.1.call-start = ((), (), s32[]{:S(2)}) async-start(), calls=%async_computation.2 | async-start | bytes 12976128 | tf_op jit(solution)/shard_map/all_gather | solution.py:673
  13.2 181.6 %all-gather.8.cloned.1.call-start = ((), (), s32[]{:S(2)}) async-start(), calls=%async_computation.3 | async-start | bytes 6488064 | tf_op jit(solution)/shard_map/all_gather | solution.py:673
  13.8 29.8 %collective-permute-start.2 = (bf16[96,2048]{1,0:T(8,128)(2,1)S(1)}, bf16[96,2048]{1,0:T(8,128)(2,1)S(1)}, u32[]{:S(2)}, u32[]{:S(2)}) collective-permute-start(bf16[96,2048]{1,0:T(8,128)(2,1)S(1)} %copy-done.10), channel_id=1, source_target_pairs={{0,3},{1,0},{2,1},{3,2},{4,7},{5,4},{6,5},{7,6},{8,11},{9,8},{10,9... | collective-permute-start | bytes 1179656 | tf_op jit(solution)/shard_map/ppermute | solution.py:632
  18.5 34.3 %collective-permute-start.1 = (bf16[96,2048]{1,0:T(8,128)(2,1)S(1)}, bf16[96,2048]{1,0:T(8,128)(2,1)}, u32[]{:S(2)}, u32[]{:S(2)}) collective-permute-start(bf16[96,2048]{1,0:T(8,128)(2,1)S(1)} %copy-done.10), channel_id=1, source_target_pairs={{0,2},{1,3},{2,0},{3,1},{4,6},{5,7},{6,4},{7,5},{8,10},{9,11},{10,... | collective-permute-start | bytes 1179656 | tf_op jit(solution)/shard_map/ppermute | solution.py:632
  18.5 34.3 %collective-permute-start = (bf16[96,2048]{1,0:T(8,128)(2,1)S(1)}, bf16[96,2048]{1,0:T(8,128)(2,1)}, u32[]{:S(2)}, u32[]{:S(2)}) collective-permute-start(bf16[96,2048]{1,0:T(8,128)(2,1)S(1)} %copy-done.10), channel_id=1, source_target_pairs={{0,1},{1,2},{2,3},{3,0},{4,5},{5,6},{6,7},{7,4},{8,9},{9,10},{10,1... | collective-permute-start | bytes 1179656 | tf_op jit(solution)/shard_map/ppermute | solution.py:632
  22.1 457.8 %reduce-scatter.2.cloned.1.call-start = ((), (), s32[]{:S(2)}) async-start(), calls=%async_computation.4 | async-start | bytes 12976128 | tf_op jit(solution)/shard_map/reduce_scatter | solution.py:927
  110.0 35.7 %collective-permute-start.10 = (bf16[96,2176]{1,0:T(8,128)(2,1)}, bf16[96,2176]{1,0:T(8,128)(2,1)}, u32[]{:S(2)}, u32[]{:S(2)}) collective-permute-start(bf16[96,2176]{1,0:T(8,128)(2,1)} %pad_maximum_fusion.5), channel_id=1, source_target_pairs={{0,2},{1,3},{2,0},{3,1},{4,6},{5,7},{6,4},{7,5},{8,10},{9,11},{10,... | collective-permute-start | bytes 1253384 | tf_op jit(solution)/shard_map/ppermute | solution.py:632
  110.9 34.8 %collective-permute-start.11 = (bf16[96,2176]{1,0:T(8,128)(2,1)}, bf16[96,2176]{1,0:T(8,128)(2,1)}, u32[]{:S(2)}, u32[]{:S(2)}) collective-permute-start(bf16[96,2176]{1,0:T(8,128)(2,1)} %pad_maximum_fusion.6), channel_id=1, source_target_pairs={{0,1},{1,2},{2,3},{3,0},{4,5},{5,6},{6,7},{7,4},{8,9},{9,10},{10,1... | collective-permute-start | bytes 1253384 | tf_op jit(solution)/shard_map/ppermute | solution.py:632
  149.1 17.8 %collective-permute-start.12 = (bf16[96,2048]{1,0:T(8,128)(2,1)S(1)}, bf16[96,2048]{1,0:T(8,128)(2,1)S(1)}, u32[]{:S(2)}, u32[]{:S(2)}) collective-permute-start(bf16[96,2048]{1,0:T(8,128)(2,1)S(1)} %get-tuple-element.84), channel_id=1, source_target_pairs={{0,1},{1,2},{2,3},{3,0},{4,5},{5,6},{6,7},{7,4},{8,9},{9,10},{10,1... | collective-permute-start | bytes 1179656 | tf_op jit(solution)/shard_map/ppermute | solution.py:632
  151.0 27.3 %collective-permute-start.13 = (bf16[96,2048]{1,0:T(8,128)(2,1)S(1)}, bf16[96,2048]{1,0:T(8,128)(2,1)S(1)}, u32[]{:S(2)}, u32[]{:S(2)}) collective-permute-start(bf16[96,2048]{1,0:T(8,128)(2,1)S(1)} %get-tuple-element.84), channel_id=1, source_target_pairs={{0,2},{1,3},{2,0},{3,1},{4,6},{5,7},{6,4},{7,5},{8,10},{9,11},{10,... | collective-permute-start | bytes 1179656 | tf_op jit(solution)/shard_map/ppermute | solution.py:632
  153.0 30.0 %collective-permute-start.14 = (bf16[96,2048]{1,0:T(8,128)(2,1)S(1)}, bf16[96,2048]{1,0:T(8,128)(2,1)S(1)}, u32[]{:S(2)}, u32[]{:S(2)}) collective-permute-start(bf16[96,2048]{1,0:T(8,128)(2,1)S(1)} %get-tuple-element.84), channel_id=1, source_target_pairs={{0,3},{1,0},{2,1},{3,2},{4,7},{5,4},{6,5},{7,6},{8,11},{9,8},{10,9... | collective-permute-start | bytes 1179656 | tf_op jit(solution)/shard_map/ppermute | solution.py:632
  206.1 28.1 %collective-permute-start.16 = (bf16[96,2048]{1,0:T(8,128)(2,1)}, bf16[96,2048]{1,0:T(8,128)(2,1)S(1)}, u32[]{:S(2)}, u32[]{:S(2)}) collective-permute-start(bf16[96,2048]{1,0:T(8,128)(2,1)} %get-tuple-element.168), channel_id=1, source_target_pairs={{0,2},{1,3},{2,0},{3,1},{4,6},{5,7},{6,4},{7,5},{8,10},{9,11},{10,... | collective-permute-start | bytes 1179656 | tf_op jit(solution)/shard_map/ppermute | solution.py:632
  209.5 24.7 %collective-permute-start.15 = (bf16[96,2048]{1,0:T(8,128)(2,1)S(1)}, bf16[96,2048]{1,0:T(8,128)(2,1)}, u32[]{:S(2)}, u32[]{:S(2)}) collective-permute-start(bf16[96,2048]{1,0:T(8,128)(2,1)S(1)} %get-tuple-element.166), channel_id=1, source_target_pairs={{0,3},{1,0},{2,1},{3,2},{4,7},{5,4},{6,5},{7,6},{8,11},{9,8},{10,9... | collective-permute-start | bytes 1179656 | tf_op jit(solution)/shard_map/ppermute | solution.py:632
  238.7 19.1 %collective-permute-start.20 = (bf16[96,2048]{1,0:T(8,128)(2,1)S(1)}, bf16[96,2048]{1,0:T(8,128)(2,1)S(1)}, u32[]{:S(2)}, u32[]{:S(2)}) collective-permute-start(bf16[96,2048]{1,0:T(8,128)(2,1)S(1)} %get-tuple-element.151), channel_id=1, source_target_pairs={{0,3},{1,0},{2,1},{3,2},{4,7},{5,4},{6,5},{7,6},{8,11},{9,8},{10,9... | collective-permute-start | bytes 1179656 | tf_op jit(solution)/shard_map/ppermute | solution.py:632
  248.2 34.6 %collective-permute-start.19 = (bf16[96,2048]{1,0:T(8,128)(2,1)S(1)}, bf16[96,2048]{1,0:T(8,128)(2,1)S(1)}, u32[]{:S(2)}, u32[]{:S(2)}) collective-permute-start(bf16[96,2048]{1,0:T(8,128)(2,1)S(1)} %get-tuple-element.151), channel_id=1, source_target_pairs={{0,2},{1,3},{2,0},{3,1},{4,6},{5,7},{6,4},{7,5},{8,10},{9,11},{10,... | collective-permute-start | bytes 1179656 | tf_op jit(solution)/shard_map/ppermute | solution.py:632
  248.5 34.3 %collective-permute-start.18 = (bf16[96,2048]{1,0:T(8,128)(2,1)S(1)}, bf16[96,2048]{1,0:T(8,128)(2,1)S(1)}, u32[]{:S(2)}, u32[]{:S(2)}) collective-permute-start(bf16[96,2048]{1,0:T(8,128)(2,1)S(1)} %get-tuple-element.151), channel_id=1, source_target_pairs={{0,1},{1,2},{2,3},{3,0},{4,5},{5,6},{6,7},{7,4},{8,9},{9,10},{10,1... | collective-permute-start | bytes 1179656 | tf_op jit(solution)/shard_map/ppermute | solution.py:632
  299.8 20.8 %collective-permute-start.24 = (bf16[1408,1024]{1,0:T(8,128)(2,1)}, bf16[1408,1024]{1,0:T(8,128)(2,1)}, u32[]{:S(2)}, u32[]{:S(2)}) collective-permute-start(bf16[1408,1024]{1,0:T(8,128)(2,1)} %wide_gradient.4), channel_id=1, source_target_pairs={{0,4},{4,0},{8,12},{12,8},{16,20},{20,16},{24,28},{28,24},{1,5},{5... | collective-permute-start | bytes 8650760 | tf_op jit(solution)/shard_map/ppermute | solution.py:637
  299.8 24.4 %collective-permute-start.21 = (bf16[96,2048]{1,0:T(8,128)(2,1)}, bf16[96,2048]{1,0:T(8,128)(2,1)S(1)}, u32[]{:S(2)}, u32[]{:S(2)}) collective-permute-start(bf16[96,2048]{1,0:T(8,128)(2,1)} %get-tuple-element.86), channel_id=1, source_target_pairs={{0,3},{1,0},{2,1},{3,2},{4,7},{5,4},{6,5},{7,6},{8,11},{9,8},{10,9... | collective-permute-start | bytes 1179656 | tf_op jit(solution)/shard_map/ppermute | solution.py:632
  299.8 37.1 %collective-permute-start.22 = (bf16[96,2048]{1,0:T(8,128)(2,1)}, bf16[96,2048]{1,0:T(8,128)(2,1)}, u32[]{:S(2)}, u32[]{:S(2)}) collective-permute-start(bf16[96,2048]{1,0:T(8,128)(2,1)} %get-tuple-element.87), channel_id=1, source_target_pairs={{0,2},{1,3},{2,0},{3,1},{4,6},{5,7},{6,4},{7,5},{8,10},{9,11},{10,... | collective-permute-start | bytes 1179656 | tf_op jit(solution)/shard_map/ppermute | solution.py:632
  301.4 35.4 %collective-permute-start.23 = (bf16[96,2048]{1,0:T(8,128)(2,1)}, bf16[96,2048]{1,0:T(8,128)(2,1)}, u32[]{:S(2)}, u32[]{:S(2)}) collective-permute-start(bf16[96,2048]{1,0:T(8,128)(2,1)} %get-tuple-element.88), channel_id=1, source_target_pairs={{0,1},{1,2},{2,3},{3,0},{4,5},{5,6},{6,7},{7,4},{8,9},{9,10},{10,1... | collective-permute-start | bytes 1179656 | tf_op jit(solution)/shard_map/ppermute | solution.py:632
  336.8 19.3 %collective-permute-start.28 = (bf16[1408,512]{1,0:T(8,128)(2,1)}, bf16[1408,512]{1,0:T(8,128)(2,1)S(1)}, u32[]{:S(2)}, u32[]{:S(2)}) collective-permute-start(bf16[1408,512]{1,0:T(8,128)(2,1)} %copy-done.39), channel_id=1, source_target_pairs={{0,8},{4,20},{8,0},{12,28},{16,24},{20,4},{24,16},{28,12},{1,9},{5... | collective-permute-start | bytes 4325384 | tf_op jit(solution)/shard_map/ppermute | solution.py:702
  347.7 30.0 %collective-permute-start.26 = (bf16[96,2176]{1,0:T(8,128)(2,1)S(1)}, bf16[96,2176]{1,0:T(8,128)(2,1)S(1)}, u32[]{:S(2)}, u32[]{:S(2)}) collective-permute-start(bf16[96,2176]{1,0:T(8,128)(2,1)S(1)} %get-tuple-element.97), channel_id=1, source_target_pairs={{0,2},{1,3},{2,0},{3,1},{4,6},{5,7},{6,4},{7,5},{8,10},{9,11},{10,... | collective-permute-start | bytes 1253384 | tf_op jit(solution)/shard_map/ppermute | solution.py:632
  348.4 29.4 %collective-permute-start.27 = (bf16[96,2176]{1,0:T(8,128)(2,1)S(1)}, bf16[96,2176]{1,0:T(8,128)(2,1)S(1)}, u32[]{:S(2)}, u32[]{:S(2)}) collective-permute-start(bf16[96,2176]{1,0:T(8,128)(2,1)S(1)} %get-tuple-element.97), channel_id=1, source_target_pairs={{0,3},{1,0},{2,1},{3,2},{4,7},{5,4},{6,5},{7,6},{8,11},{9,8},{10,9... | collective-permute-start | bytes 1253384 | tf_op jit(solution)/shard_map/ppermute | solution.py:632
  419.2 41.8 %collective-permute-start.33 = (bf16[512,2176]{1,0:T(8,128)(2,1)}, bf16[512,2176]{1,0:T(8,128)(2,1)}, u32[]{:S(2)}, u32[]{:S(2)}) collective-permute-start(bf16[512,2176]{1,0:T(8,128)(2,1)} %mixer_gradient.4), channel_id=1, source_target_pairs={{0,8},{4,20},{8,0},{12,28},{16,24},{20,4},{24,16},{28,12},{1,9},{5... | collective-permute-start | bytes 6684680 | tf_op jit(solution)/shard_map/ppermute | solution.py:702
  424.1 19.1 %collective-permute-start.41 = (bf16[1408,256]{1,0:T(8,128)(2,1)S(1)}, bf16[1408,256]{1,0:T(8,128)(2,1)S(1)}, u32[]{:S(2)}, u32[]{:S(2)}) collective-permute-start(bf16[1408,256]{1,0:T(8,128)(2,1)S(1)} %copy-done.48), channel_id=1, source_target_pairs={{0,16},{4,12},{8,24},{12,4},{16,0},{20,28},{24,8},{28,20},{1,17},{... | collective-permute-start | bytes 2162696 | tf_op jit(solution)/shard_map/ppermute | solution.py:702
  427.2 46.1 %collective-permute-start.39 = (bf16[512,512]{1,0:T(8,128)(2,1)}, bf16[512,512]{1,0:T(8,128)(2,1)}, u32[]{:S(2)}, u32[]{:S(2)}) collective-permute-start(bf16[512,512]{1,0:T(8,128)(2,1)} %fusion.8), channel_id=1, source_target_pairs={{0,8},{4,20},{8,0},{12,28},{16,24},{20,4},{24,16},{28,12},{1,9},{5... | collective-permute-start | bytes 1572872 | tf_op jit(solution)/shard_map/ppermute | solution.py:702
  428.5 37.6 %collective-permute-start.30 = (bf16[96,2048]{1,0:T(8,128)(2,1)}, bf16[96,2048]{1,0:T(8,128)(2,1)}, u32[]{:S(2)}, u32[]{:S(2)}) collective-permute-start(bf16[96,2048]{1,0:T(8,128)(2,1)} %get-tuple-element.107), channel_id=1, source_target_pairs={{0,3},{1,0},{2,1},{3,2},{4,7},{5,4},{6,5},{7,6},{8,11},{9,8},{10,9... | collective-permute-start | bytes 1179656 | tf_op jit(solution)/shard_map/ppermute | solution.py:632
  438.0 35.3 %collective-permute-start.31 = (bf16[96,2048]{1,0:T(8,128)(2,1)}, bf16[96,2048]{1,0:T(8,128)(2,1)}, u32[]{:S(2)}, u32[]{:S(2)}) collective-permute-start(bf16[96,2048]{1,0:T(8,128)(2,1)} %get-tuple-element.108), channel_id=1, source_target_pairs={{0,2},{1,3},{2,0},{3,1},{4,6},{5,7},{6,4},{7,5},{8,10},{9,11},{10,... | collective-permute-start | bytes 1179656 | tf_op jit(solution)/shard_map/ppermute | solution.py:632
  444.0 29.3 %collective-permute-start.32 = (bf16[96,2048]{1,0:T(8,128)(2,1)}, bf16[96,2048]{1,0:T(8,128)(2,1)}, u32[]{:S(2)}, u32[]{:S(2)}) collective-permute-start(bf16[96,2048]{1,0:T(8,128)(2,1)} %get-tuple-element.109), channel_id=1, source_target_pairs={{0,1},{1,2},{2,3},{3,0},{4,5},{5,6},{6,7},{7,4},{8,9},{9,10},{10,1... | collective-permute-start | bytes 1179656 | tf_op jit(solution)/shard_map/ppermute | solution.py:632
  464.3 24.6 %collective-permute-start.34 = (bf16[256,2176]{1,0:T(8,128)(2,1)}, bf16[256,2176]{1,0:T(8,128)(2,1)}, u32[]{:S(2)}, u32[]{:S(2)}) collective-permute-start(bf16[256,2176]{1,0:T(8,128)(2,1)} %mixer_gradient.5), channel_id=1, source_target_pairs={{0,16},{4,12},{8,24},{12,4},{16,0},{20,28},{24,8},{28,20},{1,17},{... | collective-permute-start | bytes 3342344 | tf_op jit(solution)/shard_map/ppermute | solution.py:702
  475.5 32.9 %collective-permute-start.40 = (bf16[256,512]{1,0:T(8,128)(2,1)}, bf16[256,512]{1,0:T(8,128)(2,1)}, u32[]{:S(2)}, u32[]{:S(2)}) collective-permute-start(bf16[256,512]{1,0:T(8,128)(2,1)} %fusion.10), channel_id=1, source_target_pairs={{0,16},{4,12},{8,24},{12,4},{16,0},{20,28},{24,8},{28,20},{1,17},{... | collective-permute-start | bytes 786440 | tf_op jit(solution)/shard_map/ppermute | solution.py:702
  (115 other events, 1247.1 us)
Sparse Core Ops, SparseCore 0:
  10.5 62.4 all-gather.3
  75.5 67.6 all-gather.5
  145.7 44.3 all-gather.7
  337.0 84.7 reduce-scatter.1

commit v3 on v2

--- a/solution.py
+++ b/solution.py
@@ -14,6 +14,7 @@
 BLOCK = 32
 CHUNK = 128
 LEVELS = 7
+TOGETHER = 1
 VMEM_LIMIT = 16 * 1024 * 1024
 
 EPS = 1e-06
@@ -70,9 +71,11 @@
     return logf, key
 
 
-def split_sum(mat, logf_pair):
-    both = dot(mat, logf_pair)
-    return both[:, :HEAD_DIM] + both[:, HEAD_DIM:]
+def all_decays(sums_ref, pair):
+    count = sums_ref.shape[0]
+    both = dot(sums_ref[...].reshape(count * CHUNK, CHUNK), pair)
+    decays = jnp.exp(both[:, :HEAD_DIM] + both[:, HEAD_DIM:])
+    return [decays[i * CHUNK : (i + 1) * CHUNK] for i in range(count)]
 
 
 def chunk_masks():
@@ -93,36 +96,41 @@
             place = lax.rem(self.rank - at // self.size + self.ranks, self.ranks)
             yield pl.ds(pl.multiple_of(place * self.size + at % self.size, self.step), self.step)
 
-    def load(self, ref, first, *index):
-        return jnp.concatenate([ref[(*index, piece)] for piece in self.pieces(first)], axis=0)
-
-    def store(self, ref, first, value, *index):
+    def load(self, ref, first, lanes, *index):
+        return jnp.concatenate([ref[(*index, piece, lanes)] for piece in self.pieces(first)], axis=0)
+
+    def store(self, ref, first, value, lanes, *index):
         for i, piece in enumerate(self.pieces(first)):
-            ref[(*index, piece)] = value[i * self.step : (i + 1) * self.step]
+            ref[(*index, piece, lanes)] = value[i * self.step : (i + 1) * self.step]
 
 
 def mixer_forward_kernel(ranks, scalar_ref, z_ref, seg_row_ref, seg_col_ref, sums_ref, o_ref, square_ref, state_ref, pair_ref):
-    head = pl.program_id(0)
+    step = pl.program_id(0)
     seqs, _, seq_len = seg_row_ref.shape
     chunks = seq_len // CHUNK
     ring = RingRows(scalar_ref[seqs], ranks, z_ref.shape[1])
     row, col, differ = chunk_masks()
-    for seq, c in ((s, c) for s in range(seqs) for c in range(chunks)):
+    together = z_ref.shape[2] // HEAD_DIM
+    carry = [None] * together
+    for seq, c, h in ((s, c, h) for s in range(seqs) for c in range(chunks) for h in range(together)):
         first = seq * seq_len + c * CHUNK
+        lanes = pl.ds(h * HEAD_DIM, HEAD_DIM)
+        state = carry[h]
         if c == 0:
             state = jnp.zeros((HEAD_DIM, HEAD_DIM), F32)
-        z0, z1, value = (ring.load(z_ref, first, j) for j in range(3))
+        z0, z1, value = (ring.load(z_ref, first, lanes, j) for j in range(3))
         query = z0 * sigmoid(z0)
         logf, key = forget_parts(z1)
         high = logf.astype(BF)
         pair = jnp.concatenate([high, (logf - high.astype(F32)).astype(BF)], axis=1)
+        decays = all_decays(sums_ref, pair)
         seg_col = seg_col_ref[seq, c * CHUNK : (c + 1) * CHUNK, :]
         seg_row = seg_row_ref[seq, :, c * CHUNK : (c + 1) * CHUNK]
         seg_last = seg_row[:, CHUNK - 1 :]
         value_low = value.astype(BF)
         scores = None
         for level in reversed(range(LEVELS)):
-            decay = jnp.exp(split_sum(sums_ref[level], pair))
+            decay = decays[level]
             right = ((row >> level) & 1) == 1
             mixed = (decay * jnp.where(right, query, key)).astype(BF)
             product = dot_nt(mixed, mixed)
@@ -130,29 +138,33 @@
         diagonal = jnp.sum(query * key, axis=1, keepdims=True)
         scores = jnp.where(differ == 0, diagonal, scores)
         scores = jnp.where(seg_col == seg_row, scores, 0.0).astype(BF)
-        pair_ref[seq, 0, c] = scores
+        pair_ref[seq, h, c] = scores
         out = dot(jnp.where(row >= col, scores, jnp.zeros_like(scores)), value_low)
-        from_start = jnp.exp(split_sum(sums_ref[LEVELS], pair))
+        from_start = decays[LEVELS]
         if c > 0:
             carried = seg_col == seg_before
             reach = jnp.where(carried, query * from_start, 0.0).astype(BF)
             out = out + dot_nt(reach, state.astype(BF))
-        state_ref[seq, 0, c] = state
+        state_ref[seq, h, c] = state
         position = c * CHUNK + lax.broadcasted_iota(jnp.int32, (CHUNK, 1), 0)
         out = jnp.where(position < scalar_ref[seq] * BLOCK, out, 0.0)
-        ring.store(o_ref, first, out)
+        ring.store(o_ref, first, out, lanes)
         square = jnp.sum(out * out, axis=1, keepdims=True)
-        square = jnp.where(head == 0, square, ring.load(square_ref, first) + square)
-        ring.store(square_ref, first, square)
+        if h == 0:
+            square = jnp.where(step == 0, square, ring.load(square_ref, first, slice(None)) + square)
+        else:
+            square = ring.load(square_ref, first, slice(None)) + square
+        ring.store(square_ref, first, square, slice(None))
         if c < chunks - 1:
-            to_end = jnp.exp(split_sum(sums_ref[LEVELS + 1], pair))
+            to_end = decays[LEVELS + 1]
             tail = jnp.where(seg_col == seg_last, key * to_end, 0.0).astype(BF)
             fresh = dot_tn(value_low, tail)
             if c > 0:
                 kept = jnp.where(seg_last == seg_before, from_start[CHUNK - 1 :], 0.0)
                 fresh = fresh + state * kept
-            state = fresh
-            seg_before = seg_last
+            carry[h] = fresh
+            if h == together - 1:
+                seg_before = seg_last
 
 
 def mixer_backward_kernel(
@@ -163,91 +175,106 @@
     ring = RingRows(scalar_ref[seqs], ranks, z_ref.shape[1])
     row, col, differ = chunk_masks()
     dz_ref[3] = gate_ref[...]
-    for seq, c in ((s, c) for s in range(seqs) for c in reversed(range(chunks))):
+    together = z_ref.shape[2] // HEAD_DIM
+    carry = [None] * together
+    for seq, c, h in ((s, c, h) for s in range(seqs) for c in reversed(range(chunks)) for h in range(together)):
         first = seq * seq_len + c * CHUNK
-        z0, z1, value = (ring.load(z_ref, first, j) for j in range(3))
+        lanes = pl.ds(h * HEAD_DIM, HEAD_DIM)
+        dstate = carry[h]
+        z0, z1, value = (ring.load(z_ref, first, lanes, j) for j in range(3))
         gate0 = sigmoid(z0)
         query = z0 * gate0
         logf, key = forget_parts(z1)
         high = logf.astype(BF)
         pair = jnp.concatenate([high, (logf - high.astype(F32)).astype(BF)], axis=1)
+        decays = all_decays(sums_ref, pair)
         seg_col = seg_col_ref[seq, c * CHUNK : (c + 1) * CHUNK, :]
         seg_row = seg_row_ref[seq, :, c * CHUNK : (c + 1) * CHUNK]
         seg_last = seg_row[:, CHUNK - 1 :]
         value_low = value.astype(BF)
         position = c * CHUNK + lax.broadcasted_iota(jnp.int32, (CHUNK, 1), 0)
-        dout = jnp.where(position < scalar_ref[seq] * BLOCK, ring.load(dout_ref, first), 0.0)
+        dout = jnp.where(position < scalar_ref[seq] * BLOCK, ring.load(dout_ref, first, lanes), 0.0)
         dout_low = dout.astype(BF)
 
         dscore = jnp.where(row > col, dot_nt(dout_low, value_low), dot_nt(value_low, dout_low))
         dscore = jnp.where(seg_col == seg_row, dscore, 0.0).astype(BF)
-        scores = pair_ref[seq, 0, c]
+        scores = pair_ref[seq, h, c]
         zero = jnp.zeros_like(scores)
         dvalue = dot(jnp.where(col >= row, scores, zero), dout_low)
         diagonal = jnp.sum(dout * value, axis=1, keepdims=True)
         dquery = diagonal * key
         dkey = diagonal * query
-        dlogf = jnp.zeros((CHUNK, HEAD_DIM), F32)
+        dsums = []
         for level in range(LEVELS):
-            decay = jnp.exp(split_sum(sums_ref[level], pair))
+            decay = decays[level]
             right = ((row >> level) & 1) == 1
             mixed = decay * jnp.where(right, query, key)
             dmixed = dot(jnp.where((differ >> level) == 1, dscore, zero), mixed.astype(BF))
             through = dmixed * decay
             dquery = dquery + jnp.where(right, through, 0.0)
             dkey = dkey + jnp.where(right, 0.0, through)
-            dlogf = dlogf + dot(sums_t_ref[level], (dmixed * mixed).astype(BF))
-        from_start = jnp.exp(split_sum(sums_ref[LEVELS], pair))
+            dsums.append((dmixed * mixed).astype(BF))
+        from_start = decays[LEVELS]
         total = from_start[CHUNK - 1 :]
         if c > 0:
             seg_before = seg_row_ref[seq, :, c * CHUNK - 1 : c * CHUNK]
             carried = seg_col == seg_before
-            state = state_ref[seq, 0, c]
+            state = state_ref[seq, h, c]
             reach = jnp.where(carried, query * from_start, 0.0)
             dreach = jnp.where(carried, dot(dout_low, state.astype(BF)), 0.0)
             dquery = dquery + dreach * from_start
-            dlogf = dlogf + dot(sums_t_ref[LEVELS], (dreach * reach).astype(BF))
+            dsums.append((dreach * reach).astype(BF))
             dstate_new = dot_tn(dout_low, reach.astype(BF))
         if c < chunks - 1:
-            to_end = jnp.exp(split_sum(sums_ref[LEVELS + 1], pair))
+            to_end = decays[LEVELS + 1]
             in_tail = seg_col == seg_last
             tail = jnp.where(in_tail, key * to_end, 0.0)
             dstate_low = dstate.astype(BF)
             dtail = jnp.where(in_tail, dot(value_low, dstate_low), 0.0)
             dkey = dkey + dtail * to_end
-            dlogf = dlogf + dot(sums_t_ref[LEVELS + 1], (dtail * tail).astype(BF))
+            dsums.append((dtail * tail).astype(BF))
             dvalue = dvalue + dot_nt(tail.astype(BF), dstate_low)
             if c > 0:
                 kept = jnp.where(seg_last == seg_before, total, 0.0)
-                dlogf = dlogf + jnp.sum(state * dstate, axis=0, keepdims=True) * kept
+                dkept = jnp.sum(state * dstate, axis=0, keepdims=True) * kept
                 dstate_new = dstate_new + dstate * kept
         if c > 0:
-            dstate = dstate_new
-        ring.store(dz_ref, first, (dquery * gate0 * (1.0 + z0 * (1.0 - gate0))).astype(BF), 0)
-        ring.store(dz_ref, first, ((dlogf - dkey * (1.0 - key)) * key).astype(BF), 1)
-        ring.store(dz_ref, first, dvalue.astype(BF), 2)
+            carry[h] = dstate_new
+        used = LEVELS + int(c > 0)
+        sums_t = sums_t_ref[:, : used * CHUNK]
+        if c < chunks - 1:
+            sums_t = jnp.concatenate([sums_t, sums_t_ref[:, (LEVELS + 1) * CHUNK :]], axis=1)
+        dlogf = dot(sums_t, jnp.concatenate(dsums, axis=0))
+        if 0 < c < chunks - 1:
+            dlogf = dlogf + dkept
+        ring.store(dz_ref, first, (dquery * gate0 * (1.0 + z0 * (1.0 - gate0))).astype(BF), lanes, 0)
+        ring.store(dz_ref, first, ((dlogf - dkey * (1.0 - key)) * key).astype(BF), lanes, 1)
+        ring.store(dz_ref, first, dvalue.astype(BF), lanes, 2)
 
 
 def mixer_call(kernel, name, operands, kinds, outputs, segments, z, ranks):
     seqs, seq_len = segments.shape
     rows, width = z.shape[1:]
     heads = width // HEAD_DIM
+    together = math.gcd(heads, TOGETHER)
+    lanes = together * HEAD_DIM
     chunks = seq_len // CHUNK
     matrices = (seqs, heads, chunks, HEAD_DIM, HEAD_DIM)
     shapes = {
-        "z": (None, pl.BlockSpec((3, rows, HEAD_DIM), lambda h: (0, 0, h))),
-        "dz": ((4, rows, width), pl.BlockSpec((4, rows, HEAD_DIM), lambda h: (0, 0, h))),
-        "token": ((rows, width), pl.BlockSpec((rows, HEAD_DIM), lambda h: (0, h))),
+        "z": (None, pl.BlockSpec((3, rows, lanes), lambda h: (0, 0, h))),
+        "dz": ((4, rows, width), pl.BlockSpec((4, rows, lanes), lambda h: (0, 0, h))),
+        "token": ((rows, width), pl.BlockSpec((rows, lanes), lambda h: (0, h))),
         "column": ((rows, 1), pl.BlockSpec((rows, 1), lambda h: (0, 0))),
-        "matrix": (matrices, pl.BlockSpec((seqs, 1) + matrices[2:], lambda h: (0, h, 0, 0, 0))),
+        "matrix": (matrices, pl.BlockSpec((seqs, together) + matrices[2:], lambda h: (0, h, 0, 0, 0))),
         "segment_row": (None, pl.BlockSpec((seqs, 1, seq_len), lambda h: (0, 0, 0))),
         "segment_column": (None, pl.BlockSpec((seqs, seq_len, 1), lambda h: (0, 0, 0))),
         "sums": (None, pl.BlockSpec((LEVELS + 2, CHUNK, CHUNK), lambda h: (0, 0, 0))),
+        "sums_t": (None, pl.BlockSpec((CHUNK, (LEVELS + 2) * CHUNK), lambda h: (0, 0))),
         "scalar": (None, pl.BlockSpec(memory_space=pltpu.SMEM)),
     }
     return pl.pallas_call(
         functools.partial(kernel, ranks),
-        grid=(heads,),
+        grid=(heads // together,),
         in_specs=[shapes[kind][1] for kind in kinds],
         out_specs=[shapes[kind][1] for kind, _ in outputs],
         out_shape=[jax.ShapeDtypeStruct(shapes[kind][0], dtype) for kind, dtype in outputs],
@@ -272,17 +299,21 @@
 
 def mixer_backward(z, dout, gate_dz, segments, scalars, states, pairs, ranks):
     sums = decay_sums()
-    sums_t = jnp.asarray(sums.transpose(0, 2, 1), BF)
+    sums_t = jnp.asarray(sums.reshape(-1, CHUNK).T, BF)
     return mixer_call(
         mixer_backward_kernel,
         "mixer_backward",
         (scalars, z, dout, gate_dz, segments[:, None, :], segments[:, :, None], jnp.asarray(sums, BF), sums_t, states, pairs),
-        ("scalar", "z", "token", "token", "segment_row", "segment_column", "sums", "sums", "matrix", "matrix"),
+        ("scalar", "z", "token", "token", "segment_row", "segment_column", "sums", "sums_t", "matrix", "matrix"),
         (("dz", BF),),
         segments,
         z,
         ranks,
     )[0]
+
+
+def in_hbm(*arrays):
+    return [pltpu.with_memory_space_constraint(a, pltpu.HBM) for a in arrays]
 
 
 FREE = pl.CostEstimate(flops=0, bytes_accessed=0, transcendentals=0)
@@ -388,7 +419,14 @@
         out_shape=[jax.ShapeDtypeStruct(master.shape, F32)] * 4 + [jax.ShapeDtypeStruct((SMALL, n), F32)] * 2,
         compiler_params=pltpu.CompilerParams(vmem_limit_bytes=2 * VMEM_LIMIT),
         name="mixer_in_update",
-    )(rows, grads, small, *[a for a, _ in arrived], *[a for a, _ in arrived], master, moment, average)
+    )(
+        rows,
+        grads,
+        small,
+        *[a for a, _ in arrived],
+        *[a for a, _ in arrived],
+        *in_hbm(master, moment, average),
+    )
 
 
 def pair_gradient_kernel(rows_ref, first_ref, second_ref, *refs):
@@ -445,7 +483,7 @@
         compiler_params=pltpu.CompilerParams(vmem_limit_bytes=VMEM_LIMIT),
         cost_estimate=FREE,
         name="wide_gradient",
-    )(left, right, *[a for a, _ in arrived])
+    )(*in_hbm(left, right, *[a for a, _ in arrived]))
 
 
 def split_column(v):
@@ -568,7 +606,7 @@
         compiler_params=pltpu.CompilerParams(vmem_limit_bytes=VMEM_LIMIT),
         cost_estimate=pl.CostEstimate(flops=0, bytes_accessed=100_000_000, transcendentals=0),
         name="project_back",
-    )(grads, weight)
+    )(grads, *in_hbm(weight))
 
 
 def take_blocks_kernel(order_ref, in_ref, out_ref):
@@ -576,7 +614,7 @@
 
 
 def take_blocks(v, order):
-    rows, width = v.shape
+    rows, width = v.shape[0], D
     count = order.shape[0]
     block = (rows, width // count)
     return pl.pallas_call(
@@ -587,7 +625,7 @@
             in_specs=[pl.BlockSpec(block, lambda i, order: (0, order[i]))],
             out_specs=pl.BlockSpec(block, lambda i, order: (0, i)),
         ),
-        out_shape=jax.ShapeDtypeStruct(v.shape, v.dtype),
+        out_shape=jax.ShapeDtypeStruct((rows, width), v.dtype),
         compiler_params=pltpu.CompilerParams(vmem_limit_bytes=VMEM_LIMIT),
         cost_estimate=FREE,
         name="take_blocks",
@@ -624,7 +662,7 @@
         out_shape=[jax.ShapeDtypeStruct(master.shape, F32)] * 4,
         compiler_params=pltpu.CompilerParams(vmem_limit_bytes=VMEM_LIMIT),
         name="mixer_out_update",
-    )(act, rows, *[a for a, _ in arrived], master, moment, average)
+    )(act, rows, *[a for a, _ in arrived], *in_hbm(master, moment, average))
 
 
 def turn(v, axis, step):
@@ -899,47 +937,34 @@
     grad_first_parts = project_back(after(dz, sent), mixer_in_work, 512)
     in_sum.piece = in_piece(after(dz, grad_first_parts))
     sent = in_sum.send()
-    parts = [grad_first_parts[k * row_total : (k + 1) * row_total] for k in range(1, model_size)]
-    *parts, act_low, resid_full, dz_then, grad_blocks = lax.optimization_barrier(
-        (*parts, act_low, resid_full, dz, grad_blocks, sent)
-    )[:-1]
-    arrived = [turn(part, "mp", -k) for k, part in enumerate(parts, 1)]
-
-    resid_blocks = take_blocks(resid_full, order)
-
-    def out_piece(a, b, arrived, dtype=BF):
-        out = dot_tn(resid_blocks[:, a:b], act_low)
-        for r, at in arrived:
-            out = out + r[at : at + b - a].astype(F32)
-        return out.astype(dtype)
-
-    out_sum = GradientSum(out_piece)
-    out_sum.send()
+    ranked = jnp.concatenate(
+        [
+            lax.dynamic_slice_in_dim(grad_first_parts, (model_rank - r) % model_size * row_total, row_total, 0)
+            for r in range(model_size)
+        ]
+    )
+    ranked, dz_then, grad_blocks, _ = lax.optimization_barrier((ranked, dz, grad_blocks, sent))
+    grad_first = lax.all_to_all(ranked, "mp", 0, 0, tiled=True).reshape(model_size, row_total, D)
+
+    sent = mixer_out_grad = dot_tn(after(act_low, ranked), resid_full).astype(BF)
     at, _, feed_arrived = feed_out_sum.last()
     feed_out_share = wide_gradient(hidden_low, grad_blocks, (at, D), feed_arrived, 512)
     fourth = apply_update(feed_out, feed_out_moment, feed_out_average, feed_out_share.astype(F32))
 
-    in_sum.piece = in_piece(dz_then)
+    in_sum.piece = in_piece(after(dz_then, fourth[3], sent))
     sent = in_sum.send_rest()
-    out_sum.send()
-    resid_blocks = after(resid_blocks, sent)
-    out_sum.send_rest()
     feed_in_share = lax.psum_scatter(feed_in_grad, "dp", scatter_dimension=1, tiled=True)
     feed_in_share = after(feed_in_share, sent)
     third = apply_update(feed_in, feed_in_moment, feed_in_average, feed_in_share.astype(F32))
-    *arrived, _ = lax.optimization_barrier((*arrived, sent))
-    grad_first = grad_first_parts[:row_total].astype(F32)
-    for piece in arrived:
-        grad_first = grad_first + piece.astype(F32)
-    tokens_grad = (grad_resid + norm_back(inputs, inputs_scale, grad_first * gains[0])).astype(BF)
     *first, gain_one, small = mixer_in_update(
-        first_blocks, after(dz, third[3], tokens_grad), small, in_sum.last()[2], mixer_in, mixer_in_moment, mixer_in_average
+        first_blocks, after(dz, third[3]), small, in_sum.last()[2], mixer_in, mixer_in_moment, mixer_in_average
     )
     sums = jnp.concatenate([gain_one[:1], small[:3]])
-    resid_blocks = after(resid_blocks, sums)
-    second = tuple(
-        mixer_out_update(act_low, resid_blocks, out_sum.last()[2], mixer_out, mixer_out_moment, mixer_out_average)
-    )
+    mixer_out_share = lax.psum_scatter(mixer_out_grad, "dp", scatter_dimension=1, tiled=True)
+    mixer_out_share = after(mixer_out_share, sums)
+    second = apply_update(mixer_out, mixer_out_moment, mixer_out_average, mixer_out_share.astype(F32))
+    grad_first = jnp.sum(after(grad_first, sums).astype(F32), axis=0)
+    tokens_grad = (grad_resid + norm_back(inputs, inputs_scale, grad_first * gains[0])).astype(BF)
     sums = sums + sum(turn(sums, "mp", k) for k in range(1, model_size))
     sums = after(sums, second[3])
     gains_share = jnp.concatenate([sums[:1] / norm_gains[:1].astype(BF).astype(F32), sums[1:3]])

time: 530 us -> 512 us (0.966)
  local copies, waits for them, and re-layouts: 52.2 us -> 37.3 us
  waiting for transfers between devices: 187 us -> 200 us
  Pallas kernels: 87.8 us -> 75.9 us
  starting transfers between devices: 91.3 us -> 85.2 us
    ppermute x8 -> x6, waiting for transfers between devices: 21 us -> 44.6 us  [cross_swap(): lax.ppermute(v, 'dp', [(i, i ^ (odd if i & 1 else even)[stage]) for i in...]
    pallas_call x3 -> x2, Pallas kernels: 40.6 us -> 21.2 us  [mixer_call(): pl.pallas_call(functools.partial(kernel, ranks), grid=(heads // together,...]
    unnamed x208 -> x152, local copies, waits for them, and re-layouts: 39.2 us -> 23.2 us
    ppermute x27 -> x24, starting transfers between devices: 74.8 us -> 61.7 us  [turn(): return lax.ppermute(v, axis, [(i, (i + step) % n) for i in range(n)])]
    ppermute x27 -> x24, waiting for transfers between devices: 153 us -> 140 us  [turn(): return lax.ppermute(v, axis, [(i, (i + step) % n) for i in range(n)])]
    all_to_all x0 -> x1, starting transfers between devices: none -> 11.8 us  [per_device(): lax.all_to_all(ranked, 'mp', 0, 0, tiled=True)]
    add x3 -> x4, other arithmetic: 12.4 us -> 13.7 us  [apply_update(): average_new = AVERAGE_RATE * average + (1.0 - AVERAGE_RATE) * master_new]
  transfers between devices with their start and end apart: 46 -> 42, of which waited for: 21 -> 20; matrix products, arithmetic and copies ran while one was open for 14% -> 15% of each run, Pallas kernels for 16% -> 14%
where the time goes in v3:
time: 512 us; the launch traced here: 503 us
  waiting for transfers between devices  200 us (39%)
  starting transfers between devices  85.2 us (17%)
  Pallas kernels  75.9 us (15%)
  matrix products  43.6 us (9%)
  other arithmetic  43.5 us (8%)
  local copies, waits for them, and re-layouts  37.3 us (7%)
  between operations  18.4 us (4%)
    ppermute x24, waiting for transfers between devices, turn(): return lax.ppermute(v, axis, [(i, (i + step) % n) for i in range(n)])  140 us
    ppermute x24, starting transfers between devices, turn(): return lax.ppermute(v, axis, [(i, (i + step) % n) for i in range(n)])  61.7 us
    ppermute x6, waiting for transfers between devices, cross_swap(): lax.ppermute(v, 'dp', [(i, i ^ (odd if i & 1 else even)[stage]) for i in...  44.6 us
    unnamed x152, local copies, waits for them, and re-layouts  23.2 us
    pallas_call x2, Pallas kernels, mixer_call(): pl.pallas_call(functools.partial(kernel, ranks), grid=(heads // together,...  21.2 us
    dot_general x4, matrix products, dot_nt(): lax.dot_general(a, b, (((1,), (1,)), ((), ())), preferred_element_type=F32)  15.7 us
    add x4, other arithmetic, apply_update(): average_new = AVERAGE_RATE * average + (1.0 - AVERAGE_RATE) * master_new  13.7 us
    all_gather x3, waiting for transfers between devices, gather_weight(): return lax.all_gather(w.astype(BF), 'dp', axis=dim, tiled=True)  13.3 us
  transfers between devices with their start and end apart: 42, of which 20 were waited for; matrix products, arithmetic and copies ran while one was open for 15% of the time, Pallas kernels for 14%

profile of v3, /device:TPU:0, one launch (start us, length us, event | category | flops | bytes accessed | tf_op | source)
XLA Modules:
  0.0 503.4 jit_solution(829547089702004966)
XLA Ops:
  12.1 4.7 collective-permute-start.2
  24.3 5.2 %collective-permute-done.6 = bf16[512,256]{1,0:T(8,128)(2,1)S(1)} collective-permute-done((bf16[512,256]{1,0:T(8,128)(2,1)S(1)}, bf16[512,256]{1,0:T(8,128)(2,1)S(1)}, u32[]{:S(2)}, u32[]{:S(2)}) %collective-permute-start.6) | collective-permute-done | bytes 262176 | tf_op jit(solution)/shard_map/ppermute | solution.py:740
  34.5 6.4 %collective-permute-done.7 = bf16[512,512]{1,0:T(8,128)(2,1)S(1)} collective-permute-done((bf16[512,512]{1,0:T(8,128)(2,1)S(1)}, bf16[512,512]{1,0:T(8,128)(2,1)S(1)}, u32[]{:S(2)}, u32[]{:S(2)}) %collective-permute-start.7) | collective-permute-done | bytes 524320 | tf_op jit(solution)/shard_map/ppermute | solution.py:740
  42.8 8.1 %collective-permute-done.1 = bf16[96,2048]{1,0:T(8,128)(2,1)S(1)} collective-permute-done((bf16[96,2048]{1,0:T(8,128)(2,1)S(1)}, bf16[96,2048]{1,0:T(8,128)(2,1)S(1)}, u32[]{:S(2)}, u32[]{:S(2)}) %collective-permute-start.1) | collective-permute-done | bytes 393248 | tf_op jit(solution)/shard_map/ppermute | solution.py:670
  60.9 12.1 %all-gather.4.cloned.1.call-done.weight_ref = bf16[4,2048,512]{2,1,0:T(8,128)(2,1)} async-done(((bf16[4,256,512]{2,1,0:T(8,128)(2,1)}), bf16[4,2048,512]{2,1,0:T(8,128)(2,1)}) %all-gather.4.cloned.1.call-update) | async-done | bytes 8388624 | tf_op jit(solution)/shard_map/all_gather | solution.py:711
  73.0 8.5 %convolution_bitcast_fusion.1.z_ref = f32[4,384,512]{2,1,0:T(8,128)} fusion(bf16[4,2048,512]{2,1,0:T(8,128)(2,1)} %all-gather.4.cloned.1.call-done.weight_ref, bf16[384,2048]{1,0:T(8,128)(2,1)S(1)} %fusion.4.in_ref), kind=kOutput, calls=%fused_computation.25 | convolution fusion | flops 3221225472 | bytes 13107200 | tf_op jit(solution)/shard_map/td,jde->jte/dot_general | solution.py:857
  81.6 10.3 %mixer_forward.1 = (f32[384,512]{1,0:T(8,128)S(1)}, f32[384,1]{1,0:T(8,128)S(1)}, f32[1,4,3,128,128]{4,3,2,1,0:T(8,128)S(1)}, bf16[1,4,3,128,128]{4,3,2,1,0:T(8,128)(2,1)S(1)}) custom-call(s32[2]{0:T(128)S(1)} %pad_add_fusion.scalar_ref, f32[4,384,512]{2,1,0:T(8,128)} %convolution_bitcast_fusion.1.z_ref, s32[1,1,384]{2,1,0:T(1,128)} %bitcast.71, ...), custom_call_target="tpu_custom_call" | custom-call | tf_op jit(solution)/shard_map/mixer_forward/pallas_call | solution.py:275
  107.0 6.3 %collective-permute-done.9.refs_0_ = bf16[96,2176]{1,0:T(8,128)(2,1)} collective-permute-done((bf16[96,2176]{1,0:T(8,128)(2,1)}, bf16[96,2176]{1,0:T(8,128)(2,1)}, u32[]{:S(2)}, u32[]{:S(2)}) %collective-permute-start.9) | collective-permute-done | bytes 417824 | tf_op jit(solution)/shard_map/ppermute | solution.py:670
  113.4 26.2 %collective-permute-done.10.refs_1_ = bf16[96,2176]{1,0:T(8,128)(2,1)} collective-permute-done((bf16[96,2176]{1,0:T(8,128)(2,1)}, bf16[96,2176]{1,0:T(8,128)(2,1)}, u32[]{:S(2)}, u32[]{:S(2)}) %collective-permute-start.10) | collective-permute-done | bytes 417824 | tf_op jit(solution)/shard_map/ppermute | solution.py:670
  147.0 13.8 %collective-permute-start.14 = (bf16[96,2048]{1,0:T(8,128)(2,1)S(1)}, bf16[96,2048]{1,0:T(8,128)(2,1)S(1)}, u32[]{:S(2)}, u32[]{:S(2)}) collective-permute-start(bf16[96,2048]{1,0:T(8,128)(2,1)S(1)} %get-tuple-element.75), channel_id=1, source_target_pairs={{0,3},{1,0},{2,1},{3,2},{4,7},{5,4},{6,5},{7,6},{8,11},{9,8},{10,9... | collective-permute-start | bytes 1179656 | tf_op jit(solution)/shard_map/ppermute | solution.py:670
  160.8 11.3 %collective-permute-done.13 = bf16[96,2048]{1,0:T(8,128)(2,1)S(1)} collective-permute-done((bf16[96,2048]{1,0:T(8,128)(2,1)S(1)}, bf16[96,2048]{1,0:T(8,128)(2,1)S(1)}, u32[]{:S(2)}, u32[]{:S(2)}) %collective-permute-start.13) | collective-permute-done | bytes 393248 | tf_op jit(solution)/shard_map/ppermute | solution.py:670
  172.2 4.7 collective-permute-done.14
  176.9 8.4 %convolution_bitcast_fusion = f32[2,384,1408]{2,1,0:T(8,128)S(1)} fusion(bf16[2,2048,1408]{2,1,0:T(8,128)(2,1)} %all-gather.6.cloned.1.call-done, bf16[384,2048]{1,0:T(8,128)(2,1)S(1)} %constant_dynamic-update-slice_fusion.rows_ref.right_ref), kind=kOutput, calls=%fused_computation.6 | convolution fusion | flops 4429185024 | bytes 17432576 | tf_op jit(solution)/shard_map/td,jdf->jtf/dot_general | solution.py:876
  190.1 5.6 %convolution_convert_fusion.1 = bf16[384,2048]{1,0:T(8,128)(2,1)S(1)} fusion(bf16[384,1408]{1,0:T(8,128)(2,1)} %multiply_convert_fusion.2.left_ref, bf16[1408,2048]{1,0:T(8,128)(2,1)} %all-gather.8.cloned.1.call-done), kind=kOutput, calls=%fused_computation.16 | convolution fusion | flops 2215378944 | bytes 8421376 | tf_op jit(solution)/shard_map/dot_general | solution.py:44
  208.5 5.4 %collective-permute-done.17 = bf16[96,2048]{1,0:T(8,128)(2,1)} collective-permute-done((bf16[96,2048]{1,0:T(8,128)(2,1)}, bf16[96,2048]{1,0:T(8,128)(2,1)}, u32[]{:S(2)}, u32[]{:S(2)}) %collective-permute-start.17) | collective-permute-done | bytes 393248 | tf_op jit(solution)/shard_map/ppermute | solution.py:670
  213.8 15.1 %collective-permute-done.16 = bf16[96,2048]{1,0:T(8,128)(2,1)} collective-permute-done((bf16[96,2048]{1,0:T(8,128)(2,1)}, bf16[96,2048]{1,0:T(8,128)(2,1)}, u32[]{:S(2)}, u32[]{:S(2)}) %collective-permute-start.16) | collective-permute-done | bytes 393248 | tf_op jit(solution)/shard_map/ppermute | solution.py:670
  232.6 9.2 %collective-permute-start.20 = (bf16[96,2048]{1,0:T(8,128)(2,1)S(1)}, bf16[96,2048]{1,0:T(8,128)(2,1)S(1)}, u32[]{:S(2)}, u32[]{:S(2)}) collective-permute-start(bf16[96,2048]{1,0:T(8,128)(2,1)S(1)} %get-tuple-element.137), channel_id=1, source_target_pairs={{0,3},{1,0},{2,1},{3,2},{4,7},{5,4},{6,5},{7,6},{8,11},{9,8},{10,9... | collective-permute-start | bytes 1179656 | tf_op jit(solution)/shard_map/ppermute | solution.py:670
  243.0 8.5 %collective-permute-done.20 = bf16[96,2048]{1,0:T(8,128)(2,1)S(1)} collective-permute-done((bf16[96,2048]{1,0:T(8,128)(2,1)S(1)}, bf16[96,2048]{1,0:T(8,128)(2,1)S(1)}, u32[]{:S(2)}, u32[]{:S(2)}) %collective-permute-start.20) | collective-permute-done | bytes 393248 | tf_op jit(solution)/shard_map/ppermute | solution.py:670
  251.4 25.8 %collective-permute-done.19 = bf16[96,2048]{1,0:T(8,128)(2,1)S(1)} collective-permute-done((bf16[96,2048]{1,0:T(8,128)(2,1)S(1)}, bf16[96,2048]{1,0:T(8,128)(2,1)S(1)}, u32[]{:S(2)}, u32[]{:S(2)}) %collective-permute-start.19) | collective-permute-done | bytes 393248 | tf_op jit(solution)/shard_map/ppermute | solution.py:670
  277.3 5.8 %multiply_convert_fusion.1 = (bf16[384,1408]{1,0:T(8,128)(2,1)S(1)}, bf16[384,1408]{1,0:T(8,128)(2,1)S(1)}) fusion(f32[2,384,1408]{2,1,0:T(8,128)S(1)} %copy-done.35, bf16[1408,2048]{1,0:T(8,128)(2,1)} %all-gather.8.cloned.1.call-done, bf16[96,2048]{1,0:T(8,128)(2,1)S(1)} %collective-permute-done.20, bf16[96,2048]{1,0:T(8,128)(2,1)S(1)} %collective-permute-done.19, ...), kind=kOutput, calls=%fused_computation.21 | convolution fusion | flops 2227912704 | bytes 13828096 | tf_op jit(solution)/shard_map/dot_general | solution.py:48
  299.1 8.9 %pair_gradient.1 = bf16[2,2048,1408]{2,1,0:T(8,128)(2,1)S(1)} custom-call(bf16[384,2048]{1,0:T(8,128)(2,1)S(1)} %copy-done.4, bf16[384,1408]{1,0:T(8,128)(2,1)S(1)} %get-tuple-element.141.first_ref, bf16[384,1408]{1,0:T(8,128)(2,1)S(1)} %get-tuple-element.81.second_ref), custom_call_target="tpu_custom_call" | custom-call | tf_op jit(solution)/shard_map/pair_gradient/pallas_call | solution.py:448
  318.7 13.7 %collective-permute-done.22.refs_1_ = bf16[96,2048]{1,0:T(8,128)(2,1)} collective-permute-done((bf16[96,2048]{1,0:T(8,128)(2,1)}, bf16[96,2048]{1,0:T(8,128)(2,1)}, u32[]{:S(2)}, u32[]{:S(2)}) %collective-permute-start.22) | collective-permute-done | bytes 393248 | tf_op jit(solution)/shard_map/ppermute | solution.py:670
  345.7 6.2 %collective-permute-done.28.refs_1_ = bf16[1408,512]{1,0:T(8,128)(2,1)S(1)} collective-permute-done((bf16[1408,512]{1,0:T(8,128)(2,1)}, bf16[1408,512]{1,0:T(8,128)(2,1)S(1)}, u32[]{:S(2)}, u32[]{:S(2)}) %collective-permute-start.28) | collective-permute-done | bytes 1441824 | tf_op jit(solution)/shard_map/ppermute | solution.py:740
  356.2 15.2 %collective-permute-done.26 = bf16[96,2176]{1,0:T(8,128)(2,1)S(1)} collective-permute-done((bf16[96,2176]{1,0:T(8,128)(2,1)S(1)}, bf16[96,2176]{1,0:T(8,128)(2,1)S(1)}, u32[]{:S(2)}, u32[]{:S(2)}) %collective-permute-start.26) | collective-permute-done | bytes 417824 | tf_op jit(solution)/shard_map/ppermute | solution.py:670
  378.0 10.9 %mixer_backward.1.grads_ref = bf16[4,384,512]{2,1,0:T(8,128)(2,1)S(1)} custom-call(s32[2]{0:T(128)S(1)} %pad_add_fusion.scalar_ref, f32[4,384,512]{2,1,0:T(8,128)} %convolution_bitcast_fusion.1.z_ref, f32[384,512]{1,0:T(8,128)} %get-tuple-element.144.dout_ref, bf16[384,512]{1,0:T(8,128)(2,1)} %get-tuple-element.143.gate_ref, s32[1,1,384]{2,1,0:T(1,128)} %bitcast.72, ...), custom_call_target="tpu_custom_call" | custom-call | tf_op jit(solution)/shard_map/mixer_backward/pallas_call | solution.py:275
  393.8 6.4 %project_back.1 = bf16[384,2048]{1,0:T(8,128)(2,1)S(1)} custom-call(bf16[4,384,512]{2,1,0:T(8,128)(2,1)S(1)} %mixer_backward.1.grads_ref, bf16[4,2048,512]{2,1,0:T(8,128)(2,1)} %all-gather.4.cloned.1.call-done.weight_ref), custom_call_target="tpu_custom_call" | custom-call | bytes 100000000 | tf_op jit(solution)/shard_map/project_back/pallas_call | solution.py:597
  410.4 11.8 %all-to-all-start = ((bf16[4,96,2048]{2,1,0:T(8,128)(2,1)}), bf16[4,96,2048]{2,1,0:T(8,128)(2,1)}, u32[]{:S(2)}, u32[]{:S(2)}) async-start(bf16[4,96,2048]{2,1,0:T(8,128)(2,1)} %bitcast.67), calls=%async_computation | async-start | bytes 3145728 | tf_op jit(solution)/shard_map/all_to_all | solution.py:947
  429.0 14.8 %collective-permute-done.31.refs_1_.refs_4_ = bf16[512,2176]{1,0:T(8,128)(2,1)} collective-permute-done((bf16[512,2176]{1,0:T(8,128)(2,1)}, bf16[512,2176]{1,0:T(8,128)(2,1)}, u32[]{:S(2)}, u32[]{:S(2)}) %collective-permute-start.31) | collective-permute-done | bytes 2228256 | tf_op jit(solution)/shard_map/ppermute | solution.py:740
  447.8 8.8 %add_multiply_fusion = (f32[2,256,1408]{2,1,0:T(8,128)}, f32[2,256,1408]{2,1,0:T(8,128)}, f32[2,256,1408]{2,1,0:T(8,128)}, f32[2,256,1408]{2,1,0:T(8,128)}) fusion(f32[2,256,1408]{2,1,0:T(8,128)} %param.38, f32[2,256,1408]{2,1,0:T(8,128)} %param.36, f32[2,256,1408]{2,1,0:T(8,128)} %param.37, bf16[2,256,1408]{2,1,0:T(8,128)(2,1)} %reduce-scatter.3.cloned.1.call-done), kind=kLoop, calls=%fused_computation.13 | loop fusion | flops 6488064 | bytes 21626880 | tf_op jit(solution)/shard_map/add | solution.py:706
  456.6 12.1 %collective-permute-done.32.refs_2_.refs_5_ = bf16[256,2176]{1,0:T(8,128)(2,1)} collective-permute-done((bf16[256,2176]{1,0:T(8,128)(2,1)}, bf16[256,2176]{1,0:T(8,128)(2,1)}, u32[]{:S(2)}, u32[]{:S(2)}) %collective-permute-start.32) | collective-permute-done | bytes 1114144 | tf_op jit(solution)/shard_map/ppermute | solution.py:740
  468.7 8.1 %mixer_in_update.1 = (f32[4,256,512]{2,1,0:T(8,128)}, f32[4,256,512]{2,1,0:T(8,128)}, f32[4,256,512]{2,1,0:T(8,128)}, f32[4,256,512]{2,1,0:T(8,128)}, f32[8,256]{1,0:T(8,128)S(1)}, /*index=5*/f32[8,256]{1,0:T(8,128)S(1)}) custom-call(bf16[384,2048]{1,0:T(8,128)(2,1)S(1)} %take_blocks.3.rows_ref, bf16[4,384,512]{2,1,0:T(8,128)(2,1)S(1)} %mixer_backward.1.grads_ref, ...), custom_call_target="tpu_custom_call" | custom-call | tf_op jit(solution)/shard_map/mixer_in_update/pallas_call | solution.py:407
  477.4 8.5 %collective-permute-start.35 = (f32[4,256]{1,0:T(4,128)}, f32[4,256]{1,0:T(4,128)}, u32[]{:S(2)}, u32[]{:S(2)}) collective-permute-start(f32[4,256]{1,0:T(4,128)} %pad_maximum_fusion.11), channel_id=1, source_target_pairs={{0,3},{1,0},{2,1},{3,2},{4,7},{5,4},{6,5},{7,6},{8,11},{9,8},{10,9... | collective-permute-start | bytes 12296 | tf_op jit(solution)/shard_map/ppermute | solution.py:670
  (314 shorter events, 158.3 us)
Async XLA Ops:
  7.2 65.8 %all-gather.4.cloned.1.call-start = ((), (), s32[]{:S(2)}) async-start(), calls=%async_computation.3 | async-start | bytes 9437184 | tf_op jit(solution)/shard_map/all_gather | solution.py:711
  10.1 166.8 %all-gather.6.cloned.1.call-start = ((), (), s32[]{:S(2)}) async-start(), calls=%async_computation.4 | async-start | bytes 12976128 | tf_op jit(solution)/shard_map/all_gather | solution.py:711
  11.5 178.6 %all-gather.8.cloned.1.call-start = ((), (), s32[]{:S(2)}) async-start(), calls=%async_computation.5 | async-start | bytes 6488064 | tf_op jit(solution)/shard_map/all_gather | solution.py:711
  12.1 30.7 %collective-permute-start.2 = (bf16[96,2048]{1,0:T(8,128)(2,1)S(1)}, bf16[96,2048]{1,0:T(8,128)(2,1)S(1)}, u32[]{:S(2)}, u32[]{:S(2)}) collective-permute-start(bf16[96,2048]{1,0:T(8,128)(2,1)S(1)} %copy-done.2), channel_id=1, source_target_pairs={{0,3},{1,0},{2,1},{3,2},{4,7},{5,4},{6,5},{7,6},{8,11},{9,8},{10,9... | collective-permute-start | bytes 1179656 | tf_op jit(solution)/shard_map/ppermute | solution.py:670
  16.8 34.1 %collective-permute-start.1 = (bf16[96,2048]{1,0:T(8,128)(2,1)S(1)}, bf16[96,2048]{1,0:T(8,128)(2,1)S(1)}, u32[]{:S(2)}, u32[]{:S(2)}) collective-permute-start(bf16[96,2048]{1,0:T(8,128)(2,1)S(1)} %copy-done.2), channel_id=1, source_target_pairs={{0,2},{1,3},{2,0},{3,1},{4,6},{5,7},{6,4},{7,5},{8,10},{9,11},{10,... | collective-permute-start | bytes 1179656 | tf_op jit(solution)/shard_map/ppermute | solution.py:670
  16.8 34.1 %collective-permute-start = (bf16[96,2048]{1,0:T(8,128)(2,1)S(1)}, bf16[96,2048]{1,0:T(8,128)(2,1)S(1)}, u32[]{:S(2)}, u32[]{:S(2)}) collective-permute-start(bf16[96,2048]{1,0:T(8,128)(2,1)S(1)} %copy-done.2), channel_id=1, source_target_pairs={{0,1},{1,2},{2,3},{3,0},{4,5},{5,6},{6,7},{7,4},{8,9},{9,10},{10,1... | collective-permute-start | bytes 1179656 | tf_op jit(solution)/shard_map/ppermute | solution.py:670
  21.4 426.4 %reduce-scatter.3.cloned.1.call-start = ((), (), s32[]{:S(2)}) async-start(), calls=%async_computation.6 | async-start | bytes 12976128 | tf_op jit(solution)/shard_map/reduce_scatter | solution.py:956
  103.8 35.7 %collective-permute-start.10 = (bf16[96,2176]{1,0:T(8,128)(2,1)}, bf16[96,2176]{1,0:T(8,128)(2,1)}, u32[]{:S(2)}, u32[]{:S(2)}) collective-permute-start(bf16[96,2176]{1,0:T(8,128)(2,1)} %pad_maximum_fusion.6), channel_id=1, source_target_pairs={{0,2},{1,3},{2,0},{3,1},{4,6},{5,7},{6,4},{7,5},{8,10},{9,11},{10,... | collective-permute-start | bytes 1253384 | tf_op jit(solution)/shard_map/ppermute | solution.py:670
  104.7 34.8 %collective-permute-start.11 = (bf16[96,2176]{1,0:T(8,128)(2,1)}, bf16[96,2176]{1,0:T(8,128)(2,1)}, u32[]{:S(2)}, u32[]{:S(2)}) collective-permute-start(bf16[96,2176]{1,0:T(8,128)(2,1)} %pad_maximum_fusion.7), channel_id=1, source_target_pairs={{0,1},{1,2},{2,3},{3,0},{4,5},{5,6},{6,7},{7,4},{8,9},{9,10},{10,1... | collective-permute-start | bytes 1253384 | tf_op jit(solution)/shard_map/ppermute | solution.py:670
  142.9 17.9 %collective-permute-start.12 = (bf16[96,2048]{1,0:T(8,128)(2,1)S(1)}, bf16[96,2048]{1,0:T(8,128)(2,1)S(1)}, u32[]{:S(2)}, u32[]{:S(2)}) collective-permute-start(bf16[96,2048]{1,0:T(8,128)(2,1)S(1)} %get-tuple-element.75), channel_id=1, source_target_pairs={{0,1},{1,2},{2,3},{3,0},{4,5},{5,6},{6,7},{7,4},{8,9},{9,10},{10,1... | collective-permute-start | bytes 1179656 | tf_op jit(solution)/shard_map/ppermute | solution.py:670
  144.8 27.3 %collective-permute-start.13 = (bf16[96,2048]{1,0:T(8,128)(2,1)S(1)}, bf16[96,2048]{1,0:T(8,128)(2,1)S(1)}, u32[]{:S(2)}, u32[]{:S(2)}) collective-permute-start(bf16[96,2048]{1,0:T(8,128)(2,1)S(1)} %get-tuple-element.75), channel_id=1, source_target_pairs={{0,2},{1,3},{2,0},{3,1},{4,6},{5,7},{6,4},{7,5},{8,10},{9,11},{10,... | collective-permute-start | bytes 1179656 | tf_op jit(solution)/shard_map/ppermute | solution.py:670
  147.0 29.9 %collective-permute-start.14 = (bf16[96,2048]{1,0:T(8,128)(2,1)S(1)}, bf16[96,2048]{1,0:T(8,128)(2,1)S(1)}, u32[]{:S(2)}, u32[]{:S(2)}) collective-permute-start(bf16[96,2048]{1,0:T(8,128)(2,1)S(1)} %get-tuple-element.75), channel_id=1, source_target_pairs={{0,3},{1,0},{2,1},{3,2},{4,7},{5,4},{6,5},{7,6},{8,11},{9,8},{10,9... | collective-permute-start | bytes 1179656 | tf_op jit(solution)/shard_map/ppermute | solution.py:670
  197.8 16.1 %collective-permute-start.17 = (bf16[96,2048]{1,0:T(8,128)(2,1)}, bf16[96,2048]{1,0:T(8,128)(2,1)}, u32[]{:S(2)}, u32[]{:S(2)}) collective-permute-start(bf16[96,2048]{1,0:T(8,128)(2,1)} %get-tuple-element.154), channel_id=1, source_target_pairs={{0,1},{1,2},{2,3},{3,0},{4,5},{5,6},{6,7},{7,4},{8,9},{9,10},{10,1... | collective-permute-start | bytes 1179656 | tf_op jit(solution)/shard_map/ppermute | solution.py:670
  200.8 28.1 %collective-permute-start.16 = (bf16[96,2048]{1,0:T(8,128)(2,1)}, bf16[96,2048]{1,0:T(8,128)(2,1)}, u32[]{:S(2)}, u32[]{:S(2)}) collective-permute-start(bf16[96,2048]{1,0:T(8,128)(2,1)} %get-tuple-element.155), channel_id=1, source_target_pairs={{0,2},{1,3},{2,0},{3,1},{4,6},{5,7},{6,4},{7,5},{8,10},{9,11},{10,... | collective-permute-start | bytes 1179656 | tf_op jit(solution)/shard_map/ppermute | solution.py:670
  203.9 25.1 %collective-permute-start.15 = (bf16[96,2048]{1,0:T(8,128)(2,1)S(1)}, bf16[96,2048]{1,0:T(8,128)(2,1)}, u32[]{:S(2)}, u32[]{:S(2)}) collective-permute-start(bf16[96,2048]{1,0:T(8,128)(2,1)S(1)} %get-tuple-element.153), channel_id=1, source_target_pairs={{0,3},{1,0},{2,1},{3,2},{4,7},{5,4},{6,5},{7,6},{8,11},{9,8},{10,9... | collective-permute-start | bytes 1179656 | tf_op jit(solution)/shard_map/ppermute | solution.py:670
  232.6 18.8 %collective-permute-start.20 = (bf16[96,2048]{1,0:T(8,128)(2,1)S(1)}, bf16[96,2048]{1,0:T(8,128)(2,1)S(1)}, u32[]{:S(2)}, u32[]{:S(2)}) collective-permute-start(bf16[96,2048]{1,0:T(8,128)(2,1)S(1)} %get-tuple-element.137), channel_id=1, source_target_pairs={{0,3},{1,0},{2,1},{3,2},{4,7},{5,4},{6,5},{7,6},{8,11},{9,8},{10,9... | collective-permute-start | bytes 1179656 | tf_op jit(solution)/shard_map/ppermute | solution.py:670
  241.8 35.4 %collective-permute-start.19 = (bf16[96,2048]{1,0:T(8,128)(2,1)S(1)}, bf16[96,2048]{1,0:T(8,128)(2,1)S(1)}, u32[]{:S(2)}, u32[]{:S(2)}) collective-permute-start(bf16[96,2048]{1,0:T(8,128)(2,1)S(1)} %get-tuple-element.137), channel_id=1, source_target_pairs={{0,2},{1,3},{2,0},{3,1},{4,6},{5,7},{6,4},{7,5},{8,10},{9,11},{10,... | collective-permute-start | bytes 1179656 | tf_op jit(solution)/shard_map/ppermute | solution.py:670
  243.0 34.3 %collective-permute-start.18 = (bf16[96,2048]{1,0:T(8,128)(2,1)S(1)}, bf16[96,2048]{1,0:T(8,128)(2,1)S(1)}, u32[]{:S(2)}, u32[]{:S(2)}) collective-permute-start(bf16[96,2048]{1,0:T(8,128)(2,1)S(1)} %get-tuple-element.137), channel_id=1, source_target_pairs={{0,1},{1,2},{2,3},{3,0},{4,5},{5,6},{6,7},{7,4},{8,9},{9,10},{10,1... | collective-permute-start | bytes 1179656 | tf_op jit(solution)/shard_map/ppermute | solution.py:670
  296.4 18.4 %collective-permute-start.24 = (bf16[1408,1024]{1,0:T(8,128)(2,1)}, bf16[1408,1024]{1,0:T(8,128)(2,1)}, u32[]{:S(2)}, u32[]{:S(2)}) collective-permute-start(bf16[1408,1024]{1,0:T(8,128)(2,1)} %wide_gradient.4), channel_id=1, source_target_pairs={{0,4},{4,0},{8,12},{12,8},{16,20},{20,16},{24,28},{28,24},{1,5},{5... | collective-permute-start | bytes 8650760 | tf_op jit(solution)/shard_map/ppermute | solution.py:675
  296.4 22.3 %collective-permute-start.21 = (bf16[96,2048]{1,0:T(8,128)(2,1)}, bf16[96,2048]{1,0:T(8,128)(2,1)}, u32[]{:S(2)}, u32[]{:S(2)}) collective-permute-start(bf16[96,2048]{1,0:T(8,128)(2,1)} %get-tuple-element.77), channel_id=1, source_target_pairs={{0,3},{1,0},{2,1},{3,2},{4,7},{5,4},{6,5},{7,6},{8,11},{9,8},{10,9... | collective-permute-start | bytes 1179656 | tf_op jit(solution)/shard_map/ppermute | solution.py:670
  296.4 36.0 %collective-permute-start.22 = (bf16[96,2048]{1,0:T(8,128)(2,1)}, bf16[96,2048]{1,0:T(8,128)(2,1)}, u32[]{:S(2)}, u32[]{:S(2)}) collective-permute-start(bf16[96,2048]{1,0:T(8,128)(2,1)} %get-tuple-element.78), channel_id=1, source_target_pairs={{0,2},{1,3},{2,0},{3,1},{4,6},{5,7},{6,4},{7,5},{8,10},{9,11},{10,... | collective-permute-start | bytes 1179656 | tf_op jit(solution)/shard_map/ppermute | solution.py:670
  297.2 35.3 %collective-permute-start.23 = (bf16[96,2048]{1,0:T(8,128)(2,1)}, bf16[96,2048]{1,0:T(8,128)(2,1)}, u32[]{:S(2)}, u32[]{:S(2)}) collective-permute-start(bf16[96,2048]{1,0:T(8,128)(2,1)} %get-tuple-element.79), channel_id=1, source_target_pairs={{0,1},{1,2},{2,3},{3,0},{4,5},{5,6},{6,7},{7,4},{8,9},{9,10},{10,1... | collective-permute-start | bytes 1179656 | tf_op jit(solution)/shard_map/ppermute | solution.py:670
  332.5 157.1 %reduce-scatter.5.cloned.1.call-start = ((), (), s32[]{:S(2)}) async-start(), calls=%async_computation.7 | async-start | bytes 2359296 | tf_op jit(solution)/shard_map/reduce_scatter | solution.py:963
  332.5 19.3 %collective-permute-start.28 = (bf16[1408,512]{1,0:T(8,128)(2,1)}, bf16[1408,512]{1,0:T(8,128)(2,1)S(1)}, u32[]{:S(2)}, u32[]{:S(2)}) collective-permute-start(bf16[1408,512]{1,0:T(8,128)(2,1)} %copy-done.16), channel_id=1, source_target_pairs={{0,8},{4,20},{8,0},{12,28},{16,24},{20,4},{24,16},{28,12},{1,9},{5... | collective-permute-start | bytes 4325384 | tf_op jit(solution)/shard_map/ppermute | solution.py:740
  340.2 16.0 %collective-permute-start.25 = (bf16[96,2176]{1,0:T(8,128)(2,1)S(1)}, bf16[96,2176]{1,0:T(8,128)(2,1)S(1)}, u32[]{:S(2)}, u32[]{:S(2)}) collective-permute-start(bf16[96,2176]{1,0:T(8,128)(2,1)S(1)} %get-tuple-element.88), channel_id=1, source_target_pairs={{0,1},{1,2},{2,3},{3,0},{4,5},{5,6},{6,7},{7,4},{8,9},{9,10},{10,1... | collective-permute-start | bytes 1253384 | tf_op jit(solution)/shard_map/ppermute | solution.py:670
  340.5 30.9 %collective-permute-start.26 = (bf16[96,2176]{1,0:T(8,128)(2,1)S(1)}, bf16[96,2176]{1,0:T(8,128)(2,1)S(1)}, u32[]{:S(2)}, u32[]{:S(2)}) collective-permute-start(bf16[96,2176]{1,0:T(8,128)(2,1)S(1)} %get-tuple-element.88), channel_id=1, source_target_pairs={{0,2},{1,3},{2,0},{3,1},{4,6},{5,7},{6,4},{7,5},{8,10},{9,11},{10,... | collective-permute-start | bytes 1253384 | tf_op jit(solution)/shard_map/ppermute | solution.py:670
  342.7 28.6 %collective-permute-start.27 = (bf16[96,2176]{1,0:T(8,128)(2,1)S(1)}, bf16[96,2176]{1,0:T(8,128)(2,1)S(1)}, u32[]{:S(2)}, u32[]{:S(2)}) collective-permute-start(bf16[96,2176]{1,0:T(8,128)(2,1)S(1)} %get-tuple-element.88), channel_id=1, source_target_pairs={{0,3},{1,0},{2,1},{3,2},{4,7},{5,4},{6,5},{7,6},{8,11},{9,8},{10,9... | collective-permute-start | bytes 1253384 | tf_op jit(solution)/shard_map/ppermute | solution.py:670
  393.3 29.6 %collective-permute-start.30 = (bf16[1408,256]{1,0:T(8,128)(2,1)}, bf16[1408,256]{1,0:T(8,128)(2,1)}, u32[]{:S(2)}, u32[]{:S(2)}) collective-permute-start(bf16[1408,256]{1,0:T(8,128)(2,1)} %copy-done.22), channel_id=1, source_target_pairs={{0,16},{4,12},{8,24},{12,4},{16,0},{20,28},{24,8},{28,20},{1,17},{... | collective-permute-start | bytes 2162696 | tf_op jit(solution)/shard_map/ppermute | solution.py:740
  405.0 38.8 %collective-permute-start.31 = (bf16[512,2176]{1,0:T(8,128)(2,1)}, bf16[512,2176]{1,0:T(8,128)(2,1)}, u32[]{:S(2)}, u32[]{:S(2)}) collective-permute-start(bf16[512,2176]{1,0:T(8,128)(2,1)} %mixer_gradient.4), channel_id=1, source_target_pairs={{0,8},{4,20},{8,0},{12,28},{16,24},{20,4},{24,16},{28,12},{1,9},{5... | collective-permute-start | bytes 6684680 | tf_op jit(solution)/shard_map/ppermute | solution.py:740
  410.4 76.6 %all-to-all-start = ((bf16[4,96,2048]{2,1,0:T(8,128)(2,1)}), bf16[4,96,2048]{2,1,0:T(8,128)(2,1)}, u32[]{:S(2)}, u32[]{:S(2)}) async-start(bf16[4,96,2048]{2,1,0:T(8,128)(2,1)} %bitcast.67), calls=%async_computation | async-start | bytes 3145728 | tf_op jit(solution)/shard_map/all_to_all | solution.py:947
  447.2 21.4 %collective-permute-start.32 = (bf16[256,2176]{1,0:T(8,128)(2,1)}, bf16[256,2176]{1,0:T(8,128)(2,1)}, u32[]{:S(2)}, u32[]{:S(2)}) collective-permute-start(bf16[256,2176]{1,0:T(8,128)(2,1)} %mixer_gradient.5), channel_id=1, source_target_pairs={{0,16},{4,12},{8,24},{12,4},{16,0},{20,28},{24,8},{28,20},{1,17},{... | collective-permute-start | bytes 3342344 | tf_op jit(solution)/shard_map/ppermute | solution.py:740
  477.4 15.4 %collective-permute-start.35 = (f32[4,256]{1,0:T(4,128)}, f32[4,256]{1,0:T(4,128)}, u32[]{:S(2)}, u32[]{:S(2)}) collective-permute-start(f32[4,256]{1,0:T(4,128)} %pad_maximum_fusion.11), channel_id=1, source_target_pairs={{0,3},{1,0},{2,1},{3,2},{4,7},{5,4},{6,5},{7,6},{8,11},{9,8},{10,9... | collective-permute-start | bytes 12296 | tf_op jit(solution)/shard_map/ppermute | solution.py:670
  (83 other events, 866.0 us)
Sparse Core Ops, SparseCore 0:
  10.5 62.4 all-gather.3
  75.5 67.6 all-gather.5
  145.7 44.3 all-gather.7
  332.6 94.8 reduce-scatter.2
  430.6 45.4 reduce-scatter.4

commit v4 on v3

--- a/solution.py
+++ b/solution.py
@@ -104,7 +104,9 @@
             ref[(*index, piece, lanes)] = value[i * self.step : (i + 1) * self.step]
 
 
-def mixer_forward_kernel(ranks, scalar_ref, z_ref, seg_row_ref, seg_col_ref, sums_ref, o_ref, square_ref, state_ref, pair_ref):
+def mixer_forward_kernel(
+    ranks, scalar_ref, z_ref, gain_ref, seg_row_ref, seg_col_ref, sums_ref, o_ref, act_ref, square_ref, state_ref, pair_ref
+):
     step = pl.program_id(0)
     seqs, _, seq_len = seg_row_ref.shape
     chunks = seq_len // CHUNK
@@ -149,6 +151,8 @@
         position = c * CHUNK + lax.broadcasted_iota(jnp.int32, (CHUNK, 1), 0)
         out = jnp.where(position < scalar_ref[seq] * BLOCK, out, 0.0)
         ring.store(o_ref, first, out, lanes)
+        gate = ring.load(z_ref, first, lanes, 3)
+        ring.store(act_ref, first, (out * gain_ref[:, lanes] * (gate * sigmoid(gate))).astype(BF), lanes)
         square = jnp.sum(out * out, axis=1, keepdims=True)
         if h == 0:
             square = jnp.where(step == 0, square, ring.load(square_ref, first, slice(None)) + square)
@@ -262,6 +266,8 @@
     matrices = (seqs, heads, chunks, HEAD_DIM, HEAD_DIM)
     shapes = {
         "z": (None, pl.BlockSpec((3, rows, lanes), lambda h: (0, 0, h))),
+        "z_all": (None, pl.BlockSpec((4, rows, lanes), lambda h: (0, 0, h))),
+        "gain": (None, pl.BlockSpec((1, lanes), lambda h: (0, h))),
         "dz": ((4, rows, width), pl.BlockSpec((4, rows, lanes), lambda h: (0, 0, h))),
         "token": ((rows, width), pl.BlockSpec((rows, lanes), lambda h: (0, h))),
         "column": ((rows, 1), pl.BlockSpec((rows, 1), lambda h: (0, 0))),
@@ -280,17 +286,17 @@
         out_shape=[jax.ShapeDtypeStruct(shapes[kind][0], dtype) for kind, dtype in outputs],
         compiler_params=pltpu.CompilerParams(vmem_limit_bytes=VMEM_LIMIT),
         name=name,
-    )(*[pltpu.with_memory_space_constraint(v, pltpu.HBM) if v.ndim > 1 else v for v in operands])
-
-
-def mixer_forward(z, segments, scalars, ranks):
+    )(*operands)
+
+
+def mixer_forward(z, gain, segments, scalars, ranks):
     sums = jnp.asarray(decay_sums(), BF)
     return mixer_call(
         mixer_forward_kernel,
         "mixer_forward",
-        (scalars, z, segments[:, None, :], segments[:, :, None], sums),
-        ("scalar", "z", "segment_row", "segment_column", "sums"),
-        (("token", F32), ("column", F32), ("matrix", F32), ("matrix", BF)),
+        (scalars, z, gain, segments[:, None, :], segments[:, :, None], sums),
+        ("scalar", "z_all", "gain", "segment_row", "segment_column", "sums"),
+        (("token", F32), ("token", BF), ("column", F32), ("matrix", F32), ("matrix", BF)),
         segments,
         z,
         ranks,
@@ -303,7 +309,12 @@
     return mixer_call(
         mixer_backward_kernel,
         "mixer_backward",
-        (scalars, z, dout, gate_dz, segments[:, None, :], segments[:, :, None], jnp.asarray(sums, BF), sums_t, states, pairs),
+        (scalars,)
+        + tuple(
+            in_hbm(
+                z, dout, gate_dz, segments[:, None, :], segments[:, :, None], jnp.asarray(sums, BF), sums_t, states, pairs
+            )
+        ),
         ("scalar", "z", "token", "token", "segment_row", "segment_column", "sums", "sums_t", "matrix", "matrix"),
         (("dz", BF),),
         segments,
@@ -523,7 +534,7 @@
         ],
         compiler_params=pltpu.CompilerParams(vmem_limit_bytes=VMEM_LIMIT),
         name="after_mixer",
-    )(parts, square, tokens, gain, *arrived)
+    )(parts, square, *in_hbm(tokens), gain, *arrived)
 
 
 def after_feed_kernel(count, own_ref, resid_ref, tokens_ref, final_ref, gain_ref, scale_ref, *refs):
@@ -560,7 +571,7 @@
         out_shape=[jax.ShapeDtypeStruct((rows, D), F32), jax.ShapeDtypeStruct((rows, D + EXTRA), BF)],
         compiler_params=pltpu.CompilerParams(vmem_limit_bytes=VMEM_LIMIT),
         name="after_feed",
-    )(parts, resid, tokens, final, gain, scale, *arrived)
+    )(parts, *in_hbm(resid, tokens, final), gain, scale, *arrived)
 
 
 def column_sums_kernel(left_ref, right_ref, out_ref):
@@ -858,10 +869,9 @@
     gate_z = z[3]
     local_width = z.shape[2]
     gain_out = lax.dynamic_slice_in_dim(gains[2], model_rank * local_width, local_width, 0)[None]
-    recurrent, square, states, pairs = mixer_forward(z, segments, scalars, model_size)
+    recurrent, act_raw, square, states, pairs = mixer_forward(z, gain_out, segments, scalars, model_size)
     gate_z_sig = jax.nn.sigmoid(gate_z)
     gate_z_act = gate_z * gate_z_sig
-    act_raw = (recurrent * gain_out * gate_z_act).astype(BF)
     mixed_parts = dot(act_raw, mixer_out_work).astype(BF)
     arrived = []
     for k in range(1, model_size):

time: 512 us -> 509 us (level)
  waiting for transfers between devices: 200 us -> 213 us
  starting transfers between devices: 85.2 us -> 77.1 us
  local copies, waits for them, and re-layouts: 37.3 us -> 30.7 us
    ppermute x24, starting transfers between devices: 61.7 us -> 50.8 us  [turn(): return lax.ppermute(v, axis, [(i, (i + step) % n) for i in range(n)])]
    all_gather x3, waiting for transfers between devices: 13.3 us -> 23.7 us  [gather_weight(): return lax.all_gather(w.astype(BF), 'dp', axis=dim, tiled=True)]
    unnamed x152 -> x142, local copies, waits for them, and re-layouts: 23.2 us -> 18.1 us
  transfers between devices with their start and end apart: 42 -> 42, of which waited for: 20 -> 19; matrix products, arithmetic and copies ran while one was open for 15% -> 14% of each run, Pallas kernels for 14% -> 14%
where the time goes in v4:
time: 509 us; the launch traced here: 501 us
  waiting for transfers between devices  213 us (42%)
  starting transfers between devices  77.1 us (15%)
  Pallas kernels  76.1 us (15%)
  other arithmetic  44 us (9%)
  matrix products  41.4 us (8%)
  local copies, waits for them, and re-layouts  30.7 us (6%)
  between operations  18.3 us (4%)
    ppermute x24, waiting for transfers between devices, turn(): return lax.ppermute(v, axis, [(i, (i + step) % n) for i in range(n)])  143 us
    ppermute x24, starting transfers between devices, turn(): return lax.ppermute(v, axis, [(i, (i + step) % n) for i in range(n)])  50.8 us
    ppermute x6, waiting for transfers between devices, cross_swap(): lax.ppermute(v, 'dp', [(i, i ^ (odd if i & 1 else even)[stage]) for i in...  45.5 us
    all_gather x3, waiting for transfers between devices, gather_weight(): return lax.all_gather(w.astype(BF), 'dp', axis=dim, tiled=True)  23.7 us
    pallas_call x2, Pallas kernels, mixer_call(): pl.pallas_call(functools.partial(kernel, ranks), grid=(heads // together,...  20.4 us
    unnamed x142, local copies, waits for them, and re-layouts  18.1 us
    dot_general x4, matrix products, dot_nt(): lax.dot_general(a, b, (((1,), (1,)), ((), ())), preferred_element_type=F32)  16 us
    add x4, other arithmetic, apply_update(): average_new = AVERAGE_RATE * average + (1.0 - AVERAGE_RATE) * master_new  13.7 us
  transfers between devices with their start and end apart: 42, of which 19 were waited for; matrix products, arithmetic and copies ran while one was open for 14% of the time, Pallas kernels for 14%

profile of v4, /device:TPU:0, one launch (start us, length us, event | category | flops | bytes accessed | tf_op | source)
XLA Modules:
  0.0 501.1 jit_solution(2640771216425334696)
XLA Ops:
  12.1 4.7 collective-permute-start.2
  23.6 5.9 %collective-permute-done.6 = bf16[512,256]{1,0:T(8,128)(2,1)S(1)} collective-permute-done((bf16[512,256]{1,0:T(8,128)(2,1)S(1)}, bf16[512,256]{1,0:T(8,128)(2,1)S(1)}, u32[]{:S(2)}, u32[]{:S(2)}) %collective-permute-start.6) | collective-permute-done | bytes 262176 | tf_op jit(solution)/shard_map/ppermute | solution.py:751
  34.5 6.3 %collective-permute-done.7 = bf16[512,512]{1,0:T(8,128)(2,1)S(1)} collective-permute-done((bf16[512,512]{1,0:T(8,128)(2,1)S(1)}, bf16[512,512]{1,0:T(8,128)(2,1)S(1)}, u32[]{:S(2)}, u32[]{:S(2)}) %collective-permute-start.7) | collective-permute-done | bytes 524320 | tf_op jit(solution)/shard_map/ppermute | solution.py:751
  42.9 8.0 %collective-permute-done.1 = bf16[96,2048]{1,0:T(8,128)(2,1)S(1)} collective-permute-done((bf16[96,2048]{1,0:T(8,128)(2,1)S(1)}, bf16[96,2048]{1,0:T(8,128)(2,1)S(1)}, u32[]{:S(2)}, u32[]{:S(2)}) %collective-permute-start.1) | collective-permute-done | bytes 393248 | tf_op jit(solution)/shard_map/ppermute | solution.py:681
  61.6 11.4 %all-gather.4.cloned.1.call-done.weight_ref = bf16[4,2048,512]{2,1,0:T(8,128)(2,1)} async-done(((bf16[4,256,512]{2,1,0:T(8,128)(2,1)}), bf16[4,2048,512]{2,1,0:T(8,128)(2,1)}) %all-gather.4.cloned.1.call-update) | async-done | bytes 8388624 | tf_op jit(solution)/shard_map/all_gather | solution.py:722
  73.0 5.9 %convolution_bitcast_fusion.1.z_ref = f32[4,384,512]{2,1,0:T(8,128)S(1)} fusion(bf16[4,2048,512]{2,1,0:T(8,128)(2,1)} %all-gather.4.cloned.1.call-done.weight_ref, bf16[384,2048]{1,0:T(8,128)(2,1)S(1)} %fusion.4.in_ref), kind=kOutput, calls=%fused_computation.25 | convolution fusion | flops 3221225472 | bytes 13107200 | tf_op jit(solution)/shard_map/td,jde->jte/dot_general | solution.py:868
  78.9 9.8 %mixer_forward.1 = (f32[384,512]{1,0:T(8,128)S(1)}, bf16[384,512]{1,0:T(8,128)(2,1)S(1)}, f32[384,1]{1,0:T(8,128)S(1)}, f32[1,4,3,128,128]{4,3,2,1,0:T(8,128)S(1)}, bf16[1,4,3,128,128]{4,3,2,1,0:T(8,128)(2,1)S(1)}) custom-call(s32[2]{0:T(128)S(1)} %pad_add_fusion.scalar_ref, f32[4,384,512]{2,1,0:T(8,128)S(1)} %convolution_bitcast_fusion.1.z_ref, ...), custom_call_target="tpu_custom_call" | custom-call | tf_op jit(solution)/shard_map/mixer_forward/pallas_call | solution.py:281
  101.9 6.3 %collective-permute-done.9.refs_0_ = bf16[96,2176]{1,0:T(8,128)(2,1)} collective-permute-done((bf16[96,2176]{1,0:T(8,128)(2,1)}, bf16[96,2176]{1,0:T(8,128)(2,1)}, u32[]{:S(2)}, u32[]{:S(2)}) %collective-permute-start.9) | collective-permute-done | bytes 417824 | tf_op jit(solution)/shard_map/ppermute | solution.py:681
  108.2 26.2 %collective-permute-done.10.refs_1_ = bf16[96,2176]{1,0:T(8,128)(2,1)} collective-permute-done((bf16[96,2176]{1,0:T(8,128)(2,1)}, bf16[96,2176]{1,0:T(8,128)(2,1)}, u32[]{:S(2)}, u32[]{:S(2)}) %collective-permute-start.10) | collective-permute-done | bytes 417824 | tf_op jit(solution)/shard_map/ppermute | solution.py:681
  143.7 6.7 %collective-permute-done.12 = bf16[96,2048]{1,0:T(8,128)(2,1)S(1)} collective-permute-done((bf16[96,2048]{1,0:T(8,128)(2,1)S(1)}, bf16[96,2048]{1,0:T(8,128)(2,1)S(1)}, u32[]{:S(2)}, u32[]{:S(2)}) %collective-permute-start.12) | collective-permute-done | bytes 393248 | tf_op jit(solution)/shard_map/ppermute | solution.py:681
  150.4 15.2 %collective-permute-done.13 = bf16[96,2048]{1,0:T(8,128)(2,1)S(1)} collective-permute-done((bf16[96,2048]{1,0:T(8,128)(2,1)S(1)}, bf16[96,2048]{1,0:T(8,128)(2,1)S(1)}, u32[]{:S(2)}, u32[]{:S(2)}) %collective-permute-start.13) | collective-permute-done | bytes 393248 | tf_op jit(solution)/shard_map/ppermute | solution.py:681
  165.8 8.4 %convolution_bitcast_fusion = f32[2,384,1408]{2,1,0:T(8,128)S(1)} fusion(bf16[2,2048,1408]{2,1,0:T(8,128)(2,1)} %all-gather.6.cloned.1.call-done, bf16[384,2048]{1,0:T(8,128)(2,1)S(1)} %constant_dynamic-update-slice_fusion.rows_ref.right_ref), kind=kOutput, calls=%fused_computation.6 | convolution fusion | flops 4429185024 | bytes 17432576 | tf_op jit(solution)/shard_map/td,jdf->jtf/dot_general | solution.py:886
  177.8 12.3 %all-gather.8.cloned.1.call-done = bf16[1408,2048]{1,0:T(8,128)(2,1)} async-done(((bf16[1408,256]{1,0:T(8,128)(2,1)}), bf16[1408,2048]{1,0:T(8,128)(2,1)}) %all-gather.8.cloned.1.call-update) | async-done | bytes 5767184 | tf_op jit(solution)/shard_map/all_gather | solution.py:722
  190.1 5.6 %convolution_convert_fusion.1 = bf16[384,2048]{1,0:T(8,128)(2,1)S(1)} fusion(bf16[384,1408]{1,0:T(8,128)(2,1)} %multiply_convert_fusion.2.left_ref, bf16[1408,2048]{1,0:T(8,128)(2,1)} %all-gather.8.cloned.1.call-done), kind=kOutput, calls=%fused_computation.16 | convolution fusion | flops 2215378944 | bytes 8421376 | tf_op jit(solution)/shard_map/dot_general | solution.py:44
  211.9 16.2 %collective-permute-done.16 = bf16[96,2048]{1,0:T(8,128)(2,1)} collective-permute-done((bf16[96,2048]{1,0:T(8,128)(2,1)S(1)}, bf16[96,2048]{1,0:T(8,128)(2,1)}, u32[]{:S(2)}, u32[]{:S(2)}) %collective-permute-start.16) | collective-permute-done | bytes 393248 | tf_op jit(solution)/shard_map/ppermute | solution.py:681
  232.7 9.9 %collective-permute-start.20 = (bf16[96,2048]{1,0:T(8,128)(2,1)S(1)}, bf16[96,2048]{1,0:T(8,128)(2,1)S(1)}, u32[]{:S(2)}, u32[]{:S(2)}) collective-permute-start(bf16[96,2048]{1,0:T(8,128)(2,1)S(1)} %get-tuple-element.139), channel_id=1, source_target_pairs={{0,3},{1,0},{2,1},{3,2},{4,7},{5,4},{6,5},{7,6},{8,11},{9,8},{10,9... | collective-permute-start | bytes 1179656 | tf_op jit(solution)/shard_map/ppermute | solution.py:681
  243.3 8.8 %collective-permute-done.20 = bf16[96,2048]{1,0:T(8,128)(2,1)S(1)} collective-permute-done((bf16[96,2048]{1,0:T(8,128)(2,1)S(1)}, bf16[96,2048]{1,0:T(8,128)(2,1)S(1)}, u32[]{:S(2)}, u32[]{:S(2)}) %collective-permute-start.20) | collective-permute-done | bytes 393248 | tf_op jit(solution)/shard_map/ppermute | solution.py:681
  252.1 25.2 %collective-permute-done.19 = bf16[96,2048]{1,0:T(8,128)(2,1)S(1)} collective-permute-done((bf16[96,2048]{1,0:T(8,128)(2,1)S(1)}, bf16[96,2048]{1,0:T(8,128)(2,1)S(1)}, u32[]{:S(2)}, u32[]{:S(2)}) %collective-permute-start.19) | collective-permute-done | bytes 393248 | tf_op jit(solution)/shard_map/ppermute | solution.py:681
  277.4 5.7 %multiply_convert_fusion.1 = (bf16[384,1408]{1,0:T(8,128)(2,1)S(1)}, bf16[384,1408]{1,0:T(8,128)(2,1)S(1)}) fusion(f32[2,384,1408]{2,1,0:T(8,128)S(1)} %copy-done.36, bf16[1408,2048]{1,0:T(8,128)(2,1)} %all-gather.8.cloned.1.call-done, bf16[96,2048]{1,0:T(8,128)(2,1)S(1)} %collective-permute-done.20, bf16[96,2048]{1,0:T(8,128)(2,1)S(1)} %collective-permute-done.19, ...), kind=kOutput, calls=%fused_computation.21 | convolution fusion | flops 2227912704 | bytes 13828096 | tf_op jit(solution)/shard_map/dot_general | solution.py:48
  299.5 8.9 %pair_gradient.1 = bf16[2,2048,1408]{2,1,0:T(8,128)(2,1)S(1)} custom-call(bf16[384,2048]{1,0:T(8,128)(2,1)S(1)} %copy-done.4, bf16[384,1408]{1,0:T(8,128)(2,1)S(1)} %get-tuple-element.143.first_ref, bf16[384,1408]{1,0:T(8,128)(2,1)S(1)} %get-tuple-element.82.second_ref), custom_call_target="tpu_custom_call" | custom-call | tf_op jit(solution)/shard_map/pair_gradient/pallas_call | solution.py:459
  319.0 13.8 %collective-permute-done.22.refs_1_ = bf16[96,2048]{1,0:T(8,128)(2,1)} collective-permute-done((bf16[96,2048]{1,0:T(8,128)(2,1)}, bf16[96,2048]{1,0:T(8,128)(2,1)}, u32[]{:S(2)}, u32[]{:S(2)}) %collective-permute-start.22) | collective-permute-done | bytes 393248 | tf_op jit(solution)/shard_map/ppermute | solution.py:681
  343.7 8.5 %collective-permute-done.28.refs_1_ = bf16[1408,512]{1,0:T(8,128)(2,1)S(1)} collective-permute-done((bf16[1408,512]{1,0:T(8,128)(2,1)}, bf16[1408,512]{1,0:T(8,128)(2,1)S(1)}, u32[]{:S(2)}, u32[]{:S(2)}) %collective-permute-start.28) | collective-permute-done | bytes 1441824 | tf_op jit(solution)/shard_map/ppermute | solution.py:751
  356.5 12.3 %collective-permute-done.26 = bf16[96,2176]{1,0:T(8,128)(2,1)S(1)} collective-permute-done((bf16[96,2176]{1,0:T(8,128)(2,1)S(1)}, bf16[96,2176]{1,0:T(8,128)(2,1)S(1)}, u32[]{:S(2)}, u32[]{:S(2)}) %collective-permute-start.26) | collective-permute-done | bytes 417824 | tf_op jit(solution)/shard_map/ppermute | solution.py:681
  369.4 5.0 multiply_convert_fusion.4
  375.8 10.6 %mixer_backward.1.grads_ref = bf16[4,384,512]{2,1,0:T(8,128)(2,1)S(1)} custom-call(s32[2]{0:T(128)S(1)} %copy-done.22, f32[4,384,512]{2,1,0:T(8,128)} %copy-done.2, f32[384,512]{1,0:T(8,128)} %get-tuple-element.146.dout_ref, bf16[384,512]{1,0:T(8,128)(2,1)} %get-tuple-element.145.gate_ref, s32[1,1,384]{2,1,0:T(1,128)} %bitcast.65, s32[1,384,1]{2,1,0:T(8,128)} %copy-done.10, ...), custom_call_target="tpu_custom_call" | custom-call | tf_op jit(solution)/shard_map/mixer_backward/pallas_call | solution.py:281
  392.3 6.5 %project_back.1 = bf16[384,2048]{1,0:T(8,128)(2,1)S(1)} custom-call(bf16[4,384,512]{2,1,0:T(8,128)(2,1)S(1)} %mixer_backward.1.grads_ref, bf16[4,2048,512]{2,1,0:T(8,128)(2,1)} %all-gather.4.cloned.1.call-done.weight_ref), custom_call_target="tpu_custom_call" | custom-call | bytes 100000000 | tf_op jit(solution)/shard_map/project_back/pallas_call | solution.py:608
  409.2 11.7 %all-to-all-start = ((bf16[4,96,2048]{2,1,0:T(8,128)(2,1)}), bf16[4,96,2048]{2,1,0:T(8,128)(2,1)}, u32[]{:S(2)}, u32[]{:S(2)}) async-start(bf16[4,96,2048]{2,1,0:T(8,128)(2,1)} %bitcast.69), calls=%async_computation | async-start | bytes 3145728 | tf_op jit(solution)/shard_map/all_to_all | solution.py:957
  427.7 13.6 %collective-permute-done.31.refs_1_.refs_4_ = bf16[512,2176]{1,0:T(8,128)(2,1)} collective-permute-done((bf16[512,2176]{1,0:T(8,128)(2,1)}, bf16[512,2176]{1,0:T(8,128)(2,1)}, u32[]{:S(2)}, u32[]{:S(2)}) %collective-permute-start.31) | collective-permute-done | bytes 2228256 | tf_op jit(solution)/shard_map/ppermute | solution.py:751
  446.3 8.8 %add_multiply_fusion = (f32[2,256,1408]{2,1,0:T(8,128)}, f32[2,256,1408]{2,1,0:T(8,128)}, f32[2,256,1408]{2,1,0:T(8,128)}, f32[2,256,1408]{2,1,0:T(8,128)}) fusion(f32[2,256,1408]{2,1,0:T(8,128)} %param.38, f32[2,256,1408]{2,1,0:T(8,128)} %param.36, f32[2,256,1408]{2,1,0:T(8,128)} %param.37, bf16[2,256,1408]{2,1,0:T(8,128)(2,1)} %reduce-scatter.3.cloned.1.call-done), kind=kLoop, calls=%fused_computation.13 | loop fusion | flops 6488064 | bytes 21626880 | tf_op jit(solution)/shard_map/add | solution.py:717
  455.1 11.1 %collective-permute-done.32.refs_2_.refs_5_ = bf16[256,2176]{1,0:T(8,128)(2,1)} collective-permute-done((bf16[256,2176]{1,0:T(8,128)(2,1)}, bf16[256,2176]{1,0:T(8,128)(2,1)}, u32[]{:S(2)}, u32[]{:S(2)}) %collective-permute-start.32) | collective-permute-done | bytes 1114144 | tf_op jit(solution)/shard_map/ppermute | solution.py:751
  466.2 8.1 %mixer_in_update.1 = (f32[4,256,512]{2,1,0:T(8,128)}, f32[4,256,512]{2,1,0:T(8,128)}, f32[4,256,512]{2,1,0:T(8,128)}, f32[4,256,512]{2,1,0:T(8,128)}, f32[8,256]{1,0:T(8,128)S(1)}, /*index=5*/f32[8,256]{1,0:T(8,128)S(1)}) custom-call(bf16[384,2048]{1,0:T(8,128)(2,1)S(1)} %take_blocks.3.rows_ref, bf16[4,384,512]{2,1,0:T(8,128)(2,1)S(1)} %mixer_backward.1.grads_ref, ...), custom_call_target="tpu_custom_call" | custom-call | tf_op jit(solution)/shard_map/mixer_in_update/pallas_call | solution.py:418
  474.9 9.3 %collective-permute-start.35 = (f32[4,256]{1,0:T(4,128)}, f32[4,256]{1,0:T(4,128)}, u32[]{:S(2)}, u32[]{:S(2)}) collective-permute-start(f32[4,256]{1,0:T(4,128)} %pad_maximum_fusion.11), channel_id=1, source_target_pairs={{0,3},{1,0},{2,1},{3,2},{4,7},{5,4},{6,5},{7,6},{8,11},{9,8},{10,9... | collective-permute-start | bytes 12296 | tf_op jit(solution)/shard_map/ppermute | solution.py:681
  (303 shorter events, 156.0 us)
Async XLA Ops:
  7.2 65.8 %all-gather.4.cloned.1.call-start = ((), (), s32[]{:S(2)}) async-start(), calls=%async_computation.3 | async-start | bytes 9437184 | tf_op jit(solution)/shard_map/all_gather | solution.py:722
  10.1 155.6 %all-gather.6.cloned.1.call-start = ((), (), s32[]{:S(2)}) async-start(), calls=%async_computation.4 | async-start | bytes 12976128 | tf_op jit(solution)/shard_map/all_gather | solution.py:722
  11.5 178.6 %all-gather.8.cloned.1.call-start = ((), (), s32[]{:S(2)}) async-start(), calls=%async_computation.5 | async-start | bytes 6488064 | tf_op jit(solution)/shard_map/all_gather | solution.py:722
  12.1 30.8 %collective-permute-start.2 = (bf16[96,2048]{1,0:T(8,128)(2,1)S(1)}, bf16[96,2048]{1,0:T(8,128)(2,1)S(1)}, u32[]{:S(2)}, u32[]{:S(2)}) collective-permute-start(bf16[96,2048]{1,0:T(8,128)(2,1)S(1)} %copy-done.27), channel_id=1, source_target_pairs={{0,3},{1,0},{2,1},{3,2},{4,7},{5,4},{6,5},{7,6},{8,11},{9,8},{10,9... | collective-permute-start | bytes 1179656 | tf_op jit(solution)/shard_map/ppermute | solution.py:681
  16.8 34.1 %collective-permute-start.1 = (bf16[96,2048]{1,0:T(8,128)(2,1)S(1)}, bf16[96,2048]{1,0:T(8,128)(2,1)S(1)}, u32[]{:S(2)}, u32[]{:S(2)}) collective-permute-start(bf16[96,2048]{1,0:T(8,128)(2,1)S(1)} %copy-done.27), channel_id=1, source_target_pairs={{0,2},{1,3},{2,0},{3,1},{4,6},{5,7},{6,4},{7,5},{8,10},{9,11},{10,... | collective-permute-start | bytes 1179656 | tf_op jit(solution)/shard_map/ppermute | solution.py:681
  16.8 34.1 %collective-permute-start = (bf16[96,2048]{1,0:T(8,128)(2,1)S(1)}, bf16[96,2048]{1,0:T(8,128)(2,1)}, u32[]{:S(2)}, u32[]{:S(2)}) collective-permute-start(bf16[96,2048]{1,0:T(8,128)(2,1)S(1)} %copy-done.27), channel_id=1, source_target_pairs={{0,1},{1,2},{2,3},{3,0},{4,5},{5,6},{6,7},{7,4},{8,9},{9,10},{10,1... | collective-permute-start | bytes 1179656 | tf_op jit(solution)/shard_map/ppermute | solution.py:681
  21.4 424.9 %reduce-scatter.3.cloned.1.call-start = ((), (), s32[]{:S(2)}) async-start(), calls=%async_computation.6 | async-start | bytes 12976128 | tf_op jit(solution)/shard_map/reduce_scatter | solution.py:966
  98.7 35.7 %collective-permute-start.10 = (bf16[96,2176]{1,0:T(8,128)(2,1)}, bf16[96,2176]{1,0:T(8,128)(2,1)}, u32[]{:S(2)}, u32[]{:S(2)}) collective-permute-start(bf16[96,2176]{1,0:T(8,128)(2,1)} %pad_maximum_fusion.6), channel_id=1, source_target_pairs={{0,2},{1,3},{2,0},{3,1},{4,6},{5,7},{6,4},{7,5},{8,10},{9,11},{10,... | collective-permute-start | bytes 1253384 | tf_op jit(solution)/shard_map/ppermute | solution.py:681
  99.6 34.8 %collective-permute-start.11 = (bf16[96,2176]{1,0:T(8,128)(2,1)}, bf16[96,2176]{1,0:T(8,128)(2,1)}, u32[]{:S(2)}, u32[]{:S(2)}) collective-permute-start(bf16[96,2176]{1,0:T(8,128)(2,1)} %pad_maximum_fusion.7), channel_id=1, source_target_pairs={{0,1},{1,2},{2,3},{3,0},{4,5},{5,6},{6,7},{7,4},{8,9},{9,10},{10,1... | collective-permute-start | bytes 1253384 | tf_op jit(solution)/shard_map/ppermute | solution.py:681
  136.3 14.0 %collective-permute-start.12 = (bf16[96,2048]{1,0:T(8,128)(2,1)S(1)}, bf16[96,2048]{1,0:T(8,128)(2,1)S(1)}, u32[]{:S(2)}, u32[]{:S(2)}) collective-permute-start(bf16[96,2048]{1,0:T(8,128)(2,1)S(1)} %get-tuple-element.76), channel_id=1, source_target_pairs={{0,1},{1,2},{2,3},{3,0},{4,5},{5,6},{6,7},{7,4},{8,9},{9,10},{10,1... | collective-permute-start | bytes 1179656 | tf_op jit(solution)/shard_map/ppermute | solution.py:681
  138.3 27.3 %collective-permute-start.13 = (bf16[96,2048]{1,0:T(8,128)(2,1)S(1)}, bf16[96,2048]{1,0:T(8,128)(2,1)S(1)}, u32[]{:S(2)}, u32[]{:S(2)}) collective-permute-start(bf16[96,2048]{1,0:T(8,128)(2,1)S(1)} %get-tuple-element.76), channel_id=1, source_target_pairs={{0,2},{1,3},{2,0},{3,1},{4,6},{5,7},{6,4},{7,5},{8,10},{9,11},{10,... | collective-permute-start | bytes 1179656 | tf_op jit(solution)/shard_map/ppermute | solution.py:681
  140.4 25.3 %collective-permute-start.14 = (bf16[96,2048]{1,0:T(8,128)(2,1)S(1)}, bf16[96,2048]{1,0:T(8,128)(2,1)S(1)}, u32[]{:S(2)}, u32[]{:S(2)}) collective-permute-start(bf16[96,2048]{1,0:T(8,128)(2,1)S(1)} %get-tuple-element.76), channel_id=1, source_target_pairs={{0,3},{1,0},{2,1},{3,2},{4,7},{5,4},{6,5},{7,6},{8,11},{9,8},{10,9... | collective-permute-start | bytes 1179656 | tf_op jit(solution)/shard_map/ppermute | solution.py:681
  197.7 14.2 %collective-permute-start.17 = (bf16[96,2048]{1,0:T(8,128)(2,1)}, bf16[96,2048]{1,0:T(8,128)(2,1)}, u32[]{:S(2)}, u32[]{:S(2)}) collective-permute-start(bf16[96,2048]{1,0:T(8,128)(2,1)} %get-tuple-element.156), channel_id=1, source_target_pairs={{0,1},{1,2},{2,3},{3,0},{4,5},{5,6},{6,7},{7,4},{8,9},{9,10},{10,1... | collective-permute-start | bytes 1179656 | tf_op jit(solution)/shard_map/ppermute | solution.py:681
  199.2 28.9 %collective-permute-start.16 = (bf16[96,2048]{1,0:T(8,128)(2,1)S(1)}, bf16[96,2048]{1,0:T(8,128)(2,1)}, u32[]{:S(2)}, u32[]{:S(2)}) collective-permute-start(bf16[96,2048]{1,0:T(8,128)(2,1)S(1)} %get-tuple-element.157), channel_id=1, source_target_pairs={{0,2},{1,3},{2,0},{3,1},{4,6},{5,7},{6,4},{7,5},{8,10},{9,11},{10,... | collective-permute-start | bytes 1179656 | tf_op jit(solution)/shard_map/ppermute | solution.py:681
  201.6 26.5 %collective-permute-start.15 = (bf16[96,2048]{1,0:T(8,128)(2,1)S(1)}, bf16[96,2048]{1,0:T(8,128)(2,1)}, u32[]{:S(2)}, u32[]{:S(2)}) collective-permute-start(bf16[96,2048]{1,0:T(8,128)(2,1)S(1)} %get-tuple-element.155), channel_id=1, source_target_pairs={{0,3},{1,0},{2,1},{3,2},{4,7},{5,4},{6,5},{7,6},{8,11},{9,8},{10,9... | collective-permute-start | bytes 1179656 | tf_op jit(solution)/shard_map/ppermute | solution.py:681
  232.7 19.5 %collective-permute-start.20 = (bf16[96,2048]{1,0:T(8,128)(2,1)S(1)}, bf16[96,2048]{1,0:T(8,128)(2,1)S(1)}, u32[]{:S(2)}, u32[]{:S(2)}) collective-permute-start(bf16[96,2048]{1,0:T(8,128)(2,1)S(1)} %get-tuple-element.139), channel_id=1, source_target_pairs={{0,3},{1,0},{2,1},{3,2},{4,7},{5,4},{6,5},{7,6},{8,11},{9,8},{10,9... | collective-permute-start | bytes 1179656 | tf_op jit(solution)/shard_map/ppermute | solution.py:681
  242.5 34.8 %collective-permute-start.19 = (bf16[96,2048]{1,0:T(8,128)(2,1)S(1)}, bf16[96,2048]{1,0:T(8,128)(2,1)S(1)}, u32[]{:S(2)}, u32[]{:S(2)}) collective-permute-start(bf16[96,2048]{1,0:T(8,128)(2,1)S(1)} %get-tuple-element.139), channel_id=1, source_target_pairs={{0,2},{1,3},{2,0},{3,1},{4,6},{5,7},{6,4},{7,5},{8,10},{9,11},{10,... | collective-permute-start | bytes 1179656 | tf_op jit(solution)/shard_map/ppermute | solution.py:681
  243.1 34.3 %collective-permute-start.18 = (bf16[96,2048]{1,0:T(8,128)(2,1)S(1)}, bf16[96,2048]{1,0:T(8,128)(2,1)S(1)}, u32[]{:S(2)}, u32[]{:S(2)}) collective-permute-start(bf16[96,2048]{1,0:T(8,128)(2,1)S(1)} %get-tuple-element.139), channel_id=1, source_target_pairs={{0,1},{1,2},{2,3},{3,0},{4,5},{5,6},{6,7},{7,4},{8,9},{9,10},{10,1... | collective-permute-start | bytes 1179656 | tf_op jit(solution)/shard_map/ppermute | solution.py:681
  296.4 18.7 %collective-permute-start.24 = (bf16[1408,1024]{1,0:T(8,128)(2,1)}, bf16[1408,1024]{1,0:T(8,128)(2,1)}, u32[]{:S(2)}, u32[]{:S(2)}) collective-permute-start(bf16[1408,1024]{1,0:T(8,128)(2,1)} %wide_gradient.4), channel_id=1, source_target_pairs={{0,4},{4,0},{8,12},{12,8},{16,20},{20,16},{24,28},{28,24},{1,5},{5... | collective-permute-start | bytes 8650760 | tf_op jit(solution)/shard_map/ppermute | solution.py:686
  296.4 22.5 %collective-permute-start.21 = (bf16[96,2048]{1,0:T(8,128)(2,1)}, bf16[96,2048]{1,0:T(8,128)(2,1)S(1)}, u32[]{:S(2)}, u32[]{:S(2)}) collective-permute-start(bf16[96,2048]{1,0:T(8,128)(2,1)} %get-tuple-element.78), channel_id=1, source_target_pairs={{0,3},{1,0},{2,1},{3,2},{4,7},{5,4},{6,5},{7,6},{8,11},{9,8},{10,9... | collective-permute-start | bytes 1179656 | tf_op jit(solution)/shard_map/ppermute | solution.py:681
  296.4 36.4 %collective-permute-start.22 = (bf16[96,2048]{1,0:T(8,128)(2,1)}, bf16[96,2048]{1,0:T(8,128)(2,1)}, u32[]{:S(2)}, u32[]{:S(2)}) collective-permute-start(bf16[96,2048]{1,0:T(8,128)(2,1)} %get-tuple-element.79), channel_id=1, source_target_pairs={{0,2},{1,3},{2,0},{3,1},{4,6},{5,7},{6,4},{7,5},{8,10},{9,11},{10,... | collective-permute-start | bytes 1179656 | tf_op jit(solution)/shard_map/ppermute | solution.py:681
  297.5 35.3 %collective-permute-start.23 = (bf16[96,2048]{1,0:T(8,128)(2,1)}, bf16[96,2048]{1,0:T(8,128)(2,1)}, u32[]{:S(2)}, u32[]{:S(2)}) collective-permute-start(bf16[96,2048]{1,0:T(8,128)(2,1)} %get-tuple-element.80), channel_id=1, source_target_pairs={{0,1},{1,2},{2,3},{3,0},{4,5},{5,6},{6,7},{7,4},{8,9},{9,10},{10,1... | collective-permute-start | bytes 1179656 | tf_op jit(solution)/shard_map/ppermute | solution.py:681
  332.9 154.6 %reduce-scatter.5.cloned.1.call-start = ((), (), s32[]{:S(2)}) async-start(), calls=%async_computation.7 | async-start | bytes 2359296 | tf_op jit(solution)/shard_map/reduce_scatter | solution.py:973
  332.9 19.3 %collective-permute-start.28 = (bf16[1408,512]{1,0:T(8,128)(2,1)}, bf16[1408,512]{1,0:T(8,128)(2,1)S(1)}, u32[]{:S(2)}, u32[]{:S(2)}) collective-permute-start(bf16[1408,512]{1,0:T(8,128)(2,1)} %copy-done.11), channel_id=1, source_target_pairs={{0,8},{4,20},{8,0},{12,28},{16,24},{20,4},{24,16},{28,12},{1,9},{5... | collective-permute-start | bytes 4325384 | tf_op jit(solution)/shard_map/ppermute | solution.py:751
  338.7 17.8 %collective-permute-start.25 = (bf16[96,2176]{1,0:T(8,128)(2,1)S(1)}, bf16[96,2176]{1,0:T(8,128)(2,1)S(1)}, u32[]{:S(2)}, u32[]{:S(2)}) collective-permute-start(bf16[96,2176]{1,0:T(8,128)(2,1)S(1)} %get-tuple-element.89), channel_id=1, source_target_pairs={{0,1},{1,2},{2,3},{3,0},{4,5},{5,6},{6,7},{7,4},{8,9},{9,10},{10,1... | collective-permute-start | bytes 1253384 | tf_op jit(solution)/shard_map/ppermute | solution.py:681
  338.7 30.1 %collective-permute-start.26 = (bf16[96,2176]{1,0:T(8,128)(2,1)S(1)}, bf16[96,2176]{1,0:T(8,128)(2,1)S(1)}, u32[]{:S(2)}, u32[]{:S(2)}) collective-permute-start(bf16[96,2176]{1,0:T(8,128)(2,1)S(1)} %get-tuple-element.89), channel_id=1, source_target_pairs={{0,2},{1,3},{2,0},{3,1},{4,6},{5,7},{6,4},{7,5},{8,10},{9,11},{10,... | collective-permute-start | bytes 1253384 | tf_op jit(solution)/shard_map/ppermute | solution.py:681
  340.6 28.2 %collective-permute-start.27 = (bf16[96,2176]{1,0:T(8,128)(2,1)S(1)}, bf16[96,2176]{1,0:T(8,128)(2,1)S(1)}, u32[]{:S(2)}, u32[]{:S(2)}) collective-permute-start(bf16[96,2176]{1,0:T(8,128)(2,1)S(1)} %get-tuple-element.89), channel_id=1, source_target_pairs={{0,3},{1,0},{2,1},{3,2},{4,7},{5,4},{6,5},{7,6},{8,11},{9,8},{10,9... | collective-permute-start | bytes 1253384 | tf_op jit(solution)/shard_map/ppermute | solution.py:681
  390.8 30.7 %collective-permute-start.30 = (bf16[1408,256]{1,0:T(8,128)(2,1)}, bf16[1408,256]{1,0:T(8,128)(2,1)}, u32[]{:S(2)}, u32[]{:S(2)}) collective-permute-start(bf16[1408,256]{1,0:T(8,128)(2,1)} %copy-done.16), channel_id=1, source_target_pairs={{0,16},{4,12},{8,24},{12,4},{16,0},{20,28},{24,8},{28,20},{1,17},{... | collective-permute-start | bytes 2162696 | tf_op jit(solution)/shard_map/ppermute | solution.py:751
  402.9 38.4 %collective-permute-start.31 = (bf16[512,2176]{1,0:T(8,128)(2,1)}, bf16[512,2176]{1,0:T(8,128)(2,1)}, u32[]{:S(2)}, u32[]{:S(2)}) collective-permute-start(bf16[512,2176]{1,0:T(8,128)(2,1)} %mixer_gradient.4), channel_id=1, source_target_pairs={{0,8},{4,20},{8,0},{12,28},{16,24},{20,4},{24,16},{28,12},{1,9},{5... | collective-permute-start | bytes 6684680 | tf_op jit(solution)/shard_map/ppermute | solution.py:751
  409.2 75.7 %all-to-all-start = ((bf16[4,96,2048]{2,1,0:T(8,128)(2,1)}), bf16[4,96,2048]{2,1,0:T(8,128)(2,1)}, u32[]{:S(2)}, u32[]{:S(2)}) async-start(bf16[4,96,2048]{2,1,0:T(8,128)(2,1)} %bitcast.69), calls=%async_computation | async-start | bytes 3145728 | tf_op jit(solution)/shard_map/all_to_all | solution.py:957
  444.8 21.4 %collective-permute-start.32 = (bf16[256,2176]{1,0:T(8,128)(2,1)}, bf16[256,2176]{1,0:T(8,128)(2,1)}, u32[]{:S(2)}, u32[]{:S(2)}) collective-permute-start(bf16[256,2176]{1,0:T(8,128)(2,1)} %mixer_gradient.5), channel_id=1, source_target_pairs={{0,16},{4,12},{8,24},{12,4},{16,0},{20,28},{24,8},{28,20},{1,17},{... | collective-permute-start | bytes 3342344 | tf_op jit(solution)/shard_map/ppermute | solution.py:751
  474.9 15.7 %collective-permute-start.35 = (f32[4,256]{1,0:T(4,128)}, f32[4,256]{1,0:T(4,128)}, u32[]{:S(2)}, u32[]{:S(2)}) collective-permute-start(f32[4,256]{1,0:T(4,128)} %pad_maximum_fusion.11), channel_id=1, source_target_pairs={{0,3},{1,0},{2,1},{3,2},{4,7},{5,4},{6,5},{7,6},{8,11},{9,8},{10,9... | collective-permute-start | bytes 12296 | tf_op jit(solution)/shard_map/ppermute | solution.py:681
  (78 other events, 896.8 us)
Sparse Core Ops, SparseCore 0:
  10.5 62.4 all-gather.3
  75.5 67.6 all-gather.5
  145.7 44.3 all-gather.7
  333.0 92.3 reduce-scatter.2
  428.5 48.6 reduce-scatter.4

commit v5 on v4

--- a/solution.py
+++ b/solution.py
@@ -14,7 +14,7 @@
 BLOCK = 32
 CHUNK = 128
 LEVELS = 7
-TOGETHER = 1
+TOGETHER = 2
 VMEM_LIMIT = 16 * 1024 * 1024
 
 EPS = 1e-06

time: 509 us -> 510 us (level)
  no operation moved by 1% of the time
where the time goes in v5:
time: 510 us; the launch traced here: 501 us
  waiting for transfers between devices  215 us (42%)
  starting transfers between devices  76.4 us (15%)
  Pallas kernels  75.4 us (15%)
  other arithmetic  44 us (9%)
  matrix products  41.4 us (8%)
  local copies, waits for them, and re-layouts  30.7 us (6%)
  between operations  18.3 us (4%)
    ppermute x24, waiting for transfers between devices, turn(): return lax.ppermute(v, axis, [(i, (i + step) % n) for i in range(n)])  144 us
    ppermute x24, starting transfers between devices, turn(): return lax.ppermute(v, axis, [(i, (i + step) % n) for i in range(n)])  50.2 us
    ppermute x6, waiting for transfers between devices, cross_swap(): lax.ppermute(v, 'dp', [(i, i ^ (odd if i & 1 else even)[stage]) for i in...  45.7 us
    all_gather x3, waiting for transfers between devices, gather_weight(): return lax.all_gather(w.astype(BF), 'dp', axis=dim, tiled=True)  24.2 us
    pallas_call x2, Pallas kernels, mixer_call(): pl.pallas_call(functools.partial(kernel, ranks), grid=(heads // together,...  19.5 us
    unnamed x142, local copies, waits for them, and re-layouts  18.1 us
    dot_general x4, matrix products, dot_nt(): lax.dot_general(a, b, (((1,), (1,)), ((), ())), preferred_element_type=F32)  15.9 us
    add x4, other arithmetic, apply_update(): average_new = AVERAGE_RATE * average + (1.0 - AVERAGE_RATE) * master_new  13.7 us
  transfers between devices with their start and end apart: 42, of which 19 were waited for; matrix products, arithmetic and copies ran while one was open for 14% of the time, Pallas kernels for 14%

profile of v5, /device:TPU:0, one launch (start us, length us, event | category | flops | bytes accessed | tf_op | source)
XLA Modules:
  0.0 500.8 jit_solution(541469312530709430)
XLA Ops:
  12.1 4.7 collective-permute-start.2
  23.6 5.9 %collective-permute-done.6 = bf16[512,256]{1,0:T(8,128)(2,1)S(1)} collective-permute-done((bf16[512,256]{1,0:T(8,128)(2,1)S(1)}, bf16[512,256]{1,0:T(8,128)(2,1)S(1)}, u32[]{:S(2)}, u32[]{:S(2)}) %collective-permute-start.6) | collective-permute-done | bytes 262176 | tf_op jit(solution)/shard_map/ppermute | solution.py:751
  34.5 6.3 %collective-permute-done.7 = bf16[512,512]{1,0:T(8,128)(2,1)S(1)} collective-permute-done((bf16[512,512]{1,0:T(8,128)(2,1)S(1)}, bf16[512,512]{1,0:T(8,128)(2,1)S(1)}, u32[]{:S(2)}, u32[]{:S(2)}) %collective-permute-start.7) | collective-permute-done | bytes 524320 | tf_op jit(solution)/shard_map/ppermute | solution.py:751
  42.9 8.0 %collective-permute-done.1 = bf16[96,2048]{1,0:T(8,128)(2,1)S(1)} collective-permute-done((bf16[96,2048]{1,0:T(8,128)(2,1)S(1)}, bf16[96,2048]{1,0:T(8,128)(2,1)S(1)}, u32[]{:S(2)}, u32[]{:S(2)}) %collective-permute-start.1) | collective-permute-done | bytes 393248 | tf_op jit(solution)/shard_map/ppermute | solution.py:681
  61.6 11.4 %all-gather.4.cloned.1.call-done.weight_ref = bf16[4,2048,512]{2,1,0:T(8,128)(2,1)} async-done(((bf16[4,256,512]{2,1,0:T(8,128)(2,1)}), bf16[4,2048,512]{2,1,0:T(8,128)(2,1)}) %all-gather.4.cloned.1.call-update) | async-done | bytes 8388624 | tf_op jit(solution)/shard_map/all_gather | solution.py:722
  73.0 5.9 %convolution_bitcast_fusion.1.z_ref = f32[4,384,512]{2,1,0:T(8,128)S(1)} fusion(bf16[4,2048,512]{2,1,0:T(8,128)(2,1)} %all-gather.4.cloned.1.call-done.weight_ref, bf16[384,2048]{1,0:T(8,128)(2,1)S(1)} %fusion.4.in_ref), kind=kOutput, calls=%fused_computation.25 | convolution fusion | flops 3221225472 | bytes 13107200 | tf_op jit(solution)/shard_map/td,jde->jte/dot_general | solution.py:868
  78.9 9.2 %mixer_forward.1 = (f32[384,512]{1,0:T(8,128)S(1)}, bf16[384,512]{1,0:T(8,128)(2,1)S(1)}, f32[384,1]{1,0:T(8,128)S(1)}, f32[1,4,3,128,128]{4,3,2,1,0:T(8,128)S(1)}, bf16[1,4,3,128,128]{4,3,2,1,0:T(8,128)(2,1)S(1)}) custom-call(s32[2]{0:T(128)S(1)} %pad_add_fusion.scalar_ref, f32[4,384,512]{2,1,0:T(8,128)S(1)} %convolution_bitcast_fusion.1.z_ref, ...), custom_call_target="tpu_custom_call" | custom-call | tf_op jit(solution)/shard_map/mixer_forward/pallas_call | solution.py:281
  101.3 6.3 %collective-permute-done.9.refs_0_ = bf16[96,2176]{1,0:T(8,128)(2,1)} collective-permute-done((bf16[96,2176]{1,0:T(8,128)(2,1)}, bf16[96,2176]{1,0:T(8,128)(2,1)}, u32[]{:S(2)}, u32[]{:S(2)}) %collective-permute-start.9) | collective-permute-done | bytes 417824 | tf_op jit(solution)/shard_map/ppermute | solution.py:681
  107.6 26.2 %collective-permute-done.10.refs_1_ = bf16[96,2176]{1,0:T(8,128)(2,1)} collective-permute-done((bf16[96,2176]{1,0:T(8,128)(2,1)}, bf16[96,2176]{1,0:T(8,128)(2,1)}, u32[]{:S(2)}, u32[]{:S(2)}) %collective-permute-start.10) | collective-permute-done | bytes 417824 | tf_op jit(solution)/shard_map/ppermute | solution.py:681
  142.9 7.0 %collective-permute-done.12 = bf16[96,2048]{1,0:T(8,128)(2,1)S(1)} collective-permute-done((bf16[96,2048]{1,0:T(8,128)(2,1)S(1)}, bf16[96,2048]{1,0:T(8,128)(2,1)S(1)}, u32[]{:S(2)}, u32[]{:S(2)}) %collective-permute-start.12) | collective-permute-done | bytes 393248 | tf_op jit(solution)/shard_map/ppermute | solution.py:681
  150.0 15.2 %collective-permute-done.13 = bf16[96,2048]{1,0:T(8,128)(2,1)S(1)} collective-permute-done((bf16[96,2048]{1,0:T(8,128)(2,1)S(1)}, bf16[96,2048]{1,0:T(8,128)(2,1)S(1)}, u32[]{:S(2)}, u32[]{:S(2)}) %collective-permute-start.13) | collective-permute-done | bytes 393248 | tf_op jit(solution)/shard_map/ppermute | solution.py:681
  165.3 8.4 %convolution_bitcast_fusion = f32[2,384,1408]{2,1,0:T(8,128)S(1)} fusion(bf16[2,2048,1408]{2,1,0:T(8,128)(2,1)} %all-gather.6.cloned.1.call-done, bf16[384,2048]{1,0:T(8,128)(2,1)S(1)} %constant_dynamic-update-slice_fusion.rows_ref.right_ref), kind=kOutput, calls=%fused_computation.6 | convolution fusion | flops 4429185024 | bytes 17432576 | tf_op jit(solution)/shard_map/td,jdf->jtf/dot_general | solution.py:886
  177.3 12.7 %all-gather.8.cloned.1.call-done = bf16[1408,2048]{1,0:T(8,128)(2,1)} async-done(((bf16[1408,256]{1,0:T(8,128)(2,1)}), bf16[1408,2048]{1,0:T(8,128)(2,1)}) %all-gather.8.cloned.1.call-update) | async-done | bytes 5767184 | tf_op jit(solution)/shard_map/all_gather | solution.py:722
  190.1 5.6 %convolution_convert_fusion.1 = bf16[384,2048]{1,0:T(8,128)(2,1)S(1)} fusion(bf16[384,1408]{1,0:T(8,128)(2,1)} %multiply_convert_fusion.2.left_ref, bf16[1408,2048]{1,0:T(8,128)(2,1)} %all-gather.8.cloned.1.call-done), kind=kOutput, calls=%fused_computation.16 | convolution fusion | flops 2215378944 | bytes 8421376 | tf_op jit(solution)/shard_map/dot_general | solution.py:44
  211.9 16.2 %collective-permute-done.16 = bf16[96,2048]{1,0:T(8,128)(2,1)} collective-permute-done((bf16[96,2048]{1,0:T(8,128)(2,1)S(1)}, bf16[96,2048]{1,0:T(8,128)(2,1)}, u32[]{:S(2)}, u32[]{:S(2)}) %collective-permute-start.16) | collective-permute-done | bytes 393248 | tf_op jit(solution)/shard_map/ppermute | solution.py:681
  232.7 9.8 %collective-permute-start.20 = (bf16[96,2048]{1,0:T(8,128)(2,1)S(1)}, bf16[96,2048]{1,0:T(8,128)(2,1)S(1)}, u32[]{:S(2)}, u32[]{:S(2)}) collective-permute-start(bf16[96,2048]{1,0:T(8,128)(2,1)S(1)} %get-tuple-element.139), channel_id=1, source_target_pairs={{0,3},{1,0},{2,1},{3,2},{4,7},{5,4},{6,5},{7,6},{8,11},{9,8},{10,9... | collective-permute-start | bytes 1179656 | tf_op jit(solution)/shard_map/ppermute | solution.py:681
  243.2 9.0 %collective-permute-done.20 = bf16[96,2048]{1,0:T(8,128)(2,1)S(1)} collective-permute-done((bf16[96,2048]{1,0:T(8,128)(2,1)S(1)}, bf16[96,2048]{1,0:T(8,128)(2,1)S(1)}, u32[]{:S(2)}, u32[]{:S(2)}) %collective-permute-start.20) | collective-permute-done | bytes 393248 | tf_op jit(solution)/shard_map/ppermute | solution.py:681
  252.1 25.2 %collective-permute-done.19 = bf16[96,2048]{1,0:T(8,128)(2,1)S(1)} collective-permute-done((bf16[96,2048]{1,0:T(8,128)(2,1)S(1)}, bf16[96,2048]{1,0:T(8,128)(2,1)S(1)}, u32[]{:S(2)}, u32[]{:S(2)}) %collective-permute-start.19) | collective-permute-done | bytes 393248 | tf_op jit(solution)/shard_map/ppermute | solution.py:681
  277.4 5.7 %multiply_convert_fusion.1 = (bf16[384,1408]{1,0:T(8,128)(2,1)S(1)}, bf16[384,1408]{1,0:T(8,128)(2,1)S(1)}) fusion(f32[2,384,1408]{2,1,0:T(8,128)S(1)} %copy-done.36, bf16[1408,2048]{1,0:T(8,128)(2,1)} %all-gather.8.cloned.1.call-done, bf16[96,2048]{1,0:T(8,128)(2,1)S(1)} %collective-permute-done.20, bf16[96,2048]{1,0:T(8,128)(2,1)S(1)} %collective-permute-done.19, ...), kind=kOutput, calls=%fused_computation.21 | convolution fusion | flops 2227912704 | bytes 13828096 | tf_op jit(solution)/shard_map/dot_general | solution.py:48
  299.5 8.9 %pair_gradient.1 = bf16[2,2048,1408]{2,1,0:T(8,128)(2,1)S(1)} custom-call(bf16[384,2048]{1,0:T(8,128)(2,1)S(1)} %copy-done.4, bf16[384,1408]{1,0:T(8,128)(2,1)S(1)} %get-tuple-element.143.first_ref, bf16[384,1408]{1,0:T(8,128)(2,1)S(1)} %get-tuple-element.82.second_ref), custom_call_target="tpu_custom_call" | custom-call | tf_op jit(solution)/shard_map/pair_gradient/pallas_call | solution.py:459
  319.0 13.8 %collective-permute-done.22.refs_1_ = bf16[96,2048]{1,0:T(8,128)(2,1)} collective-permute-done((bf16[96,2048]{1,0:T(8,128)(2,1)}, bf16[96,2048]{1,0:T(8,128)(2,1)}, u32[]{:S(2)}, u32[]{:S(2)}) %collective-permute-start.22) | collective-permute-done | bytes 393248 | tf_op jit(solution)/shard_map/ppermute | solution.py:681
  343.7 8.5 %collective-permute-done.28.refs_1_ = bf16[1408,512]{1,0:T(8,128)(2,1)S(1)} collective-permute-done((bf16[1408,512]{1,0:T(8,128)(2,1)}, bf16[1408,512]{1,0:T(8,128)(2,1)S(1)}, u32[]{:S(2)}, u32[]{:S(2)}) %collective-permute-start.28) | collective-permute-done | bytes 1441824 | tf_op jit(solution)/shard_map/ppermute | solution.py:751
  356.5 12.3 %collective-permute-done.26 = bf16[96,2176]{1,0:T(8,128)(2,1)S(1)} collective-permute-done((bf16[96,2176]{1,0:T(8,128)(2,1)S(1)}, bf16[96,2176]{1,0:T(8,128)(2,1)S(1)}, u32[]{:S(2)}, u32[]{:S(2)}) %collective-permute-start.26) | collective-permute-done | bytes 417824 | tf_op jit(solution)/shard_map/ppermute | solution.py:681
  369.4 5.0 multiply_convert_fusion.4
  375.8 10.3 %mixer_backward.1.grads_ref = bf16[4,384,512]{2,1,0:T(8,128)(2,1)S(1)} custom-call(s32[2]{0:T(128)S(1)} %copy-done.22, f32[4,384,512]{2,1,0:T(8,128)} %copy-done.2, f32[384,512]{1,0:T(8,128)} %get-tuple-element.146.dout_ref, bf16[384,512]{1,0:T(8,128)(2,1)} %get-tuple-element.145.gate_ref, s32[1,1,384]{2,1,0:T(1,128)} %bitcast.65, s32[1,384,1]{2,1,0:T(8,128)} %copy-done.10, ...), custom_call_target="tpu_custom_call" | custom-call | tf_op jit(solution)/shard_map/mixer_backward/pallas_call | solution.py:281
  392.0 6.4 %project_back.1 = bf16[384,2048]{1,0:T(8,128)(2,1)S(1)} custom-call(bf16[4,384,512]{2,1,0:T(8,128)(2,1)S(1)} %mixer_backward.1.grads_ref, bf16[4,2048,512]{2,1,0:T(8,128)(2,1)} %all-gather.4.cloned.1.call-done.weight_ref), custom_call_target="tpu_custom_call" | custom-call | bytes 100000000 | tf_op jit(solution)/shard_map/project_back/pallas_call | solution.py:608
  408.8 11.6 %all-to-all-start = ((bf16[4,96,2048]{2,1,0:T(8,128)(2,1)}), bf16[4,96,2048]{2,1,0:T(8,128)(2,1)}, u32[]{:S(2)}, u32[]{:S(2)}) async-start(bf16[4,96,2048]{2,1,0:T(8,128)(2,1)} %bitcast.69), calls=%async_computation | async-start | bytes 3145728 | tf_op jit(solution)/shard_map/all_to_all | solution.py:957
  427.3 13.8 %collective-permute-done.31.refs_1_.refs_4_ = bf16[512,2176]{1,0:T(8,128)(2,1)} collective-permute-done((bf16[512,2176]{1,0:T(8,128)(2,1)}, bf16[512,2176]{1,0:T(8,128)(2,1)}, u32[]{:S(2)}, u32[]{:S(2)}) %collective-permute-start.31) | collective-permute-done | bytes 2228256 | tf_op jit(solution)/shard_map/ppermute | solution.py:751
  446.0 8.8 %add_multiply_fusion = (f32[2,256,1408]{2,1,0:T(8,128)}, f32[2,256,1408]{2,1,0:T(8,128)}, f32[2,256,1408]{2,1,0:T(8,128)}, f32[2,256,1408]{2,1,0:T(8,128)}) fusion(f32[2,256,1408]{2,1,0:T(8,128)} %param.38, f32[2,256,1408]{2,1,0:T(8,128)} %param.36, f32[2,256,1408]{2,1,0:T(8,128)} %param.37, bf16[2,256,1408]{2,1,0:T(8,128)(2,1)} %reduce-scatter.3.cloned.1.call-done), kind=kLoop, calls=%fused_computation.13 | loop fusion | flops 6488064 | bytes 21626880 | tf_op jit(solution)/shard_map/add | solution.py:717
  454.8 11.2 %collective-permute-done.32.refs_2_.refs_5_ = bf16[256,2176]{1,0:T(8,128)(2,1)} collective-permute-done((bf16[256,2176]{1,0:T(8,128)(2,1)}, bf16[256,2176]{1,0:T(8,128)(2,1)}, u32[]{:S(2)}, u32[]{:S(2)}) %collective-permute-start.32) | collective-permute-done | bytes 1114144 | tf_op jit(solution)/shard_map/ppermute | solution.py:751
  466.0 8.1 %mixer_in_update.1 = (f32[4,256,512]{2,1,0:T(8,128)}, f32[4,256,512]{2,1,0:T(8,128)}, f32[4,256,512]{2,1,0:T(8,128)}, f32[4,256,512]{2,1,0:T(8,128)}, f32[8,256]{1,0:T(8,128)S(1)}, /*index=5*/f32[8,256]{1,0:T(8,128)S(1)}) custom-call(bf16[384,2048]{1,0:T(8,128)(2,1)S(1)} %take_blocks.3.rows_ref, bf16[4,384,512]{2,1,0:T(8,128)(2,1)S(1)} %mixer_backward.1.grads_ref, ...), custom_call_target="tpu_custom_call" | custom-call | tf_op jit(solution)/shard_map/mixer_in_update/pallas_call | solution.py:418
  474.7 9.3 %collective-permute-start.35 = (f32[4,256]{1,0:T(4,128)}, f32[4,256]{1,0:T(4,128)}, u32[]{:S(2)}, u32[]{:S(2)}) collective-permute-start(f32[4,256]{1,0:T(4,128)} %pad_maximum_fusion.11), channel_id=1, source_target_pairs={{0,3},{1,0},{2,1},{3,2},{4,7},{5,4},{6,5},{7,6},{8,11},{9,8},{10,9... | collective-permute-start | bytes 12296 | tf_op jit(solution)/shard_map/ppermute | solution.py:681
  (303 shorter events, 155.6 us)
Async XLA Ops:
  7.2 65.8 %all-gather.4.cloned.1.call-start = ((), (), s32[]{:S(2)}) async-start(), calls=%async_computation.3 | async-start | bytes 9437184 | tf_op jit(solution)/shard_map/all_gather | solution.py:722
  10.1 155.2 %all-gather.6.cloned.1.call-start = ((), (), s32[]{:S(2)}) async-start(), calls=%async_computation.4 | async-start | bytes 12976128 | tf_op jit(solution)/shard_map/all_gather | solution.py:722
  11.5 178.6 %all-gather.8.cloned.1.call-start = ((), (), s32[]{:S(2)}) async-start(), calls=%async_computation.5 | async-start | bytes 6488064 | tf_op jit(solution)/shard_map/all_gather | solution.py:722
  12.1 30.8 %collective-permute-start.2 = (bf16[96,2048]{1,0:T(8,128)(2,1)S(1)}, bf16[96,2048]{1,0:T(8,128)(2,1)S(1)}, u32[]{:S(2)}, u32[]{:S(2)}) collective-permute-start(bf16[96,2048]{1,0:T(8,128)(2,1)S(1)} %copy-done.27), channel_id=1, source_target_pairs={{0,3},{1,0},{2,1},{3,2},{4,7},{5,4},{6,5},{7,6},{8,11},{9,8},{10,9... | collective-permute-start | bytes 1179656 | tf_op jit(solution)/shard_map/ppermute | solution.py:681
  16.8 34.1 %collective-permute-start.1 = (bf16[96,2048]{1,0:T(8,128)(2,1)S(1)}, bf16[96,2048]{1,0:T(8,128)(2,1)S(1)}, u32[]{:S(2)}, u32[]{:S(2)}) collective-permute-start(bf16[96,2048]{1,0:T(8,128)(2,1)S(1)} %copy-done.27), channel_id=1, source_target_pairs={{0,2},{1,3},{2,0},{3,1},{4,6},{5,7},{6,4},{7,5},{8,10},{9,11},{10,... | collective-permute-start | bytes 1179656 | tf_op jit(solution)/shard_map/ppermute | solution.py:681
  16.8 34.1 %collective-permute-start = (bf16[96,2048]{1,0:T(8,128)(2,1)S(1)}, bf16[96,2048]{1,0:T(8,128)(2,1)}, u32[]{:S(2)}, u32[]{:S(2)}) collective-permute-start(bf16[96,2048]{1,0:T(8,128)(2,1)S(1)} %copy-done.27), channel_id=1, source_target_pairs={{0,1},{1,2},{2,3},{3,0},{4,5},{5,6},{6,7},{7,4},{8,9},{9,10},{10,1... | collective-permute-start | bytes 1179656 | tf_op jit(solution)/shard_map/ppermute | solution.py:681
  21.4 424.6 %reduce-scatter.3.cloned.1.call-start = ((), (), s32[]{:S(2)}) async-start(), calls=%async_computation.6 | async-start | bytes 12976128 | tf_op jit(solution)/shard_map/reduce_scatter | solution.py:966
  98.1 35.7 %collective-permute-start.10 = (bf16[96,2176]{1,0:T(8,128)(2,1)}, bf16[96,2176]{1,0:T(8,128)(2,1)}, u32[]{:S(2)}, u32[]{:S(2)}) collective-permute-start(bf16[96,2176]{1,0:T(8,128)(2,1)} %pad_maximum_fusion.6), channel_id=1, source_target_pairs={{0,2},{1,3},{2,0},{3,1},{4,6},{5,7},{6,4},{7,5},{8,10},{9,11},{10,... | collective-permute-start | bytes 1253384 | tf_op jit(solution)/shard_map/ppermute | solution.py:681
  99.0 34.8 %collective-permute-start.11 = (bf16[96,2176]{1,0:T(8,128)(2,1)}, bf16[96,2176]{1,0:T(8,128)(2,1)}, u32[]{:S(2)}, u32[]{:S(2)}) collective-permute-start(bf16[96,2176]{1,0:T(8,128)(2,1)} %pad_maximum_fusion.7), channel_id=1, source_target_pairs={{0,1},{1,2},{2,3},{3,0},{4,5},{5,6},{6,7},{7,4},{8,9},{9,10},{10,1... | collective-permute-start | bytes 1253384 | tf_op jit(solution)/shard_map/ppermute | solution.py:681
  135.9 14.0 %collective-permute-start.12 = (bf16[96,2048]{1,0:T(8,128)(2,1)S(1)}, bf16[96,2048]{1,0:T(8,128)(2,1)S(1)}, u32[]{:S(2)}, u32[]{:S(2)}) collective-permute-start(bf16[96,2048]{1,0:T(8,128)(2,1)S(1)} %get-tuple-element.76), channel_id=1, source_target_pairs={{0,1},{1,2},{2,3},{3,0},{4,5},{5,6},{6,7},{7,4},{8,9},{9,10},{10,1... | collective-permute-start | bytes 1179656 | tf_op jit(solution)/shard_map/ppermute | solution.py:681
  137.9 27.3 %collective-permute-start.13 = (bf16[96,2048]{1,0:T(8,128)(2,1)S(1)}, bf16[96,2048]{1,0:T(8,128)(2,1)S(1)}, u32[]{:S(2)}, u32[]{:S(2)}) collective-permute-start(bf16[96,2048]{1,0:T(8,128)(2,1)S(1)} %get-tuple-element.76), channel_id=1, source_target_pairs={{0,2},{1,3},{2,0},{3,1},{4,6},{5,7},{6,4},{7,5},{8,10},{9,11},{10,... | collective-permute-start | bytes 1179656 | tf_op jit(solution)/shard_map/ppermute | solution.py:681
  139.7 25.5 %collective-permute-start.14 = (bf16[96,2048]{1,0:T(8,128)(2,1)S(1)}, bf16[96,2048]{1,0:T(8,128)(2,1)S(1)}, u32[]{:S(2)}, u32[]{:S(2)}) collective-permute-start(bf16[96,2048]{1,0:T(8,128)(2,1)S(1)} %get-tuple-element.76), channel_id=1, source_target_pairs={{0,3},{1,0},{2,1},{3,2},{4,7},{5,4},{6,5},{7,6},{8,11},{9,8},{10,9... | collective-permute-start | bytes 1179656 | tf_op jit(solution)/shard_map/ppermute | solution.py:681
  197.7 14.2 %collective-permute-start.17 = (bf16[96,2048]{1,0:T(8,128)(2,1)}, bf16[96,2048]{1,0:T(8,128)(2,1)}, u32[]{:S(2)}, u32[]{:S(2)}) collective-permute-start(bf16[96,2048]{1,0:T(8,128)(2,1)} %get-tuple-element.156), channel_id=1, source_target_pairs={{0,1},{1,2},{2,3},{3,0},{4,5},{5,6},{6,7},{7,4},{8,9},{9,10},{10,1... | collective-permute-start | bytes 1179656 | tf_op jit(solution)/shard_map/ppermute | solution.py:681
  199.2 28.9 %collective-permute-start.16 = (bf16[96,2048]{1,0:T(8,128)(2,1)S(1)}, bf16[96,2048]{1,0:T(8,128)(2,1)}, u32[]{:S(2)}, u32[]{:S(2)}) collective-permute-start(bf16[96,2048]{1,0:T(8,128)(2,1)S(1)} %get-tuple-element.157), channel_id=1, source_target_pairs={{0,2},{1,3},{2,0},{3,1},{4,6},{5,7},{6,4},{7,5},{8,10},{9,11},{10,... | collective-permute-start | bytes 1179656 | tf_op jit(solution)/shard_map/ppermute | solution.py:681
  201.6 26.5 %collective-permute-start.15 = (bf16[96,2048]{1,0:T(8,128)(2,1)S(1)}, bf16[96,2048]{1,0:T(8,128)(2,1)}, u32[]{:S(2)}, u32[]{:S(2)}) collective-permute-start(bf16[96,2048]{1,0:T(8,128)(2,1)S(1)} %get-tuple-element.155), channel_id=1, source_target_pairs={{0,3},{1,0},{2,1},{3,2},{4,7},{5,4},{6,5},{7,6},{8,11},{9,8},{10,9... | collective-permute-start | bytes 1179656 | tf_op jit(solution)/shard_map/ppermute | solution.py:681
  232.7 19.5 %collective-permute-start.20 = (bf16[96,2048]{1,0:T(8,128)(2,1)S(1)}, bf16[96,2048]{1,0:T(8,128)(2,1)S(1)}, u32[]{:S(2)}, u32[]{:S(2)}) collective-permute-start(bf16[96,2048]{1,0:T(8,128)(2,1)S(1)} %get-tuple-element.139), channel_id=1, source_target_pairs={{0,3},{1,0},{2,1},{3,2},{4,7},{5,4},{6,5},{7,6},{8,11},{9,8},{10,9... | collective-permute-start | bytes 1179656 | tf_op jit(solution)/shard_map/ppermute | solution.py:681
  242.5 34.8 %collective-permute-start.19 = (bf16[96,2048]{1,0:T(8,128)(2,1)S(1)}, bf16[96,2048]{1,0:T(8,128)(2,1)S(1)}, u32[]{:S(2)}, u32[]{:S(2)}) collective-permute-start(bf16[96,2048]{1,0:T(8,128)(2,1)S(1)} %get-tuple-element.139), channel_id=1, source_target_pairs={{0,2},{1,3},{2,0},{3,1},{4,6},{5,7},{6,4},{7,5},{8,10},{9,11},{10,... | collective-permute-start | bytes 1179656 | tf_op jit(solution)/shard_map/ppermute | solution.py:681
  243.1 34.3 %collective-permute-start.18 = (bf16[96,2048]{1,0:T(8,128)(2,1)S(1)}, bf16[96,2048]{1,0:T(8,128)(2,1)S(1)}, u32[]{:S(2)}, u32[]{:S(2)}) collective-permute-start(bf16[96,2048]{1,0:T(8,128)(2,1)S(1)} %get-tuple-element.139), channel_id=1, source_target_pairs={{0,1},{1,2},{2,3},{3,0},{4,5},{5,6},{6,7},{7,4},{8,9},{9,10},{10,1... | collective-permute-start | bytes 1179656 | tf_op jit(solution)/shard_map/ppermute | solution.py:681
  296.4 18.7 %collective-permute-start.24 = (bf16[1408,1024]{1,0:T(8,128)(2,1)}, bf16[1408,1024]{1,0:T(8,128)(2,1)}, u32[]{:S(2)}, u32[]{:S(2)}) collective-permute-start(bf16[1408,1024]{1,0:T(8,128)(2,1)} %wide_gradient.4), channel_id=1, source_target_pairs={{0,4},{4,0},{8,12},{12,8},{16,20},{20,16},{24,28},{28,24},{1,5},{5... | collective-permute-start | bytes 8650760 | tf_op jit(solution)/shard_map/ppermute | solution.py:686
  296.4 22.6 %collective-permute-start.21 = (bf16[96,2048]{1,0:T(8,128)(2,1)}, bf16[96,2048]{1,0:T(8,128)(2,1)S(1)}, u32[]{:S(2)}, u32[]{:S(2)}) collective-permute-start(bf16[96,2048]{1,0:T(8,128)(2,1)} %get-tuple-element.78), channel_id=1, source_target_pairs={{0,3},{1,0},{2,1},{3,2},{4,7},{5,4},{6,5},{7,6},{8,11},{9,8},{10,9... | collective-permute-start | bytes 1179656 | tf_op jit(solution)/shard_map/ppermute | solution.py:681
  296.4 36.4 %collective-permute-start.22 = (bf16[96,2048]{1,0:T(8,128)(2,1)}, bf16[96,2048]{1,0:T(8,128)(2,1)}, u32[]{:S(2)}, u32[]{:S(2)}) collective-permute-start(bf16[96,2048]{1,0:T(8,128)(2,1)} %get-tuple-element.79), channel_id=1, source_target_pairs={{0,2},{1,3},{2,0},{3,1},{4,6},{5,7},{6,4},{7,5},{8,10},{9,11},{10,... | collective-permute-start | bytes 1179656 | tf_op jit(solution)/shard_map/ppermute | solution.py:681
  297.5 35.3 %collective-permute-start.23 = (bf16[96,2048]{1,0:T(8,128)(2,1)}, bf16[96,2048]{1,0:T(8,128)(2,1)}, u32[]{:S(2)}, u32[]{:S(2)}) collective-permute-start(bf16[96,2048]{1,0:T(8,128)(2,1)} %get-tuple-element.80), channel_id=1, source_target_pairs={{0,1},{1,2},{2,3},{3,0},{4,5},{5,6},{6,7},{7,4},{8,9},{9,10},{10,1... | collective-permute-start | bytes 1179656 | tf_op jit(solution)/shard_map/ppermute | solution.py:681
  332.9 154.3 %reduce-scatter.5.cloned.1.call-start = ((), (), s32[]{:S(2)}) async-start(), calls=%async_computation.7 | async-start | bytes 2359296 | tf_op jit(solution)/shard_map/reduce_scatter | solution.py:973
  332.9 19.3 %collective-permute-start.28 = (bf16[1408,512]{1,0:T(8,128)(2,1)}, bf16[1408,512]{1,0:T(8,128)(2,1)S(1)}, u32[]{:S(2)}, u32[]{:S(2)}) collective-permute-start(bf16[1408,512]{1,0:T(8,128)(2,1)} %copy-done.11), channel_id=1, source_target_pairs={{0,8},{4,20},{8,0},{12,28},{16,24},{20,4},{24,16},{28,12},{1,9},{5... | collective-permute-start | bytes 4325384 | tf_op jit(solution)/shard_map/ppermute | solution.py:751
  338.7 17.8 %collective-permute-start.25 = (bf16[96,2176]{1,0:T(8,128)(2,1)S(1)}, bf16[96,2176]{1,0:T(8,128)(2,1)S(1)}, u32[]{:S(2)}, u32[]{:S(2)}) collective-permute-start(bf16[96,2176]{1,0:T(8,128)(2,1)S(1)} %get-tuple-element.89), channel_id=1, source_target_pairs={{0,1},{1,2},{2,3},{3,0},{4,5},{5,6},{6,7},{7,4},{8,9},{9,10},{10,1... | collective-permute-start | bytes 1253384 | tf_op jit(solution)/shard_map/ppermute | solution.py:681
  338.7 30.1 %collective-permute-start.26 = (bf16[96,2176]{1,0:T(8,128)(2,1)S(1)}, bf16[96,2176]{1,0:T(8,128)(2,1)S(1)}, u32[]{:S(2)}, u32[]{:S(2)}) collective-permute-start(bf16[96,2176]{1,0:T(8,128)(2,1)S(1)} %get-tuple-element.89), channel_id=1, source_target_pairs={{0,2},{1,3},{2,0},{3,1},{4,6},{5,7},{6,4},{7,5},{8,10},{9,11},{10,... | collective-permute-start | bytes 1253384 | tf_op jit(solution)/shard_map/ppermute | solution.py:681
  340.6 28.3 %collective-permute-start.27 = (bf16[96,2176]{1,0:T(8,128)(2,1)S(1)}, bf16[96,2176]{1,0:T(8,128)(2,1)S(1)}, u32[]{:S(2)}, u32[]{:S(2)}) collective-permute-start(bf16[96,2176]{1,0:T(8,128)(2,1)S(1)} %get-tuple-element.89), channel_id=1, source_target_pairs={{0,3},{1,0},{2,1},{3,2},{4,7},{5,4},{6,5},{7,6},{8,11},{9,8},{10,9... | collective-permute-start | bytes 1253384 | tf_op jit(solution)/shard_map/ppermute | solution.py:681
  390.6 30.6 %collective-permute-start.30 = (bf16[1408,256]{1,0:T(8,128)(2,1)}, bf16[1408,256]{1,0:T(8,128)(2,1)}, u32[]{:S(2)}, u32[]{:S(2)}) collective-permute-start(bf16[1408,256]{1,0:T(8,128)(2,1)} %copy-done.16), channel_id=1, source_target_pairs={{0,16},{4,12},{8,24},{12,4},{16,0},{20,28},{24,8},{28,20},{1,17},{... | collective-permute-start | bytes 2162696 | tf_op jit(solution)/shard_map/ppermute | solution.py:751
  402.6 38.4 %collective-permute-start.31 = (bf16[512,2176]{1,0:T(8,128)(2,1)}, bf16[512,2176]{1,0:T(8,128)(2,1)}, u32[]{:S(2)}, u32[]{:S(2)}) collective-permute-start(bf16[512,2176]{1,0:T(8,128)(2,1)} %mixer_gradient.4), channel_id=1, source_target_pairs={{0,8},{4,20},{8,0},{12,28},{16,24},{20,4},{24,16},{28,12},{1,9},{5... | collective-permute-start | bytes 6684680 | tf_op jit(solution)/shard_map/ppermute | solution.py:751
  408.8 75.8 %all-to-all-start = ((bf16[4,96,2048]{2,1,0:T(8,128)(2,1)}), bf16[4,96,2048]{2,1,0:T(8,128)(2,1)}, u32[]{:S(2)}, u32[]{:S(2)}) async-start(bf16[4,96,2048]{2,1,0:T(8,128)(2,1)} %bitcast.69), calls=%async_computation | async-start | bytes 3145728 | tf_op jit(solution)/shard_map/all_to_all | solution.py:957
  444.5 21.4 %collective-permute-start.32 = (bf16[256,2176]{1,0:T(8,128)(2,1)}, bf16[256,2176]{1,0:T(8,128)(2,1)}, u32[]{:S(2)}, u32[]{:S(2)}) collective-permute-start(bf16[256,2176]{1,0:T(8,128)(2,1)} %mixer_gradient.5), channel_id=1, source_target_pairs={{0,16},{4,12},{8,24},{12,4},{16,0},{20,28},{24,8},{28,20},{1,17},{... | collective-permute-start | bytes 3342344 | tf_op jit(solution)/shard_map/ppermute | solution.py:751
  474.7 15.6 %collective-permute-start.35 = (f32[4,256]{1,0:T(4,128)}, f32[4,256]{1,0:T(4,128)}, u32[]{:S(2)}, u32[]{:S(2)}) collective-permute-start(f32[4,256]{1,0:T(4,128)} %pad_maximum_fusion.11), channel_id=1, source_target_pairs={{0,3},{1,0},{2,1},{3,2},{4,7},{5,4},{6,5},{7,6},{8,11},{9,8},{10,9... | collective-permute-start | bytes 12296 | tf_op jit(solution)/shard_map/ppermute | solution.py:681
  (78 other events, 896.0 us)
Sparse Core Ops, SparseCore 0:
  10.5 62.4 all-gather.3
  75.5 67.6 all-gather.5
  145.7 44.3 all-gather.7
  333.0 92.0 reduce-scatter.2
  428.2 48.9 reduce-scatter.4
